TPU v7x, 256 devices: a whole 4x4x8 slice. The times are simulated.
256 devices in a mesh: rcv: 32 (over z, x_lo, core), src: 8 (over x_hi, y).
Axes of the slice: x: 4 (x_hi: 2, x_lo: 2; x = x_hi * 2 + x_lo), y: 4, z: 8, core: 2. Of those that a mesh axis runs over, the one named last changes fastest.
Arguments:
- traces: bfloat16 [2, 2, 4096, 8192], P(None, None, 'rcv', 'src')
- tile_table: int32 [32, 17, 2], replicated, may hold values from 0 to 31, as said below
Outputs:
- psf_tiles: float32 [32, 17, 2, 2, 128, 128], P('rcv', None, None, None, 'src')
Inputs may be any that keep to these rules, and one draw needn't show every extreme that they name: `tile_table`: each entry names a row block and a column block, the row block never past the column block; every such pair of the 32 blocks appears in some slot, and over all 544 slots no pair appears more than twice.
All inputs are finite; a program needn't handle non-finite values.
Results may differ from a plain program's by a relative error of at most 0.0003.
Values may be sent and summed in bfloat16 or wider, within the bound.
No kernel may reach another device: no remote copies, remote signals or barrier semaphores. Data moves between devices by JAX's collectives and lax.ppermute only.
A program may use at most 256 MiB of HBM per device.

v0:
```python
import jax
import jax.numpy as jnp
from jax import lax
from jax.sharding import PartitionSpec as P


def owned_tiles(gathered, slots, block_rows, offset, count):

    def tile_of(pair):
        row_block = lax.dynamic_slice_in_dim(gathered, pair[0] * block_rows + offset, count, 2)
        col_block = lax.dynamic_slice_in_dim(gathered, pair[1] * block_rows, block_rows, 2)
        real_part = jnp.einsum(
            "frs,fts->frt", row_block[:, 0], col_block[:, 0], preferred_element_type=jnp.float32
        ) + jnp.einsum(
            "frs,fts->frt", row_block[:, 1], col_block[:, 1], preferred_element_type=jnp.float32
        )
        imag_part = jnp.einsum(
            "frs,fts->frt", row_block[:, 1], col_block[:, 0], preferred_element_type=jnp.float32
        ) - jnp.einsum(
            "frs,fts->frt", row_block[:, 0], col_block[:, 1], preferred_element_type=jnp.float32
        )
        return jnp.stack([real_part, imag_part], axis=1)

    return jax.vmap(tile_of)(slots)


def body(traces, tile_table):
    block_rows = traces.shape[2]
    gathered = lax.all_gather(traces, "rcv", axis=2, tiled=True)
    owner = lax.axis_index("rcv")
    slots = lax.dynamic_index_in_dim(tile_table, owner, 0, keepdims=False)
    partial_tiles = owned_tiles(gathered, slots, block_rows, 0, block_rows)
    summed = lax.psum_scatter(partial_tiles, "src", scatter_dimension=3, tiled=True)
    return summed[None]


def solution(mesh):
    placed = (P(None, None, "rcv", "src"), P())
    return jax.shard_map(
        body,
        mesh=mesh,
        in_specs=placed,
        out_specs=P("rcv", None, None, None, "src", None),
        check_vma=False,
    )
```

profile of v0, /device:TPU:6, one launch (start us, length us, event | category | flops | bytes accessed | tf_op | source)
XLA Modules:
  0.0 478.0 jit_solution(4626826742751646107)
XLA Ops:
  6.5 0.7 all-gather.2.cloned.1.call-update
  7.6 188.6 %all-gather.2.cloned.1.call-done = bf16[2,2,4096,1024]{3,2,1,0:T(8,128)(2,1)} async-done(((bf16[2,2,128,1024]{3,2,1,0:T(8,128)(2,1)}), bf16[2,2,4096,1024]{3,2,1,0:T(8,128)(2,1)}) %all-gather.2.cloned.1.call-update) | async-done | bytes 33554448 | tf_op jit(solution)/shard_map/all_gather | solution.py:29
  196.2 6.3 %broadcast.23.clone2 = bf16[17,2,2,128,1024]{4,3,1,0,2:T(8,128)(2,1)} broadcast(bf16[]{:T(256)} %constant.19), dimensions={} | broadcast | bytes 17825794
  202.5 61.5 %while.3 = (s32[]{:T(128)}, bf16[2,2,4096,1024]{3,2,1,0:T(8,128)(2,1)}, s32[17,4]{0,1:T(4,128)S(1)}, bf16[17,2,2,128,1024]{4,3,1,0,2:T(8,128)(2,1)}, s32[]{:T(128)}) while((s32[]{:T(128)}, bf16[2,2,4096,1024]{3,2,1,0:T(8,128)(2,1)}, s32[17,4]{0,1:T(4,128)S(1)}, bf16[17,2,2,128,1024]{4,3,1,0,2:T(8,128)(2,1)}, s32[]{:T(128)}) %tuple.29), condition=%wide.while_cond.1, body=%wide.while_body.1.sunk | while | flops 2 | bytes 2097781 | solution.py:11
  203.1 3.1 copy_dynamic-update-slice_fusion.5
  206.7 3.1 copy_dynamic-update-slice_fusion.5
  210.3 3.0 copy_dynamic-update-slice_fusion.5
  214.0 3.0 copy_dynamic-update-slice_fusion.5
  217.5 3.0 copy_dynamic-update-slice_fusion.5
  221.1 3.1 copy_dynamic-update-slice_fusion.5
  224.8 3.1 copy_dynamic-update-slice_fusion.5
  228.4 3.1 copy_dynamic-update-slice_fusion.5
  232.0 3.1 copy_dynamic-update-slice_fusion.5
  235.7 3.1 copy_dynamic-update-slice_fusion.5
  239.3 3.1 copy_dynamic-update-slice_fusion.5
  242.9 3.1 copy_dynamic-update-slice_fusion.5
  246.5 3.1 copy_dynamic-update-slice_fusion.5
  250.2 3.1 copy_dynamic-update-slice_fusion.5
  253.8 3.1 copy_dynamic-update-slice_fusion.5
  257.4 3.1 copy_dynamic-update-slice_fusion.5
  261.0 3.0 copy_dynamic-update-slice_fusion.5
  264.1 6.3 %broadcast.23.clone2.1 = bf16[17,2,2,128,1024]{4,3,1,0,2:T(8,128)(2,1)} broadcast(bf16[]{:T(256)} %constant.19), dimensions={} | broadcast | bytes 17825794
  270.4 63.9 %while.2 = (s32[]{:T(128)}, bf16[2,2,4096,1024]{3,2,1,0:T(8,128)(2,1)}, s32[17,4]{0,1:T(4,128)S(1)}, bf16[17,2,2,128,1024]{4,3,1,0,2:T(8,128)(2,1)}, s32[]{:T(128)}) while((s32[]{:T(128)}, bf16[2,2,4096,1024]{3,2,1,0:T(8,128)(2,1)}, s32[17,4]{0,1:T(4,128)S(1)}, bf16[17,2,2,128,1024]{4,3,1,0,2:T(8,128)(2,1)}, s32[]{:T(128)}) %tuple.39), condition=%wide.while_cond, body=%wide.while_body.sunk | while | flops 2 | bytes 2097781 | solution.py:10
  271.0 3.2 copy_dynamic-update-slice_fusion.4
  274.2 0.5 slice.110
  274.8 3.2 copy_dynamic-update-slice_fusion.4
  278.5 3.2 copy_dynamic-update-slice_fusion.4
  282.3 3.2 copy_dynamic-update-slice_fusion.4
  286.0 3.1 copy_dynamic-update-slice_fusion.4
  289.8 3.1 copy_dynamic-update-slice_fusion.4
  293.5 3.1 copy_dynamic-update-slice_fusion.4
  297.2 3.2 copy_dynamic-update-slice_fusion.4
  301.0 3.2 copy_dynamic-update-slice_fusion.4
  304.8 3.2 copy_dynamic-update-slice_fusion.4
  308.5 3.2 copy_dynamic-update-slice_fusion.4
  312.3 3.2 copy_dynamic-update-slice_fusion.4
  316.0 3.2 copy_dynamic-update-slice_fusion.4
  319.8 3.1 copy_dynamic-update-slice_fusion.4
  323.5 3.2 copy_dynamic-update-slice_fusion.4
  327.3 3.2 copy_dynamic-update-slice_fusion.4
  331.1 3.2 copy_dynamic-update-slice_fusion.4
  334.3 10.0 %fusion.2 = f32[17,2,128,128]{3,2,1,0:T(8,128)} fusion(bf16[17,2,2,128,1024]{4,3,1,0,2:T(8,128)(2,1)} %get-tuple-element.20, bf16[17,2,2,128,1024]{4,3,1,0,2:T(8,128)(2,1)} %get-tuple-element.12), kind=kOutput, calls=%fused_computation.8 | convolution fusion | flops 1140850688 | bytes 20054016 | tf_op jit(solution)/shard_map/vmap(frs,fts->frt)/dot_general | solution.py:14
  344.2 10.0 %fusion = f32[17,2,128,128]{3,2,1,0:T(8,128)} fusion(bf16[17,2,2,128,1024]{4,3,1,0,2:T(8,128)(2,1)} %get-tuple-element.20, bf16[17,2,2,128,1024]{4,3,1,0,2:T(8,128)(2,1)} %get-tuple-element.12), kind=kOutput, calls=%fused_computation.6 | convolution fusion | flops 1140850688 | bytes 20054016 | tf_op jit(solution)/shard_map/vmap(frs,fts->frt)/dot_general | solution.py:19
  354.2 9.2 %add_bitcast_fusion = f32[17,2,1,128,128]{4,3,1,0,2:T(8,128)S(1)} fusion(f32[17,2,128,128]{3,2,1,0:T(8,128)} %fusion.2, bf16[17,2,2,128,1024]{4,3,1,0,2:T(8,128)(2,1)} %get-tuple-element.20, bf16[17,2,2,128,1024]{4,3,1,0,2:T(8,128)(2,1)} %get-tuple-element.12), kind=kOutput, calls=%fused_computation.28 | convolution fusion | flops 1141407744 | bytes 22282240 | tf_op jit(solution)/shard_map/vmap(frs,fts->frt)/dot_general | solution.py:12
  363.4 10.6 %subtract_bitcast_fusion = f32[17,2,1,128,128]{4,3,1,0,2:T(8,128)} fusion(f32[17,2,128,128]{3,2,1,0:T(8,128)} %fusion, bf16[17,2,2,128,1024]{4,3,1,0,2:T(8,128)(2,1)} %get-tuple-element.20, bf16[17,2,2,128,1024]{4,3,1,0,2:T(8,128)(2,1)} %get-tuple-element.12), kind=kOutput, calls=%fused_computation.27 | convolution fusion | flops 1141407744 | bytes 22282240 | tf_op jit(solution)/shard_map/vmap(frs,fts->frt)/dot_general | solution.py:17
  374.0 4.5 pad_maximum_fusion
  378.5 90.7 %reduce-scatter.2.cloned.1.call-done = f32[17,2,2,16,128]{4,3,1,0,2:T(8,128)} async-done(((f32[17,2,2,128,128]{4,3,1,0,2:T(8,128)}), f32[17,2,2,16,128]{4,3,1,0,2:T(8,128)}) %reduce-scatter.2.cloned.1.call-update) | async-done | bytes 557072 | tf_op jit(solution)/shard_map/reduce_scatter | solution.py:33
  469.2 1.9 copy.8
  (81 shorter events, 19.3 us)
Async XLA Ops:
  6.5 0.8 copy-start
  6.5 189.7 %all-gather.2.cloned.1.call-start = ((), (), s32[]{:S(2)}) async-start(), calls=%async_computation.1 | async-start | bytes 34603008 | tf_op jit(solution)/shard_map/all_gather | solution.py:29
  7.3 461.9 %reduce-scatter.2.cloned.1.call-start = ((), (), s32[]{:S(2)}) async-start(), calls=%async_computation.2 | async-start | bytes 5013504 | tf_op jit(solution)/shard_map/reduce_scatter | solution.py:33
  354.2 116.9 %copy-start.1 = (s32[32,17,2]{0,2,1:T(2,128)S(1)}, s32[32,17,2]{0,2,1:T(2,128)}, u32[]{:S(2)}) copy-start(s32[32,17,2]{0,2,1:T(2,128)} %param.3) | copy-start | bytes 13060
Sparse Core Ops, SparseCore 0:
  9.2 186.9 all-gather.1
  378.6 90.5 reduce-scatter.1
where the time goes:
time: 481 us; the launch traced here: 478 us
  waiting for transfers between devices  280 us (58%)
  local copies, waits for them, and re-layouts  140 us (29%)
  matrix products  39.7 us (8%)
  between operations  13.5 us (3%)
    all_gather x1, waiting for transfers between devices, body(): gathered = lax.all_gather(traces, 'rcv', axis=2, tiled=True)  189 us
    gather x102, local copies, waits for them, and re-layouts  125 us
    reduce_scatter x1, waiting for transfers between devices, body(): lax.psum_scatter(partial_tiles, 'src', scatter_dimension=3, tiled=True)  90.7 us
    unnamed x6, local copies, waits for them, and re-layouts  12.7 us
    dot_general x1, matrix products, tile_of(): jnp.einsum('frs,fts->frt', row_block[:, 1], col_block[:, 0], preferred_el...  10.6 us
    dot_general x1, matrix products, tile_of(): jnp.einsum('frs,fts->frt', row_block[:, 0], col_block[:, 1], preferred_el...  9.97 us
    dot_general x1, matrix products, tile_of(): jnp.einsum('frs,fts->frt', row_block[:, 1], col_block[:, 1], preferred_el...  9.96 us
  transfers between devices with their start and end apart: 2, of which 2 were waited for; matrix products, arithmetic and copies ran while one was open for 0% of the time, Pallas kernels for 0%

commit v1 on v0

v1 whole, which is shorter than its diff:
```python
import jax
import jax.numpy as jnp
from jax import lax
from jax.experimental import pallas as pl
from jax.experimental.pallas import tpu as pltpu
from jax.sharding import Mesh
from jax.sharding import PartitionSpec as P

NZ, NXL, NC, NXH, NY = 8, 2, 2, 2, 4
NX = NXH * NXL
K = 17
BR = 128
HS = 512
X_AXIS = ("xl", "xh")


def rank(i, axis):
    return (i % NXL) * NXH + i // NXL if axis == X_AXIS else i


def shift(x, axis, size, step):
    return lax.ppermute(x, axis, [(rank(i, axis), rank((i + step) % size, axis)) for i in range(size)])


def swap(x, axis):
    return shift(x, axis, 2, 1)


def hbm_spec():
    return pl.BlockSpec(memory_space=pltpu.HBM)


def in_hbm(arrays):
    return [pltpu.with_memory_space_constraint(a, pltpu.HBM) for a in arrays]


def packed(arrays, after=()):
    n, m = len(arrays), len(after)

    def kernel(*refs):
        srcs, out, sem = refs[:n], refs[n + m], refs[-1]
        moves = [pltpu.make_async_copy(src, out.at[i], sem.at[i]) for i, src in enumerate(srcs)]
        for move in moves:
            move.start()
        for move in moves:
            move.wait()

    return pl.pallas_call(
        kernel,
        out_shape=pltpu.HBM((n,) + arrays[0].shape, arrays[0].dtype),
        in_specs=[pl.BlockSpec(memory_space=pltpu.VMEM)] * n + [pl.BlockSpec(memory_space=pl.ANY)] * m,
        out_specs=hbm_spec(),
        scratch_shapes=[pltpu.SemaphoreType.DMA((n,))],
        compiler_params=pltpu.CompilerParams(vmem_limit_bytes=8 * 1024 * 1024),
        cost_estimate=pl.CostEstimate(flops=0, bytes_accessed=4 * n * arrays[0].size, transcendentals=0),
    )(*arrays, *in_hbm(after))


def ring_step(a, b, k):
    (au, ad), (bu, bd) = a, b
    au = shift(au, "z", NZ, 1)
    ad = shift(ad, "z", NZ, -1) if k < 4 else None
    bu = shift(bu, "z", NZ, 1) if k < 4 else None
    bd = shift(bd, "z", NZ, -1)
    return (au, ad), (bu, bd)


def ring_gather(a, b):
    mine = packed([a, b])
    blocks = [(mine, (i,), (0, 0, i)) for i in range(2)]
    far = swap(mine, "c")
    blocks += [(far, (i,), (0, 1, i)) for i in range(2)]
    ra, rb = (a, a), (b, b)
    late = []
    for k in range(1, 5):
        ra, rb = ring_step(ra, rb, k)
        if k < 4:
            mine = packed([*ra, *rb])
            far = swap(mine, "c")
            late.append(far)
            for i, (dz, xr) in enumerate([(-k % NZ, 0), (k, 0), (-k % NZ, 1), (k, 1)]):
                blocks.append((mine, (i,), (dz, 0, xr)))
                blocks.append((far, (i,), (dz, 1, xr)))
        if k == 3:
            late = late[:2] + [mine]
    mine = packed([ra[0], rb[1]])
    far = swap(mine, "c")
    for i in range(2):
        blocks.append((mine, (i,), (4, 0, i)))
        blocks.append((far, (i,), (4, 1, i)))
    return blocks, late


def tile_partials(slots, pos, pairs, after=()):
    arrays = list({id(a): a for a, _, _ in pairs}.values())
    moves = [([a is x for x in arrays].index(True), src, dst) for a, src, dst in pairs]
    n, m = len(arrays), len(after)
    parts = [jax.ShapeDtypeStruct((NY, K, 16, BR), jnp.float32)] * (2 * NX)

    def kernel(slots, pos, *refs):
        chunks, outs = refs[:n], refs[n + m : n + m + len(parts)]
        xs, gs, sem = refs[n + m + len(parts) :]
        re_out, im_out = outs[:NX], outs[NX:]
        loads = [
            pltpu.make_async_copy(chunks[a].at[src], xs.at[dst], sem.at[i]) for i, (a, src, dst) in enumerate(moves)
        ]
        for load in loads:
            load.start()
        for load in loads:
            load.wait()
        px, py = pos[0], pos[1]
        rows = {}
        for dx in range(NX):
            for dy in range(NY):
                rows[dx, dy] = (((px + dx) % NX // 2) * NY + (py + dy) % NY) * 16

        def block(s):
            return xs[s // 4, (s // 2) % 2, s % 2].reshape(2 * BR, HS)

        def tile(j, buf, xr):
            t = xr * K + j
            u = block(slots[2 * t])
            v = block(slots[2 * t + 1])
            gs[buf] = lax.dot_general(u, v, (((1,), (1,)), ((), ())), preferred_element_type=jnp.float32)
            for dx in (xr, xr + 2):
                for dy in range(NY):
                    top = pl.ds(pl.multiple_of(rows[dx, dy], 16), 16)
                    low = pl.ds(pl.multiple_of(rows[dx, dy] + BR, 16), 16)
                    re_out[dx][dy, j] = gs[buf, top, :BR] + gs[buf, low, BR:]
                    im_out[dy][dx, j] = gs[buf, low, :BR] - gs[buf, top, BR:]

        for j in range(K):
            for xr in range(NXL):
                tile(j, (2 * j + xr) % 4, xr)

    smem = pl.BlockSpec(memory_space=pltpu.SMEM)
    outs = pl.pallas_call(
        kernel,
        out_shape=parts,
        in_specs=[smem, smem] + [pl.BlockSpec(memory_space=pl.ANY)] * (n + m),
        out_specs=[pl.BlockSpec(memory_space=pltpu.VMEM)] * len(parts),
        scratch_shapes=[
            pltpu.VMEM((NZ, NC, NXL, 2, BR, HS), jnp.bfloat16),
            pltpu.VMEM((4, 2 * BR, 2 * BR), jnp.float32),
            pltpu.SemaphoreType.DMA((len(pairs),)),
        ],
        compiler_params=pltpu.CompilerParams(vmem_limit_bytes=24 * 1024 * 1024),
        cost_estimate=pl.CostEstimate(flops=2 * 34 * 256 * 256 * 512, bytes_accessed=13_000_000, transcendentals=0),
    )(slots.reshape(-1), pos, *in_hbm(arrays), *after)
    return outs[:NX], outs[NX:]


def reduce_far(parts, axis):
    got = [parts[0]] + [shift(parts[d], axis, NX, d) for d in (2, 1, 3)]
    return [got[0][d] + got[1][d] + got[2][d] + got[3][d] for d in range(NY)]


def reduce_near(sums, axis):
    both = [jnp.stack([f[d] for f in sums], 1) for d in range(NY)]
    got = [both[0]] + [shift(both[d], axis, NY, d) for d in (2, 1, 3)]
    return got[0] + got[1] + got[2] + got[3]


def body(traces, tile_table):
    z, xl, c = lax.axis_index("z"), lax.axis_index("xl"), lax.axis_index("c")
    px = lax.axis_index("xh") * NXL + xl
    py = lax.axis_index("y")
    pos = jnp.stack([px, py]).astype(jnp.int32)
    mine = tile_table.reshape(NZ, NXL, NC, K, 2)[z, :, c]
    mine = jnp.where(xl == 0, mine, mine[::-1])
    near = (mine // 2) % 2 ^ xl
    slots_rel = (((mine // 4 - z) % NZ) * 4 + (mine % 2 ^ c) * 2 + near).astype(jnp.int32)
    slots_abs = ((mine // 4) * 4 + (mine % 2) * 2 + near).astype(jnp.int32)

    own = lax.dynamic_slice_in_dim(traces, xl * HS, HS, 3)
    other = lax.dynamic_slice_in_dim(traces, (1 - xl) * HS, HS, 3)

    blocks, late = ring_gather(own[0], swap(other[0], "xl"))
    both = packed([own[1], swap(other[1], "xl")], after=late)
    whole = lax.all_gather(both, ("z", "c")).reshape(NZ, NC, NXL, 2, BR, HS)

    re_parts, im_parts = tile_partials(slots_rel, pos, blocks, after=in_hbm([both]))
    re_first, im_first = reduce_far(re_parts, X_AXIS), reduce_far(im_parts, "y")

    blocks = [(whole, (dz,), (dz,)) for dz in range(NZ)]
    re_parts, im_parts = tile_partials(slots_abs, pos, blocks, after=(*re_first, *im_first))
    re_second, im_second = reduce_far(re_parts, X_AXIS), reduce_far(im_parts, "y")
    re_sum = reduce_near((re_first, re_second), "y")
    im_sum = reduce_near((im_first, im_second), X_AXIS)
    return jnp.stack([re_sum, im_sum], 2)[None]


def solution(mesh):
    axes = ("z", "xl", "c", "xh", "y")
    fine = Mesh(mesh.devices.reshape(NZ, NXL, NC, NXH, NY), axes)
    rcv, src = axes[:3], axes[3:]
    return jax.shard_map(
        body,
        mesh=fine,
        in_specs=(P(None, None, rcv, src), P()),
        out_specs=P(rcv, None, None, None, src, None),
        check_vma=False,
    )
```

time: 481 us -> 186 us (0.39)
  waiting for transfers between devices: 280 us -> 81.5 us
  local copies, waits for them, and re-layouts: 140 us -> 4.85 us
  starting transfers between devices: 0.04 us -> 58.8 us
  matrix products: 39.7 us -> 0 us
  Pallas kernels: 0 us -> 20.7 us
    all_gather x1, waiting for transfers between devices: 189 us -> 0.02 us  [body(): whole = lax.all_gather(both, ('z', 'c')).reshape(NZ, NC, NXL, 2, BR, HS)]
    gather x102 -> x0, local copies, waits for them, and re-layouts: 125 us -> none
    reduce_scatter x1 -> x0, waiting for transfers between devices: 90.7 us -> none  [body(): lax.psum_scatter(partial_tiles, 'src', scatter_dimension=3, tiled=True)]
    ppermute x0 -> x39, waiting for transfers between devices: none -> 81.5 us  [shift(): lax.ppermute(x, axis, [(rank(i, axis), rank((i + step) % size, axis)) for...]
    ppermute x0 -> x39, starting transfers between devices: none -> 58.8 us  [shift(): lax.ppermute(x, axis, [(rank(i, axis), rank((i + step) % size, axis)) for...]
    dot_general x4 -> x0, matrix products: 39.7 us -> none  [the longest x1 10.6 us: tile_of(): jnp.einsum('frs,fts->frt', row_block[:, 1], col_block[:, 0], preferred_el...]
    pallas_call x0 -> x8, Pallas kernels: none -> 20.7 us  [the longest x2 15.2 us: tile_partials(): pl.pallas_call(kernel, out_shape=parts, in_specs=[smem, smem] + [pl.Block...]
    unnamed x6 -> x13, local copies, waits for them, and re-layouts: 12.7 us -> 2.27 us
  transfers between devices with their start and end apart: 2 -> 40, of which waited for: 2 -> 23; matrix products, arithmetic and copies ran while one was open for 0% -> 2% of each run, Pallas kernels for 0% -> 7%
where the time goes in v1:
time: 186 us; the launch traced here: 184 us
  waiting for transfers between devices  81.5 us (44%)
  starting transfers between devices  58.8 us (32%)
  Pallas kernels  20.7 us (11%)
  between operations  13.7 us (7%)
  local copies, waits for them, and re-layouts  4.85 us (3%)
  other arithmetic  4.11 us (2%)
    ppermute x39, waiting for transfers between devices, shift(): lax.ppermute(x, axis, [(rank(i, axis), rank((i + step) % size, axis)) for...  81.5 us
    ppermute x39, starting transfers between devices, shift(): lax.ppermute(x, axis, [(rank(i, axis), rank((i + step) % size, axis)) for...  58.8 us
    pallas_call x2, Pallas kernels, tile_partials(): pl.pallas_call(kernel, out_shape=parts, in_specs=[smem, smem] + [pl.Block...  15.2 us
    pallas_call x6, Pallas kernels, packed(): pl.pallas_call(kernel, out_shape=pltpu.HBM((n,) + arrays[0].shape, arrays...  5.43 us
  transfers between devices with their start and end apart: 40, of which 23 were waited for; matrix products, arithmetic and copies ran while one was open for 2% of the time, Pallas kernels for 7%

profile of v1, /device:TPU:6, one launch (start us, length us, event | category | flops | bytes accessed | tf_op | source)
XLA Modules:
  0.0 183.7 jit_solution(17782662388139478769)
XLA Ops:
  6.5 1.3 dynamic-slice_bitcast_fusion.2
  8.7 5.9 %collective-permute-start.3 = (bf16[2,128,512]{2,1,0:T(8,128)(2,1)S(1)}, bf16[2,128,512]{2,1,0:T(8,128)(2,1)S(1)}, u32[]{:S(2)}, u32[]{:S(2)}) collective-permute-start(bf16[2,128,512]{2,1,0:T(8,128)(2,1)S(1)} %get-tuple-element.56.refs_0_), channel_id=1, source_target_pairs={{0,224},{32,0},{64,32},{96,64},{128,96},{160,128},{192,160},{224,1... | collective-permute-start | bytes 786440 | tf_op jit(solution)/shard_map/ppermute | solution.py:22
  14.6 1.4 collective-permute-done.refs_1_
  16.0 5.9 %collective-permute-start.5 = (bf16[2,128,512]{2,1,0:T(8,128)(2,1)S(1)}, bf16[2,128,512]{2,1,0:T(8,128)(2,1)S(1)}, u32[]{:S(2)}, u32[]{:S(2)}) collective-permute-start(bf16[2,128,512]{2,1,0:T(8,128)(2,1)S(1)} %collective-permute-done.refs_1_), channel_id=1, source_target_pairs={{0,224},{32,0},{64,32},{96,64},{128,96},{160,128},{192,160},{224,1... | collective-permute-start | bytes 786440 | tf_op jit(solution)/shard_map/ppermute | solution.py:22
  21.8 3.2 %collective-permute-start.8 = (bf16[2,128,512]{2,1,0:T(8,128)(2,1)S(1)}, bf16[2,128,512]{2,1,0:T(8,128)(2,1)S(1)}, u32[]{:S(2)}, u32[]{:S(2)}) collective-permute-start(bf16[2,128,512]{2,1,0:T(8,128)(2,1)S(1)} %collective-permute-done.3.refs_1_), channel_id=1, source_target_pairs={{0,224},{32,0},{64,32},{96,64},{128,96},{160,128},{192,160},{224,1... | collective-permute-start | bytes 786440 | tf_op jit(solution)/shard_map/ppermute | solution.py:22
  25.1 3.5 %collective-permute-done.5.refs_3_ = bf16[2,128,512]{2,1,0:T(8,128)(2,1)S(1)} collective-permute-done((bf16[2,128,512]{2,1,0:T(8,128)(2,1)S(1)}, bf16[2,128,512]{2,1,0:T(8,128)(2,1)S(1)}, u32[]{:S(2)}, u32[]{:S(2)}) %collective-permute-start.5) | collective-permute-done | bytes 262176 | tf_op jit(solution)/shard_map/ppermute | solution.py:22
  28.6 3.7 %collective-permute-start.10 = (bf16[2,128,512]{2,1,0:T(8,128)(2,1)S(1)}, bf16[2,128,512]{2,1,0:T(8,128)(2,1)S(1)}, u32[]{:S(2)}, u32[]{:S(2)}) collective-permute-start(bf16[2,128,512]{2,1,0:T(8,128)(2,1)S(1)} %collective-permute-done.5.refs_3_), channel_id=1, source_target_pairs={{0,224},{32,0},{64,32},{96,64},{128,96},{160,128},{192,160},{224,1... | collective-permute-start | bytes 786440 | tf_op jit(solution)/shard_map/ppermute | solution.py:22
  32.3 1.0 shard_map.29.refs_2_
  34.2 3.7 %collective-permute-done.7.refs_0_ = bf16[2,128,512]{2,1,0:T(8,128)(2,1)S(1)} collective-permute-done((bf16[2,128,512]{2,1,0:T(8,128)(2,1)S(1)}, bf16[2,128,512]{2,1,0:T(8,128)(2,1)S(1)}, u32[]{:S(2)}, u32[]{:S(2)}) %collective-permute-start.7) | collective-permute-done | bytes 262176 | tf_op jit(solution)/shard_map/ppermute | solution.py:22
  37.9 3.3 %collective-permute-done.9.refs_2_ = bf16[2,128,512]{2,1,0:T(8,128)(2,1)S(1)} collective-permute-done((bf16[2,128,512]{2,1,0:T(8,128)(2,1)S(1)}, bf16[2,128,512]{2,1,0:T(8,128)(2,1)S(1)}, u32[]{:S(2)}, u32[]{:S(2)}) %collective-permute-start.9) | collective-permute-done | bytes 262176 | tf_op jit(solution)/shard_map/ppermute | solution.py:22
  41.2 1.0 shard_map.30.refs_4_
  42.6 1.7 collective-permute-start.12
  44.4 1.5 collective-permute-start.15
  45.9 5.6 %collective-permute-done.13.refs_1_ = bf16[2,128,512]{2,1,0:T(8,128)(2,1)S(1)} collective-permute-done((bf16[2,128,512]{2,1,0:T(8,128)(2,1)S(1)}, bf16[2,128,512]{2,1,0:T(8,128)(2,1)S(1)}, u32[]{:S(2)}, u32[]{:S(2)}) %collective-permute-start.13) | collective-permute-done | bytes 262176 | tf_op jit(solution)/shard_map/ppermute | solution.py:22
  53.0 3.6 %collective-permute-done.15.refs_3_ = bf16[2,128,512]{2,1,0:T(8,128)(2,1)S(1)} collective-permute-done((bf16[2,128,512]{2,1,0:T(8,128)(2,1)S(1)}, bf16[2,128,512]{2,1,0:T(8,128)(2,1)S(1)}, u32[]{:S(2)}, u32[]{:S(2)}) %collective-permute-start.15) | collective-permute-done | bytes 262176 | tf_op jit(solution)/shard_map/ppermute | solution.py:22
  56.6 3.4 %collective-permute-done.14.refs_2_ = bf16[2,128,512]{2,1,0:T(8,128)(2,1)S(1)} collective-permute-done((bf16[2,128,512]{2,1,0:T(8,128)(2,1)S(1)}, bf16[2,128,512]{2,1,0:T(8,128)(2,1)S(1)}, u32[]{:S(2)}, u32[]{:S(2)}) %collective-permute-start.14) | collective-permute-done | bytes 262176 | tf_op jit(solution)/shard_map/ppermute | solution.py:22
  60.0 1.0 shard_map.31.refs_4_.refs_6_
  61.1 0.9 copy-done
  63.7 3.2 %collective-permute-start.18 = (bf16[2,128,512]{2,1,0:T(8,128)(2,1)S(1)}, bf16[2,128,512]{2,1,0:T(8,128)(2,1)S(1)}, u32[]{:S(2)}, u32[]{:S(2)}) collective-permute-start(bf16[2,128,512]{2,1,0:T(8,128)(2,1)S(1)} %collective-permute-done.15.refs_3_), channel_id=1, source_target_pairs={{0,224},{32,0},{64,32},{96,64},{128,96},{160,128},{192,160},{224,1... | collective-permute-start | bytes 786440 | tf_op jit(solution)/shard_map/ppermute | solution.py:22
  67.8 5.7 %collective-permute-done.17.refs_0_ = bf16[2,128,512]{2,1,0:T(8,128)(2,1)S(1)} collective-permute-done((bf16[2,128,512]{2,1,0:T(8,128)(2,1)S(1)}, bf16[2,128,512]{2,1,0:T(8,128)(2,1)S(1)}, u32[]{:S(2)}, u32[]{:S(2)}) %collective-permute-start.17) | collective-permute-done | bytes 262176 | tf_op jit(solution)/shard_map/ppermute | solution.py:22
  75.7 1.6 collective-permute-done.19.refs_9_
  78.2 8.2 %shard_map.34 = (f32[4,17,16,128]{3,2,1,0:T(8,128)S(1)}, f32[4,17,16,128]{3,2,1,0:T(8,128)}, f32[4,17,16,128]{3,2,1,0:T(8,128)S(1)}, f32[4,17,16,128]{3,2,1,0:T(...) custom-call(s32[68]{0:T(128)S(1)} %reshape.677.slots, ...), custom_call_target="tpu_custom_call" | custom-call | flops 2281701376 | bytes 13000000 | tf_op jit(solution)/shard_map/pallas_call | solution.py:137
  86.4 1.4 collective-permute-start.21
  87.9 2.1 %collective-permute-start.22 = (f32[4,17,16,128]{3,2,1,0:T(8,128)}, f32[4,17,16,128]{3,2,1,0:T(8,128)}, u32[]{:S(2)}, u32[]{:S(2)}) collective-permute-start(f32[4,17,16,128]{3,2,1,0:T(8,128)} %get-tuple-element.23), channel_id=1, source_target_pairs={{0,16},{16,4},{4,20},{20,0},{1,17},{17,5},{5,21},{21,1},{2,18},{18... | collective-permute-start | bytes 1671176 | tf_op jit(solution)/shard_map/ppermute | solution.py:22
  90.0 3.4 %collective-permute-start.24 = (f32[4,17,16,128]{3,2,1,0:T(8,128)}, f32[4,17,16,128]{3,2,1,0:T(8,128)}, u32[]{:S(2)}, u32[]{:S(2)}) collective-permute-start(f32[4,17,16,128]{3,2,1,0:T(8,128)} %get-tuple-element.26), channel_id=1, source_target_pairs={{0,2},{1,3},{2,0},{3,1},{4,6},{5,7},{6,4},{7,5},{8,10},{9,11},{10,... | collective-permute-start | bytes 1671176 | tf_op jit(solution)/shard_map/ppermute | solution.py:22
  94.1 9.4 %collective-permute-done.21 = f32[4,17,16,128]{3,2,1,0:T(8,128)S(1)} collective-permute-done((f32[4,17,16,128]{3,2,1,0:T(8,128)S(1)}, f32[4,17,16,128]{3,2,1,0:T(8,128)S(1)}, u32[]{:S(2)}, u32[]{:S(2)}) %collective-permute-start.21) | collective-permute-done | bytes 557088 | tf_op jit(solution)/shard_map/ppermute | solution.py:22
  103.5 3.2 %collective-permute-start.26 = (f32[4,17,16,128]{3,2,1,0:T(8,128)S(1)}, f32[4,17,16,128]{3,2,1,0:T(8,128)}, u32[]{:S(2)}, u32[]{:S(2)}) collective-permute-start(f32[4,17,16,128]{3,2,1,0:T(8,128)S(1)} %get-tuple-element.28), channel_id=1, source_target_pairs={{0,3},{1,0},{2,1},{3,2},{4,7},{5,4},{6,5},{7,6},{8,11},{9,8},{10,9... | collective-permute-start | bytes 1671176 | tf_op jit(solution)/shard_map/ppermute | solution.py:22
  107.0 5.5 %collective-permute-done.22 = f32[4,17,16,128]{3,2,1,0:T(8,128)} collective-permute-done((f32[4,17,16,128]{3,2,1,0:T(8,128)}, f32[4,17,16,128]{3,2,1,0:T(8,128)}, u32[]{:S(2)}, u32[]{:S(2)}) %collective-permute-start.22) | collective-permute-done | bytes 557088 | tf_op jit(solution)/shard_map/ppermute | solution.py:22
  112.5 2.2 %collective-permute-done.23 = f32[4,17,16,128]{3,2,1,0:T(8,128)} collective-permute-done((f32[4,17,16,128]{3,2,1,0:T(8,128)S(1)}, f32[4,17,16,128]{3,2,1,0:T(8,128)}, u32[]{:S(2)}, u32[]{:S(2)}) %collective-permute-start.23) | collective-permute-done | bytes 557088 | tf_op jit(solution)/shard_map/ppermute | solution.py:22
  114.7 1.7 slice_add_fusion.36
  116.4 1.6 collective-permute-done.25
  118.5 1.7 slice_add_fusion.24
  120.2 7.0 %shard_map.35 = (f32[4,17,16,128]{3,2,1,0:T(8,128)S(1)}, f32[4,17,16,128]{3,2,1,0:T(8,128)S(1)}, f32[4,17,16,128]{3,2,1,0:T(8,128)S(1)}, f32[4,17,16,128]{3,2,1,...) custom-call(s32[68]{0:T(128)S(1)} %reshape.678.slots, ...), custom_call_target="tpu_custom_call" | custom-call | flops 2281701376 | bytes 13000000 | tf_op jit(solution)/shard_map/pallas_call | solution.py:137
  127.2 1.9 %collective-permute-start.27 = (f32[4,17,16,128]{3,2,1,0:T(8,128)S(1)}, f32[4,17,16,128]{3,2,1,0:T(8,128)S(1)}, u32[]{:S(2)}, u32[]{:S(2)}) collective-permute-start(f32[4,17,16,128]{3,2,1,0:T(8,128)S(1)} %get-tuple-element.30), channel_id=1, source_target_pairs={{0,4},{16,20},{4,0},{20,16},{1,5},{17,21},{5,1},{21,17},{2,6},{18,... | collective-permute-start | bytes 1671176 | tf_op jit(solution)/shard_map/ppermute | solution.py:22
  129.1 1.3 collective-permute-start.28
  131.1 2.0 %collective-permute-start.33 = (f32[4,17,16,128]{3,2,1,0:T(8,128)S(1)}, f32[4,17,16,128]{3,2,1,0:T(8,128)S(1)}, u32[]{:S(2)}, u32[]{:S(2)}) collective-permute-start(f32[4,17,16,128]{3,2,1,0:T(8,128)S(1)} %get-tuple-element.34), channel_id=1, source_target_pairs={{0,2},{1,3},{2,0},{3,1},{4,6},{5,7},{6,4},{7,5},{8,10},{9,11},{10,... | collective-permute-start | bytes 1671176 | tf_op jit(solution)/shard_map/ppermute | solution.py:22
  133.1 2.5 %collective-permute-start.34 = (f32[4,17,16,128]{3,2,1,0:T(8,128)S(1)}, f32[4,17,16,128]{3,2,1,0:T(8,128)S(1)}, u32[]{:S(2)}, u32[]{:S(2)}) collective-permute-start(f32[4,17,16,128]{3,2,1,0:T(8,128)S(1)} %get-tuple-element.35), channel_id=1, source_target_pairs={{0,1},{1,2},{2,3},{3,0},{4,5},{5,6},{6,7},{7,4},{8,9},{9,10},{10,1... | collective-permute-start | bytes 1671176 | tf_op jit(solution)/shard_map/ppermute | solution.py:22
  135.5 8.8 %collective-permute-done.27 = f32[4,17,16,128]{3,2,1,0:T(8,128)S(1)} collective-permute-done((f32[4,17,16,128]{3,2,1,0:T(8,128)S(1)}, f32[4,17,16,128]{3,2,1,0:T(8,128)S(1)}, u32[]{:S(2)}, u32[]{:S(2)}) %collective-permute-start.27) | collective-permute-done | bytes 557088 | tf_op jit(solution)/shard_map/ppermute | solution.py:22
  144.4 3.5 %collective-permute-start.35 = (f32[4,17,16,128]{3,2,1,0:T(8,128)S(1)}, f32[4,17,16,128]{3,2,1,0:T(8,128)S(1)}, u32[]{:S(2)}, u32[]{:S(2)}) collective-permute-start(f32[4,17,16,128]{3,2,1,0:T(8,128)S(1)} %get-tuple-element.36), channel_id=1, source_target_pairs={{0,3},{1,0},{2,1},{3,2},{4,7},{5,4},{6,5},{7,6},{8,11},{9,8},{10,9... | collective-permute-start | bytes 1671176 | tf_op jit(solution)/shard_map/ppermute | solution.py:22
  147.9 7.2 %collective-permute-done.28 = f32[4,17,16,128]{3,2,1,0:T(8,128)S(1)} collective-permute-done((f32[4,17,16,128]{3,2,1,0:T(8,128)S(1)}, f32[4,17,16,128]{3,2,1,0:T(8,128)S(1)}, u32[]{:S(2)}, u32[]{:S(2)}) %collective-permute-start.28) | collective-permute-done | bytes 557088 | tf_op jit(solution)/shard_map/ppermute | solution.py:22
  155.3 1.6 collective-permute-start.30
  156.9 1.8 collective-permute-start.31
  158.8 1.6 collective-permute-start.32
  160.5 1.6 collective-permute-start.36
  162.1 1.4 collective-permute-start.37
  163.6 2.9 %collective-permute-done.30 = f32[17,2,16,128]{3,2,0,1:T(8,128)S(1)} collective-permute-done((f32[17,2,16,128]{3,2,0,1:T(8,128)S(1)}, f32[17,2,16,128]{3,2,0,1:T(8,128)S(1)}, u32[]{:S(2)}, u32[]{:S(2)}) %collective-permute-start.30) | collective-permute-done | bytes 278560 | tf_op jit(solution)/shard_map/ppermute | solution.py:22
  166.7 4.4 %collective-permute-done.31 = f32[17,2,16,128]{3,2,0,1:T(8,128)S(1)} collective-permute-done((f32[17,2,16,128]{3,2,0,1:T(8,128)S(1)}, f32[17,2,16,128]{3,2,0,1:T(8,128)S(1)}, u32[]{:S(2)}, u32[]{:S(2)}) %collective-permute-start.31) | collective-permute-done | bytes 278560 | tf_op jit(solution)/shard_map/ppermute | solution.py:22
  171.2 4.1 %collective-permute-done.37 = f32[17,2,16,128]{3,2,0,1:T(8,128)S(1)} collective-permute-done((f32[17,2,16,128]{3,2,0,1:T(8,128)S(1)}, f32[17,2,16,128]{3,2,0,1:T(8,128)S(1)}, u32[]{:S(2)}, u32[]{:S(2)}) %collective-permute-start.37) | collective-permute-done | bytes 278560 | tf_op jit(solution)/shard_map/ppermute | solution.py:22
  (78 shorter events, 13.9 us)
Async XLA Ops:
  6.5 68.8 %copy-start.5 = (s32[32,17,2]{0,2,1:T(2,128)S(1)}, s32[32,17,2]{0,2,1:T(2,128)}, u32[]{:S(2)}) copy-start(s32[32,17,2]{0,2,1:T(2,128)} %param.3) | copy-start | bytes 13060
  6.5 113.6 %all-gather.3.cloned.1.call-start = ((), (), s32[]{:S(2)}) async-start(), calls=%async_computation | async-start | bytes 8912896 | tf_op jit(solution)/shard_map/all_gather | solution.py:180
  7.8 8.1 %collective-permute-start = (bf16[2,128,512]{2,1,0:T(8,128)(2,1)S(1)}, bf16[2,128,512]{2,1,0:T(8,128)(2,1)S(1)}, u32[]{:S(2)}, u32[]{:S(2)}) collective-permute-start(bf16[2,128,512]{2,1,0:T(8,128)(2,1)S(1)} %get-tuple-element.55), channel_id=1, source_target_pairs={{0,16},{16,0},{1,17},{17,1},{2,18},{18,2},{3,19},{19,3},{4,20},{20... | collective-permute-start | bytes 786440 | tf_op jit(solution)/shard_map/ppermute | solution.py:22
  8.7 13.1 %collective-permute-start.3 = (bf16[2,128,512]{2,1,0:T(8,128)(2,1)S(1)}, bf16[2,128,512]{2,1,0:T(8,128)(2,1)S(1)}, u32[]{:S(2)}, u32[]{:S(2)}) collective-permute-start(bf16[2,128,512]{2,1,0:T(8,128)(2,1)S(1)} %get-tuple-element.56.refs_0_), channel_id=1, source_target_pairs={{0,224},{32,0},{64,32},{96,64},{128,96},{160,128},{192,160},{224,1... | collective-permute-start | bytes 786440 | tf_op jit(solution)/shard_map/ppermute | solution.py:22
  14.6 10.5 %collective-permute-start.2 = (bf16[2,128,512]{2,1,0:T(8,128)(2,1)S(1)}, bf16[2,128,512]{2,1,0:T(8,128)(2,1)S(1)}, u32[]{:S(2)}, u32[]{:S(2)}) collective-permute-start(bf16[2,128,512]{2,1,0:T(8,128)(2,1)S(1)} %get-tuple-element.56.refs_0_), channel_id=1, source_target_pairs={{0,32},{32,64},{64,96},{96,128},{128,160},{160,192},{192,224},{224... | collective-permute-start | bytes 786440 | tf_op jit(solution)/shard_map/ppermute | solution.py:22
  16.0 12.6 %collective-permute-start.5 = (bf16[2,128,512]{2,1,0:T(8,128)(2,1)S(1)}, bf16[2,128,512]{2,1,0:T(8,128)(2,1)S(1)}, u32[]{:S(2)}, u32[]{:S(2)}) collective-permute-start(bf16[2,128,512]{2,1,0:T(8,128)(2,1)S(1)} %collective-permute-done.refs_1_), channel_id=1, source_target_pairs={{0,224},{32,0},{64,32},{96,64},{128,96},{160,128},{192,160},{224,1... | collective-permute-start | bytes 786440 | tf_op jit(solution)/shard_map/ppermute | solution.py:22
  21.8 10.5 %collective-permute-start.4 = (bf16[2,128,512]{2,1,0:T(8,128)(2,1)S(1)}, bf16[2,128,512]{2,1,0:T(8,128)(2,1)S(1)}, u32[]{:S(2)}, u32[]{:S(2)}) collective-permute-start(bf16[2,128,512]{2,1,0:T(8,128)(2,1)S(1)} %collective-permute-done.refs_1_), channel_id=1, source_target_pairs={{0,32},{32,64},{64,96},{96,128},{128,160},{160,192},{192,224},{224... | collective-permute-start | bytes 786440 | tf_op jit(solution)/shard_map/ppermute | solution.py:22
  21.8 12.4 %collective-permute-start.8 = (bf16[2,128,512]{2,1,0:T(8,128)(2,1)S(1)}, bf16[2,128,512]{2,1,0:T(8,128)(2,1)S(1)}, u32[]{:S(2)}, u32[]{:S(2)}) collective-permute-start(bf16[2,128,512]{2,1,0:T(8,128)(2,1)S(1)} %collective-permute-done.3.refs_1_), channel_id=1, source_target_pairs={{0,224},{32,0},{64,32},{96,64},{128,96},{160,128},{192,160},{224,1... | collective-permute-start | bytes 786440 | tf_op jit(solution)/shard_map/ppermute | solution.py:22
  25.1 12.8 %collective-permute-start.7 = (bf16[2,128,512]{2,1,0:T(8,128)(2,1)S(1)}, bf16[2,128,512]{2,1,0:T(8,128)(2,1)S(1)}, u32[]{:S(2)}, u32[]{:S(2)}) collective-permute-start(bf16[2,128,512]{2,1,0:T(8,128)(2,1)S(1)} %collective-permute-done.2.refs_0_), channel_id=1, source_target_pairs={{0,32},{32,64},{64,96},{96,128},{128,160},{160,192},{192,224},{224... | collective-permute-start | bytes 786440 | tf_op jit(solution)/shard_map/ppermute | solution.py:22
  28.6 9.3 %collective-permute-start.10 = (bf16[2,128,512]{2,1,0:T(8,128)(2,1)S(1)}, bf16[2,128,512]{2,1,0:T(8,128)(2,1)S(1)}, u32[]{:S(2)}, u32[]{:S(2)}) collective-permute-start(bf16[2,128,512]{2,1,0:T(8,128)(2,1)S(1)} %collective-permute-done.5.refs_3_), channel_id=1, source_target_pairs={{0,224},{32,0},{64,32},{96,64},{128,96},{160,128},{192,160},{224,1... | collective-permute-start | bytes 786440 | tf_op jit(solution)/shard_map/ppermute | solution.py:22
  32.3 8.9 %collective-permute-start.9 = (bf16[2,128,512]{2,1,0:T(8,128)(2,1)S(1)}, bf16[2,128,512]{2,1,0:T(8,128)(2,1)S(1)}, u32[]{:S(2)}, u32[]{:S(2)}) collective-permute-start(bf16[2,128,512]{2,1,0:T(8,128)(2,1)S(1)} %collective-permute-done.4.refs_2_), channel_id=1, source_target_pairs={{0,32},{32,64},{64,96},{96,128},{128,160},{160,192},{192,224},{224... | collective-permute-start | bytes 786440 | tf_op jit(solution)/shard_map/ppermute | solution.py:22
  33.3 27.8 %collective-permute-start.6 = (bf16[4,2,128,512]{3,2,1,0:T(8,128)(2,1)}, bf16[4,2,128,512]{3,2,1,0:T(8,128)(2,1)S(1)}, u32[]{:S(2)}, u32[]{:S(2)}) collective-permute-start(bf16[4,2,128,512]{3,2,1,0:T(8,128)(2,1)} %shard_map.29.refs_2_), channel_id=1, source_target_pairs={{0,8},{8,0},{1,9},{9,1},{2,10},{10,2},{3,11},{11,3},{4,12},{12,4},... | collective-permute-start | bytes 3145736 | tf_op jit(solution)/shard_map/ppermute | solution.py:22
  42.2 18.9 %collective-permute-start.11 = (bf16[4,2,128,512]{3,2,1,0:T(8,128)(2,1)}, bf16[4,2,128,512]{3,2,1,0:T(8,128)(2,1)S(1)}, u32[]{:S(2)}, u32[]{:S(2)}) collective-permute-start(bf16[4,2,128,512]{3,2,1,0:T(8,128)(2,1)} %shard_map.30.refs_4_), channel_id=1, source_target_pairs={{0,8},{8,0},{1,9},{9,1},{2,10},{10,2},{3,11},{11,3},{4,12},{12,4},... | collective-permute-start | bytes 3145736 | tf_op jit(solution)/shard_map/ppermute | solution.py:22
  42.3 9.2 %collective-permute-start.13 = (bf16[2,128,512]{2,1,0:T(8,128)(2,1)S(1)}, bf16[2,128,512]{2,1,0:T(8,128)(2,1)S(1)}, u32[]{:S(2)}, u32[]{:S(2)}) collective-permute-start(bf16[2,128,512]{2,1,0:T(8,128)(2,1)S(1)} %collective-permute-done.8.refs_1_), channel_id=1, source_target_pairs={{0,224},{32,0},{64,32},{96,64},{128,96},{160,128},{192,160},{224,1... | collective-permute-start | bytes 786440 | tf_op jit(solution)/shard_map/ppermute | solution.py:22
  42.6 9.6 %collective-permute-start.12 = (bf16[2,128,512]{2,1,0:T(8,128)(2,1)S(1)}, bf16[2,128,512]{2,1,0:T(8,128)(2,1)S(1)}, u32[]{:S(2)}, u32[]{:S(2)}) collective-permute-start(bf16[2,128,512]{2,1,0:T(8,128)(2,1)S(1)} %collective-permute-done.7.refs_0_), channel_id=1, source_target_pairs={{0,32},{32,64},{64,96},{96,128},{128,160},{160,192},{192,224},{224... | collective-permute-start | bytes 786440 | tf_op jit(solution)/shard_map/ppermute | solution.py:22
  44.4 12.2 %collective-permute-start.15 = (bf16[2,128,512]{2,1,0:T(8,128)(2,1)S(1)}, bf16[2,128,512]{2,1,0:T(8,128)(2,1)S(1)}, u32[]{:S(2)}, u32[]{:S(2)}) collective-permute-start(bf16[2,128,512]{2,1,0:T(8,128)(2,1)S(1)} %collective-permute-done.10.refs_3_), channel_id=1, source_target_pairs={{0,224},{32,0},{64,32},{96,64},{128,96},{160,128},{192,160},{224,1... | collective-permute-start | bytes 786440 | tf_op jit(solution)/shard_map/ppermute | solution.py:22
  51.4 8.6 %collective-permute-start.14 = (bf16[2,128,512]{2,1,0:T(8,128)(2,1)S(1)}, bf16[2,128,512]{2,1,0:T(8,128)(2,1)S(1)}, u32[]{:S(2)}, u32[]{:S(2)}) collective-permute-start(bf16[2,128,512]{2,1,0:T(8,128)(2,1)S(1)} %collective-permute-done.9.refs_2_), channel_id=1, source_target_pairs={{0,32},{32,64},{64,96},{96,128},{128,160},{160,192},{192,224},{224... | collective-permute-start | bytes 786440 | tf_op jit(solution)/shard_map/ppermute | solution.py:22
  52.2 8.9 %collective-permute-start.20 = (bf16[2,128,512]{2,1,0:T(8,128)(2,1)S(1)}, bf16[2,128,512]{2,1,0:T(8,128)(2,1)S(1)}, u32[]{:S(2)}, u32[]{:S(2)}) collective-permute-start(bf16[2,128,512]{2,1,0:T(8,128)(2,1)S(1)} %get-tuple-element.57), channel_id=1, source_target_pairs={{0,16},{16,0},{1,17},{17,1},{2,18},{18,2},{3,19},{19,3},{4,20},{20... | collective-permute-start | bytes 786440 | tf_op jit(solution)/shard_map/ppermute | solution.py:22
  61.1 1.0 copy-start
  61.1 1.4 copy-start.1
  63.3 14.9 %collective-permute-start.16 = (bf16[4,2,128,512]{3,2,1,0:T(8,128)(2,1)}, bf16[4,2,128,512]{3,2,1,0:T(8,128)(2,1)}, u32[]{:S(2)}, u32[]{:S(2)}) collective-permute-start(bf16[4,2,128,512]{3,2,1,0:T(8,128)(2,1)} %shard_map.31.refs_4_.refs_6_), channel_id=1, source_target_pairs={{0,8},{8,0},{1,9},{9,1},{2,10},{10,2},{3,11},{11,3},{4,12},{12,4},... | collective-permute-start | bytes 3145736 | tf_op jit(solution)/shard_map/ppermute | solution.py:22
  63.6 9.9 %collective-permute-start.17 = (bf16[2,128,512]{2,1,0:T(8,128)(2,1)S(1)}, bf16[2,128,512]{2,1,0:T(8,128)(2,1)S(1)}, u32[]{:S(2)}, u32[]{:S(2)}) collective-permute-start(bf16[2,128,512]{2,1,0:T(8,128)(2,1)S(1)} %collective-permute-done.12.refs_0_), channel_id=1, source_target_pairs={{0,32},{32,64},{64,96},{96,128},{128,160},{160,192},{192,224},{224... | collective-permute-start | bytes 786440 | tf_op jit(solution)/shard_map/ppermute | solution.py:22
  63.7 10.7 %collective-permute-start.18 = (bf16[2,128,512]{2,1,0:T(8,128)(2,1)S(1)}, bf16[2,128,512]{2,1,0:T(8,128)(2,1)S(1)}, u32[]{:S(2)}, u32[]{:S(2)}) collective-permute-start(bf16[2,128,512]{2,1,0:T(8,128)(2,1)S(1)} %collective-permute-done.15.refs_3_), channel_id=1, source_target_pairs={{0,224},{32,0},{64,32},{96,64},{128,96},{160,128},{192,160},{224,1... | collective-permute-start | bytes 786440 | tf_op jit(solution)/shard_map/ppermute | solution.py:22
  67.7 8.0 %collective-permute-start.1 = (bf16[2,2,128,512]{3,2,1,0:T(8,128)(2,1)}, bf16[2,2,128,512]{3,2,1,0:T(8,128)(2,1)S(1)}, u32[]{:S(2)}, u32[]{:S(2)}) collective-permute-start(bf16[2,2,128,512]{3,2,1,0:T(8,128)(2,1)} %shard_map.28.refs_0_), channel_id=1, source_target_pairs={{0,8},{8,0},{1,9},{9,1},{2,10},{10,2},{3,11},{11,3},{4,12},{12,4},... | collective-permute-start | bytes 1572872 | tf_op jit(solution)/shard_map/ppermute | solution.py:22
  75.2 2.2 %collective-permute-start.19 = (bf16[2,2,128,512]{3,2,1,0:T(8,128)(2,1)}, bf16[2,2,128,512]{3,2,1,0:T(8,128)(2,1)S(1)}, u32[]{:S(2)}, u32[]{:S(2)}) collective-permute-start(bf16[2,2,128,512]{3,2,1,0:T(8,128)(2,1)} %shard_map.32.refs_8_), channel_id=1, source_target_pairs={{0,8},{8,0},{1,9},{9,1},{2,10},{10,2},{3,11},{11,3},{4,12},{12,4},... | collective-permute-start | bytes 1572872 | tf_op jit(solution)/shard_map/ppermute | solution.py:22
  75.7 1.6 copy-start.3
  77.4 0.8 copy-start.4
  86.4 17.1 %collective-permute-start.21 = (f32[4,17,16,128]{3,2,1,0:T(8,128)S(1)}, f32[4,17,16,128]{3,2,1,0:T(8,128)S(1)}, u32[]{:S(2)}, u32[]{:S(2)}) collective-permute-start(f32[4,17,16,128]{3,2,1,0:T(8,128)S(1)} %get-tuple-element.22), channel_id=1, source_target_pairs={{0,4},{16,20},{4,0},{20,16},{1,5},{17,21},{5,1},{21,17},{2,6},{18,... | collective-permute-start | bytes 1671176 | tf_op jit(solution)/shard_map/ppermute | solution.py:22
  87.9 24.6 %collective-permute-start.22 = (f32[4,17,16,128]{3,2,1,0:T(8,128)}, f32[4,17,16,128]{3,2,1,0:T(8,128)}, u32[]{:S(2)}, u32[]{:S(2)}) collective-permute-start(f32[4,17,16,128]{3,2,1,0:T(8,128)} %get-tuple-element.23), channel_id=1, source_target_pairs={{0,16},{16,4},{4,20},{20,0},{1,17},{17,5},{5,21},{21,1},{2,18},{18... | collective-permute-start | bytes 1671176 | tf_op jit(solution)/shard_map/ppermute | solution.py:22
  90.0 24.7 %collective-permute-start.23 = (f32[4,17,16,128]{3,2,1,0:T(8,128)S(1)}, f32[4,17,16,128]{3,2,1,0:T(8,128)}, u32[]{:S(2)}, u32[]{:S(2)}) collective-permute-start(f32[4,17,16,128]{3,2,1,0:T(8,128)S(1)} %get-tuple-element.24), channel_id=1, source_target_pairs={{0,20},{16,0},{4,16},{20,4},{1,21},{17,1},{5,17},{21,5},{2,22},{18... | collective-permute-start | bytes 1671176 | tf_op jit(solution)/shard_map/ppermute | solution.py:22
  90.0 26.4 %collective-permute-start.24 = (f32[4,17,16,128]{3,2,1,0:T(8,128)}, f32[4,17,16,128]{3,2,1,0:T(8,128)}, u32[]{:S(2)}, u32[]{:S(2)}) collective-permute-start(f32[4,17,16,128]{3,2,1,0:T(8,128)} %get-tuple-element.26), channel_id=1, source_target_pairs={{0,2},{1,3},{2,0},{3,1},{4,6},{5,7},{6,4},{7,5},{8,10},{9,11},{10,... | collective-permute-start | bytes 1671176 | tf_op jit(solution)/shard_map/ppermute | solution.py:22
  93.4 24.6 %collective-permute-start.25 = (f32[4,17,16,128]{3,2,1,0:T(8,128)S(1)}, f32[4,17,16,128]{3,2,1,0:T(8,128)}, u32[]{:S(2)}, u32[]{:S(2)}) collective-permute-start(f32[4,17,16,128]{3,2,1,0:T(8,128)S(1)} %get-tuple-element.27), channel_id=1, source_target_pairs={{0,1},{1,2},{2,3},{3,0},{4,5},{5,6},{6,7},{7,4},{8,9},{9,10},{10,1... | collective-permute-start | bytes 1671176 | tf_op jit(solution)/shard_map/ppermute | solution.py:22
  103.5 3.2 %copy-start.2 = (f32[4,17,16,128]{3,2,1,0:T(8,128)}, f32[4,17,16,128]{3,2,1,0:T(8,128)S(1)}, u32[]{:S(2)}) copy-start(f32[4,17,16,128]{3,2,1,0:T(8,128)S(1)} %collective-permute-done.21) | copy-start | bytes 1671172
  103.5 14.9 %collective-permute-start.26 = (f32[4,17,16,128]{3,2,1,0:T(8,128)S(1)}, f32[4,17,16,128]{3,2,1,0:T(8,128)}, u32[]{:S(2)}, u32[]{:S(2)}) collective-permute-start(f32[4,17,16,128]{3,2,1,0:T(8,128)S(1)} %get-tuple-element.28), channel_id=1, source_target_pairs={{0,3},{1,0},{2,1},{3,2},{4,7},{5,4},{6,5},{7,6},{8,11},{9,8},{10,9... | collective-permute-start | bytes 1671176 | tf_op jit(solution)/shard_map/ppermute | solution.py:22
  127.2 17.2 %collective-permute-start.27 = (f32[4,17,16,128]{3,2,1,0:T(8,128)S(1)}, f32[4,17,16,128]{3,2,1,0:T(8,128)S(1)}, u32[]{:S(2)}, u32[]{:S(2)}) collective-permute-start(f32[4,17,16,128]{3,2,1,0:T(8,128)S(1)} %get-tuple-element.30), channel_id=1, source_target_pairs={{0,4},{16,20},{4,0},{20,16},{1,5},{17,21},{5,1},{21,17},{2,6},{18,... | collective-permute-start | bytes 1671176 | tf_op jit(solution)/shard_map/ppermute | solution.py:22
  129.1 26.0 %collective-permute-start.28 = (f32[4,17,16,128]{3,2,1,0:T(8,128)S(1)}, f32[4,17,16,128]{3,2,1,0:T(8,128)S(1)}, u32[]{:S(2)}, u32[]{:S(2)}) collective-permute-start(f32[4,17,16,128]{3,2,1,0:T(8,128)S(1)} %get-tuple-element.31), channel_id=1, source_target_pairs={{0,16},{16,4},{4,20},{20,0},{1,17},{17,5},{5,21},{21,1},{2,18},{18... | collective-permute-start | bytes 1671176 | tf_op jit(solution)/shard_map/ppermute | solution.py:22
  130.3 24.8 %collective-permute-start.29 = (f32[4,17,16,128]{3,2,1,0:T(8,128)S(1)}, f32[4,17,16,128]{3,2,1,0:T(8,128)S(1)}, u32[]{:S(2)}, u32[]{:S(2)}) collective-permute-start(f32[4,17,16,128]{3,2,1,0:T(8,128)S(1)} %get-tuple-element.32), channel_id=1, source_target_pairs={{0,20},{16,0},{4,16},{20,4},{1,21},{17,1},{5,17},{21,5},{2,22},{18... | collective-permute-start | bytes 1671176 | tf_op jit(solution)/shard_map/ppermute | solution.py:22
  131.1 27.6 %collective-permute-start.33 = (f32[4,17,16,128]{3,2,1,0:T(8,128)S(1)}, f32[4,17,16,128]{3,2,1,0:T(8,128)S(1)}, u32[]{:S(2)}, u32[]{:S(2)}) collective-permute-start(f32[4,17,16,128]{3,2,1,0:T(8,128)S(1)} %get-tuple-element.34), channel_id=1, source_target_pairs={{0,2},{1,3},{2,0},{3,1},{4,6},{5,7},{6,4},{7,5},{8,10},{9,11},{10,... | collective-permute-start | bytes 1671176 | tf_op jit(solution)/shard_map/ppermute | solution.py:22
  133.1 27.3 %collective-permute-start.34 = (f32[4,17,16,128]{3,2,1,0:T(8,128)S(1)}, f32[4,17,16,128]{3,2,1,0:T(8,128)S(1)}, u32[]{:S(2)}, u32[]{:S(2)}) collective-permute-start(f32[4,17,16,128]{3,2,1,0:T(8,128)S(1)} %get-tuple-element.35), channel_id=1, source_target_pairs={{0,1},{1,2},{2,3},{3,0},{4,5},{5,6},{6,7},{7,4},{8,9},{9,10},{10,1... | collective-permute-start | bytes 1671176 | tf_op jit(solution)/shard_map/ppermute | solution.py:22
  144.4 16.0 %collective-permute-start.35 = (f32[4,17,16,128]{3,2,1,0:T(8,128)S(1)}, f32[4,17,16,128]{3,2,1,0:T(8,128)S(1)}, u32[]{:S(2)}, u32[]{:S(2)}) collective-permute-start(f32[4,17,16,128]{3,2,1,0:T(8,128)S(1)} %get-tuple-element.36), channel_id=1, source_target_pairs={{0,3},{1,0},{2,1},{3,2},{4,7},{5,4},{6,5},{7,6},{8,11},{9,8},{10,9... | collective-permute-start | bytes 1671176 | tf_op jit(solution)/shard_map/ppermute | solution.py:22
  155.3 11.2 %collective-permute-start.30 = (f32[17,2,16,128]{3,2,0,1:T(8,128)S(1)}, f32[17,2,16,128]{3,2,0,1:T(8,128)S(1)}, u32[]{:S(2)}, u32[]{:S(2)}) collective-permute-start(f32[17,2,16,128]{3,2,0,1:T(8,128)S(1)} %pad_maximum_fusion), channel_id=1, source_target_pairs={{0,2},{1,3},{2,0},{3,1},{4,6},{5,7},{6,4},{7,5},{8,10},{9,11},{10,... | collective-permute-start | bytes 835592 | tf_op jit(solution)/shard_map/ppermute | solution.py:22
  156.9 14.2 %collective-permute-start.31 = (f32[17,2,16,128]{3,2,0,1:T(8,128)S(1)}, f32[17,2,16,128]{3,2,0,1:T(8,128)S(1)}, u32[]{:S(2)}, u32[]{:S(2)}) collective-permute-start(f32[17,2,16,128]{3,2,0,1:T(8,128)S(1)} %pad_maximum_fusion.1), channel_id=1, source_target_pairs={{0,1},{1,2},{2,3},{3,0},{4,5},{5,6},{6,7},{7,4},{8,9},{9,10},{10,1... | collective-permute-start | bytes 835592 | tf_op jit(solution)/shard_map/ppermute | solution.py:22
  158.8 12.3 %collective-permute-start.32 = (f32[17,2,16,128]{3,2,0,1:T(8,128)S(1)}, f32[17,2,16,128]{3,2,0,1:T(8,128)S(1)}, u32[]{:S(2)}, u32[]{:S(2)}) collective-permute-start(f32[17,2,16,128]{3,2,0,1:T(8,128)S(1)} %pad_maximum_fusion.2), channel_id=1, source_target_pairs={{0,3},{1,0},{2,1},{3,2},{4,7},{5,4},{6,5},{7,6},{8,11},{9,8},{10,9... | collective-permute-start | bytes 835592 | tf_op jit(solution)/shard_map/ppermute | solution.py:22
  160.5 10.7 %collective-permute-start.36 = (f32[17,2,16,128]{3,2,0,1:T(8,128)S(1)}, f32[17,2,16,128]{3,2,0,1:T(8,128)S(1)}, u32[]{:S(2)}, u32[]{:S(2)}) collective-permute-start(f32[17,2,16,128]{3,2,0,1:T(8,128)S(1)} %pad_maximum_fusion.3), channel_id=1, source_target_pairs={{0,4},{16,20},{4,0},{20,16},{1,5},{17,21},{5,1},{21,17},{2,6},{18,... | collective-permute-start | bytes 835592 | tf_op jit(solution)/shard_map/ppermute | solution.py:22
  162.1 13.2 %collective-permute-start.37 = (f32[17,2,16,128]{3,2,0,1:T(8,128)S(1)}, f32[17,2,16,128]{3,2,0,1:T(8,128)S(1)}, u32[]{:S(2)}, u32[]{:S(2)}) collective-permute-start(f32[17,2,16,128]{3,2,0,1:T(8,128)S(1)} %pad_maximum_fusion.4), channel_id=1, source_target_pairs={{0,16},{16,4},{4,20},{20,0},{1,17},{17,5},{5,21},{21,1},{2,18},{18... | collective-permute-start | bytes 835592 | tf_op jit(solution)/shard_map/ppermute | solution.py:22
  166.5 9.4 %collective-permute-start.38 = (f32[17,2,16,128]{3,2,0,1:T(8,128)S(1)}, f32[17,2,16,128]{3,2,0,1:T(8,128)S(1)}, u32[]{:S(2)}, u32[]{:S(2)}) collective-permute-start(f32[17,2,16,128]{3,2,0,1:T(8,128)S(1)} %pad_maximum_fusion.5), channel_id=1, source_target_pairs={{0,20},{16,0},{4,16},{20,4},{1,21},{17,1},{5,17},{21,5},{2,22},{18... | collective-permute-start | bytes 835592 | tf_op jit(solution)/shard_map/ppermute | solution.py:22
Sparse Core Ops, SparseCore 0:
  63.4 53.2 all-gather.2

commit v2 on v1

--- a/solution.py
+++ b/solution.py
@@ -52,8 +52,8 @@
         out_specs=hbm_spec(),
         scratch_shapes=[pltpu.SemaphoreType.DMA((n,))],
         compiler_params=pltpu.CompilerParams(vmem_limit_bytes=8 * 1024 * 1024),
-        cost_estimate=pl.CostEstimate(flops=0, bytes_accessed=4 * n * arrays[0].size, transcendentals=0),
-    )(*arrays, *in_hbm(after))
+        cost_estimate=pl.CostEstimate(flops=0, bytes_accessed=16_000_000, transcendentals=0),
+    )(*arrays, *after)
 
 
 def ring_step(a, b, k):
@@ -65,44 +65,52 @@
     return (au, ad), (bu, bd)
 
 
+def place(dz, xrel, crel):
+    k = jnp.minimum(dz, NZ - dz)
+    inner = 4 * k - 2 + 2 * xrel + (dz < 4)
+    return crel * (NZ * NXL) + jnp.where(dz == 0, xrel, jnp.where(dz == 4, 14 + xrel, inner))
+
+
 def ring_gather(a, b):
-    mine = packed([a, b])
-    blocks = [(mine, (i,), (0, 0, i)) for i in range(2)]
-    far = swap(mine, "c")
-    blocks += [(far, (i,), (0, 1, i)) for i in range(2)]
+    near = [packed([a, b])]
     ra, rb = (a, a), (b, b)
-    late = []
-    for k in range(1, 5):
+    for k in range(1, 4):
         ra, rb = ring_step(ra, rb, k)
-        if k < 4:
-            mine = packed([*ra, *rb])
-            far = swap(mine, "c")
-            late.append(far)
-            for i, (dz, xr) in enumerate([(-k % NZ, 0), (k, 0), (-k % NZ, 1), (k, 1)]):
-                blocks.append((mine, (i,), (dz, 0, xr)))
-                blocks.append((far, (i,), (dz, 1, xr)))
-        if k == 3:
-            late = late[:2] + [mine]
-    mine = packed([ra[0], rb[1]])
-    far = swap(mine, "c")
-    for i in range(2):
-        blocks.append((mine, (i,), (4, 0, i)))
-        blocks.append((far, (i,), (4, 1, i)))
-    return blocks, late
-
-
-def tile_partials(slots, pos, pairs, after=()):
-    arrays = list({id(a): a for a, _, _ in pairs}.values())
-    moves = [([a is x for x in arrays].index(True), src, dst) for a, src, dst in pairs]
-    n, m = len(arrays), len(after)
-    parts = [jax.ShapeDtypeStruct((NY, K, 16, BR), jnp.float32)] * (2 * NX)
+        if k < 3:
+            near.append(packed([*ra, *rb]))
+    late = [*in_hbm(near), *ra, *rb]
+    new = list(ra + rb)
+    ra, rb = ring_step(ra, rb, 4)
+    near.append(packed([*new, ra[0], rb[1]]))
+    return near + [swap(v, "c") for v in near], late
+
+
+def tile_partials(slots, pos, stacks, after=()):
+    n, m = len(stacks), len(after)
+    starts = [sum(a.shape[0] for a in stacks[:i]) for i in range(n)]
+    parts = [jax.ShapeDtypeStruct((n2, K, 16, BR), jnp.float32) for n2 in [NY] * NX + [NX] * 3 + [NX // 2] * 2]
 
     def kernel(slots, pos, *refs):
         chunks, outs = refs[:n], refs[n + m : n + m + len(parts)]
         xs, gs, sem = refs[n + m + len(parts) :]
-        re_out, im_out = outs[:NX], outs[NX:]
+        re_out = outs[:NX]
+        im_home, im_up, im_down, im_keep_up, im_keep_down = outs[NX:]
+
+        def put_im(dy, dx, j, v):
+            low = dx < 2
+            if dy == 0:
+                im_home[dx, j] = v
+            elif dy == 2:
+                (im_up if low else im_down)[dx % 2, j] = v
+            elif dy == 1:
+                (im_keep_up if low else im_up)[dx, j] = v
+            elif low:
+                im_down[dx + 2, j] = v
+            else:
+                im_keep_down[dx - 2, j] = v
+
         loads = [
-            pltpu.make_async_copy(chunks[a].at[src], xs.at[dst], sem.at[i]) for i, (a, src, dst) in enumerate(moves)
+            pltpu.make_async_copy(chunks[i], xs.at[pl.ds(starts[i], stacks[i].shape[0])], sem.at[i]) for i in range(n)
         ]
         for load in loads:
             load.start()
@@ -115,7 +123,7 @@
                 rows[dx, dy] = (((px + dx) % NX // 2) * NY + (py + dy) % NY) * 16
 
         def block(s):
-            return xs[s // 4, (s // 2) % 2, s % 2].reshape(2 * BR, HS)
+            return xs[s].reshape(2 * BR, HS)
 
         def tile(j, buf, xr):
             t = xr * K + j
@@ -127,7 +135,7 @@
                     top = pl.ds(pl.multiple_of(rows[dx, dy], 16), 16)
                     low = pl.ds(pl.multiple_of(rows[dx, dy] + BR, 16), 16)
                     re_out[dx][dy, j] = gs[buf, top, :BR] + gs[buf, low, BR:]
-                    im_out[dy][dx, j] = gs[buf, low, :BR] - gs[buf, top, BR:]
+                    put_im(dy, dx, j, gs[buf, low, :BR] - gs[buf, top, BR:])
 
         for j in range(K):
             for xr in range(NXL):
@@ -140,19 +148,26 @@
         in_specs=[smem, smem] + [pl.BlockSpec(memory_space=pl.ANY)] * (n + m),
         out_specs=[pl.BlockSpec(memory_space=pltpu.VMEM)] * len(parts),
         scratch_shapes=[
-            pltpu.VMEM((NZ, NC, NXL, 2, BR, HS), jnp.bfloat16),
+            pltpu.VMEM((NZ * NC * NXL, 2, BR, HS), jnp.bfloat16),
             pltpu.VMEM((4, 2 * BR, 2 * BR), jnp.float32),
-            pltpu.SemaphoreType.DMA((len(pairs),)),
+            pltpu.SemaphoreType.DMA((n,)),
         ],
         compiler_params=pltpu.CompilerParams(vmem_limit_bytes=24 * 1024 * 1024),
         cost_estimate=pl.CostEstimate(flops=2 * 34 * 256 * 256 * 512, bytes_accessed=13_000_000, transcendentals=0),
-    )(slots.reshape(-1), pos, *in_hbm(arrays), *after)
+    )(slots.reshape(-1), pos, *in_hbm(stacks), *after)
     return outs[:NX], outs[NX:]
 
 
-def reduce_far(parts, axis):
-    got = [parts[0]] + [shift(parts[d], axis, NX, d) for d in (2, 1, 3)]
-    return [got[0][d] + got[1][d] + got[2][d] + got[3][d] for d in range(NY)]
+def reduce_far(re_parts, im_parts):
+    home, up, down, keep_up, keep_down = im_parts
+    got = [re_parts[0]] + [shift(re_parts[d], X_AXIS, NX, d) for d in (1, 3, 2)]
+    up, down = shift(up, "y", NY, 1), shift(down, "y", NY, -1)
+    last_up = shift(keep_up + up[:2], "y", NY, 1)
+    last_down = shift(keep_down + down[:2], "y", NY, -1)
+    re_sums = [got[0][d] + got[1][d] + got[2][d] + got[3][d] for d in range(NY)]
+    im_sums = [home[d] + down[2 + d] + last_up[d] for d in range(2)]
+    im_sums += [home[d] + up[d] + last_down[d - 2] for d in range(2, NX)]
+    return re_sums, im_sums, [*got[1:], last_up, last_down]
 
 
 def reduce_near(sums, axis):
@@ -169,22 +184,21 @@
     mine = tile_table.reshape(NZ, NXL, NC, K, 2)[z, :, c]
     mine = jnp.where(xl == 0, mine, mine[::-1])
     near = (mine // 2) % 2 ^ xl
-    slots_rel = (((mine // 4 - z) % NZ) * 4 + (mine % 2 ^ c) * 2 + near).astype(jnp.int32)
+    slots_rel = place((mine // 4 - z) % NZ, near, mine % 2 ^ c).astype(jnp.int32)
     slots_abs = ((mine // 4) * 4 + (mine % 2) * 2 + near).astype(jnp.int32)
 
     own = lax.dynamic_slice_in_dim(traces, xl * HS, HS, 3)
     other = lax.dynamic_slice_in_dim(traces, (1 - xl) * HS, HS, 3)
 
-    blocks, late = ring_gather(own[0], swap(other[0], "xl"))
+    stacks, late = ring_gather(own[0], swap(other[0], "xl"))
     both = packed([own[1], swap(other[1], "xl")], after=late)
-    whole = lax.all_gather(both, ("z", "c")).reshape(NZ, NC, NXL, 2, BR, HS)
-
-    re_parts, im_parts = tile_partials(slots_rel, pos, blocks, after=in_hbm([both]))
-    re_first, im_first = reduce_far(re_parts, X_AXIS), reduce_far(im_parts, "y")
-
-    blocks = [(whole, (dz,), (dz,)) for dz in range(NZ)]
-    re_parts, im_parts = tile_partials(slots_abs, pos, blocks, after=(*re_first, *im_first))
-    re_second, im_second = reduce_far(re_parts, X_AXIS), reduce_far(im_parts, "y")
+    whole = lax.all_gather(both, ("z", "c"), tiled=True)
+
+    re_parts, im_parts = tile_partials(slots_rel, pos, stacks, after=in_hbm([both]))
+    re_first, im_first, come = reduce_far(re_parts, im_parts)
+
+    re_parts, im_parts = tile_partials(slots_abs, pos, [whole], after=in_hbm(come))
+    re_second, im_second, _ = reduce_far(re_parts, im_parts)
     re_sum = reduce_near((re_first, re_second), "y")
     im_sum = reduce_near((im_first, im_second), X_AXIS)
     return jnp.stack([re_sum, im_sum], 2)[None]

time: 186 us -> 174 us (0.935)
  waiting for transfers between devices: 81.5 us -> 74.9 us
    ppermute x39 -> x40, waiting for transfers between devices: 81.5 us -> 74.9 us  [shift(): lax.ppermute(x, axis, [(rank(i, axis), rank((i + step) % size, axis)) for...]
    ppermute x39 -> x40, starting transfers between devices: 58.8 us -> 57.9 us  [shift(): lax.ppermute(x, axis, [(rank(i, axis), rank((i + step) % size, axis)) for...]
    pallas_call x6 -> x5, Pallas kernels: 5.43 us -> 4.94 us  [packed(): pl.pallas_call(kernel, out_shape=pltpu.HBM((n,) + arrays[0].shape, arrays...]
  transfers between devices with their start and end apart: 40 -> 41, of which waited for: 23 -> 19; matrix products, arithmetic and copies ran while one was open for 2% -> 3% of each run, Pallas kernels for 7% -> 7%
where the time goes in v2:
time: 174 us; the launch traced here: 173 us
  waiting for transfers between devices  74.9 us (43%)
  starting transfers between devices  57.9 us (33%)
  Pallas kernels  19 us (11%)
  between operations  13.7 us (8%)
  other arithmetic  4.14 us (2%)
  local copies, waits for them, and re-layouts  3.86 us (2%)
    ppermute x40, waiting for transfers between devices, shift(): lax.ppermute(x, axis, [(rank(i, axis), rank((i + step) % size, axis)) for...  74.9 us
    ppermute x40, starting transfers between devices, shift(): lax.ppermute(x, axis, [(rank(i, axis), rank((i + step) % size, axis)) for...  57.9 us
    pallas_call x2, Pallas kernels, tile_partials(): pl.pallas_call(kernel, out_shape=parts, in_specs=[smem, smem] + [pl.Block...  14 us
    pallas_call x5, Pallas kernels, packed(): pl.pallas_call(kernel, out_shape=pltpu.HBM((n,) + arrays[0].shape, arrays...  4.94 us
  transfers between devices with their start and end apart: 41, of which 19 were waited for; matrix products, arithmetic and copies ran while one was open for 3% of the time, Pallas kernels for 7%

profile of v2, /device:TPU:6, one launch (start us, length us, event | category | flops | bytes accessed | tf_op | source)
XLA Modules:
  0.0 173.5 jit_solution(7669950530085592447)
XLA Ops:
  6.5 1.3 dynamic-slice_bitcast_fusion.2
  7.8 0.9 collective-permute-start
  8.7 1.9 %collective-permute-start.1 = (bf16[2,128,512]{2,1,0:T(8,128)(2,1)S(1)}, bf16[2,128,512]{2,1,0:T(8,128)(2,1)S(1)}, u32[]{:S(2)}, u32[]{:S(2)}) collective-permute-start(bf16[2,128,512]{2,1,0:T(8,128)(2,1)S(1)} %get-tuple-element.60.refs_0_), channel_id=1, source_target_pairs={{0,32},{32,64},{64,96},{96,128},{128,160},{160,192},{192,224},{224... | collective-permute-start | bytes 786440 | tf_op jit(solution)/shard_map/ppermute | solution.py:22
  10.6 3.9 %collective-permute-start.2 = (bf16[2,128,512]{2,1,0:T(8,128)(2,1)S(1)}, bf16[2,128,512]{2,1,0:T(8,128)(2,1)S(1)}, u32[]{:S(2)}, u32[]{:S(2)}) collective-permute-start(bf16[2,128,512]{2,1,0:T(8,128)(2,1)S(1)} %get-tuple-element.60.refs_0_), channel_id=1, source_target_pairs={{0,224},{32,0},{64,32},{96,64},{128,96},{160,128},{192,160},{224,1... | collective-permute-start | bytes 786440 | tf_op jit(solution)/shard_map/ppermute | solution.py:22
  14.6 1.4 collective-permute-done.refs_1_
  15.9 5.9 %collective-permute-start.4 = (bf16[2,128,512]{2,1,0:T(8,128)(2,1)S(1)}, bf16[2,128,512]{2,1,0:T(8,128)(2,1)S(1)}, u32[]{:S(2)}, u32[]{:S(2)}) collective-permute-start(bf16[2,128,512]{2,1,0:T(8,128)(2,1)S(1)} %collective-permute-done.refs_1_), channel_id=1, source_target_pairs={{0,224},{32,0},{64,32},{96,64},{128,96},{160,128},{192,160},{224,1... | collective-permute-start | bytes 786440 | tf_op jit(solution)/shard_map/ppermute | solution.py:22
  21.8 3.3 %collective-permute-start.6 = (bf16[2,128,512]{2,1,0:T(8,128)(2,1)S(1)}, bf16[2,128,512]{2,1,0:T(8,128)(2,1)S(1)}, u32[]{:S(2)}, u32[]{:S(2)}) collective-permute-start(bf16[2,128,512]{2,1,0:T(8,128)(2,1)S(1)} %collective-permute-done.2.refs_1_), channel_id=1, source_target_pairs={{0,224},{32,0},{64,32},{96,64},{128,96},{160,128},{192,160},{224,1... | collective-permute-start | bytes 786440 | tf_op jit(solution)/shard_map/ppermute | solution.py:22
  25.1 3.4 %collective-permute-done.4.refs_3_ = bf16[2,128,512]{2,1,0:T(8,128)(2,1)S(1)} collective-permute-done((bf16[2,128,512]{2,1,0:T(8,128)(2,1)S(1)}, bf16[2,128,512]{2,1,0:T(8,128)(2,1)S(1)}, u32[]{:S(2)}, u32[]{:S(2)}) %collective-permute-start.4) | collective-permute-done | bytes 262176 | tf_op jit(solution)/shard_map/ppermute | solution.py:22
  28.5 3.7 %collective-permute-start.8 = (bf16[2,128,512]{2,1,0:T(8,128)(2,1)S(1)}, bf16[2,128,512]{2,1,0:T(8,128)(2,1)S(1)}, u32[]{:S(2)}, u32[]{:S(2)}) collective-permute-start(bf16[2,128,512]{2,1,0:T(8,128)(2,1)S(1)} %collective-permute-done.4.refs_3_), channel_id=1, source_target_pairs={{0,224},{32,0},{64,32},{96,64},{128,96},{160,128},{192,160},{224,1... | collective-permute-start | bytes 786440 | tf_op jit(solution)/shard_map/ppermute | solution.py:22
  32.2 0.8 collective-permute-start.19
  33.1 4.8 %collective-permute-done.5.refs_0_ = bf16[2,128,512]{2,1,0:T(8,128)(2,1)S(1)} collective-permute-done((bf16[2,128,512]{2,1,0:T(8,128)(2,1)S(1)}, bf16[2,128,512]{2,1,0:T(8,128)(2,1)S(1)}, u32[]{:S(2)}, u32[]{:S(2)}) %collective-permute-start.5) | collective-permute-done | bytes 262176 | tf_op jit(solution)/shard_map/ppermute | solution.py:22
  37.9 3.2 %collective-permute-start.10 = (bf16[2,128,512]{2,1,0:T(8,128)(2,1)S(1)}, bf16[2,128,512]{2,1,0:T(8,128)(2,1)S(1)}, u32[]{:S(2)}, u32[]{:S(2)}) collective-permute-start(bf16[2,128,512]{2,1,0:T(8,128)(2,1)S(1)} %collective-permute-done.6.refs_1_), channel_id=1, source_target_pairs={{0,224},{32,0},{64,32},{96,64},{128,96},{160,128},{192,160},{224,1... | collective-permute-start | bytes 786440 | tf_op jit(solution)/shard_map/ppermute | solution.py:22
  41.1 1.6 collective-permute-start.12
  44.3 1.1 shard_map.29.refs_3_.refs_1_
  45.4 1.0 shard_map.30.refs_4_.refs_2_
  46.4 2.7 %collective-permute-done.9.refs_0_.refs_5_ = bf16[2,128,512]{2,1,0:T(8,128)(2,1)S(1)} collective-permute-done((bf16[2,128,512]{2,1,0:T(8,128)(2,1)S(1)}, bf16[2,128,512]{2,1,0:T(8,128)(2,1)S(1)}, u32[]{:S(2)}, u32[]{:S(2)}) %collective-permute-start.9) | collective-permute-done | bytes 262176 | tf_op jit(solution)/shard_map/ppermute | solution.py:22
  49.1 3.3 %collective-permute-done.11.refs_2_.refs_7_ = bf16[2,128,512]{2,1,0:T(8,128)(2,1)S(1)} collective-permute-done((bf16[2,128,512]{2,1,0:T(8,128)(2,1)S(1)}, bf16[2,128,512]{2,1,0:T(8,128)(2,1)S(1)}, u32[]{:S(2)}, u32[]{:S(2)}) %collective-permute-start.11) | collective-permute-done | bytes 262176 | tf_op jit(solution)/shard_map/ppermute | solution.py:22
  53.3 3.2 %collective-permute-start.14 = (bf16[2,128,512]{2,1,0:T(8,128)(2,1)S(1)}, bf16[2,128,512]{2,1,0:T(8,128)(2,1)S(1)}, u32[]{:S(2)}, u32[]{:S(2)}) collective-permute-start(bf16[2,128,512]{2,1,0:T(8,128)(2,1)S(1)} %collective-permute-done.12.refs_3_.refs_8_), channel_id=1, source_target_pairs={{0,224},{32,0},{64,32},{96,64},{128,96},{160,128},{192,160},{224,1... | collective-permute-start | bytes 786440 | tf_op jit(solution)/shard_map/ppermute | solution.py:22
  56.6 4.3 %collective-permute-done.13.refs_4_ = bf16[2,128,512]{2,1,0:T(8,128)(2,1)S(1)} collective-permute-done((bf16[2,128,512]{2,1,0:T(8,128)(2,1)S(1)}, bf16[2,128,512]{2,1,0:T(8,128)(2,1)S(1)}, u32[]{:S(2)}, u32[]{:S(2)}) %collective-permute-start.13) | collective-permute-done | bytes 262176 | tf_op jit(solution)/shard_map/ppermute | solution.py:22
  60.9 1.2 shard_map.31.refs_3_
  63.9 5.3 %collective-permute-done.15.refs_4_ = bf16[2,2,128,512]{3,2,1,0:T(8,128)(2,1)} collective-permute-done((bf16[2,2,128,512]{3,2,1,0:T(8,128)(2,1)}, bf16[2,2,128,512]{3,2,1,0:T(8,128)(2,1)}, u32[]{:S(2)}, u32[]{:S(2)}) %collective-permute-start.15) | collective-permute-done | bytes 524320 | tf_op jit(solution)/shard_map/ppermute | solution.py:22
  70.2 7.2 %shard_map.33 = (f32[4,17,16,128]{3,2,1,0:T(8,128)S(1)}, f32[4,17,16,128]{3,2,1,0:T(8,128)S(1)}, f32[4,17,16,128]{3,2,1,0:T(8,128)S(1)}, f32[4,17,16,128]{3,2,1,...) custom-call(s32[68]{0:T(128)S(1)} %reshape.562.slots, ...), custom_call_target="tpu_custom_call" | custom-call | flops 2281701376 | bytes 13000000 | tf_op jit(solution)/shard_map/pallas_call | solution.py:145
  77.4 3.3 %collective-permute-start.25 = (f32[4,17,16,128]{3,2,1,0:T(8,128)S(1)}, f32[4,17,16,128]{3,2,1,0:T(8,128)S(1)}, u32[]{:S(2)}, u32[]{:S(2)}) collective-permute-start(f32[4,17,16,128]{3,2,1,0:T(8,128)S(1)} %get-tuple-element.30), channel_id=1, source_target_pairs={{0,3},{1,0},{2,1},{3,2},{4,7},{5,4},{6,5},{7,6},{8,11},{9,8},{10,9... | collective-permute-start | bytes 1671176 | tf_op jit(solution)/shard_map/ppermute | solution.py:22
  80.9 1.7 %collective-permute-start.21 = (f32[4,17,16,128]{3,2,1,0:T(8,128)S(1)}, f32[4,17,16,128]{3,2,1,0:T(8,128)}, u32[]{:S(2)}, u32[]{:S(2)}) collective-permute-start(f32[4,17,16,128]{3,2,1,0:T(8,128)S(1)} %get-tuple-element.25), channel_id=1, source_target_pairs={{0,20},{16,0},{4,16},{20,4},{1,21},{17,1},{5,17},{21,5},{2,22},{18... | collective-permute-start | bytes 1671176 | tf_op jit(solution)/shard_map/ppermute | solution.py:22
  82.7 1.3 collective-permute-start.22
  84.0 8.9 %collective-permute-done.25 = f32[4,17,16,128]{3,2,1,0:T(8,128)S(1)} collective-permute-done((f32[4,17,16,128]{3,2,1,0:T(8,128)S(1)}, f32[4,17,16,128]{3,2,1,0:T(8,128)S(1)}, u32[]{:S(2)}, u32[]{:S(2)}) %collective-permute-start.25) | collective-permute-done | bytes 557088 | tf_op jit(solution)/shard_map/ppermute | solution.py:22
  93.7 3.7 %collective-permute-start.26 = (f32[2,17,16,128]{3,2,1,0:T(8,128)}, f32[2,17,16,128]{3,2,1,0:T(8,128)S(1)}, u32[]{:S(2)}, u32[]{:S(2)}) collective-permute-start(f32[2,17,16,128]{3,2,1,0:T(8,128)} %slice_add_fusion.2), channel_id=1, source_target_pairs={{0,3},{1,0},{2,1},{3,2},{4,7},{5,4},{6,5},{7,6},{8,11},{9,8},{10,9... | collective-permute-start | bytes 835592 | tf_op jit(solution)/shard_map/ppermute | solution.py:22
  97.4 0.8 slice_add_fusion.3
  98.6 10.0 %collective-permute-done.21.refs_2_ = f32[4,17,16,128]{3,2,1,0:T(8,128)} collective-permute-done((f32[4,17,16,128]{3,2,1,0:T(8,128)S(1)}, f32[4,17,16,128]{3,2,1,0:T(8,128)}, u32[]{:S(2)}, u32[]{:S(2)}) %collective-permute-start.21) | collective-permute-done | bytes 557088 | tf_op jit(solution)/shard_map/ppermute | solution.py:22
  109.4 6.9 %shard_map.34 = (f32[4,17,16,128]{3,2,1,0:T(8,128)S(1)}, f32[4,17,16,128]{3,2,1,0:T(8,128)S(1)}, f32[4,17,16,128]{3,2,1,0:T(8,128)S(1)}, f32[4,17,16,128]{3,2,1,...) custom-call(s32[68]{0:T(128)S(1)} %reshape.563.slots, ...), custom_call_target="tpu_custom_call" | custom-call | flops 2281701376 | bytes 13000000 | tf_op jit(solution)/shard_map/pallas_call | solution.py:145
  116.3 3.0 %collective-permute-start.33 = (f32[4,17,16,128]{3,2,1,0:T(8,128)S(1)}, f32[4,17,16,128]{3,2,1,0:T(8,128)S(1)}, u32[]{:S(2)}, u32[]{:S(2)}) collective-permute-start(f32[4,17,16,128]{3,2,1,0:T(8,128)S(1)} %get-tuple-element.37), channel_id=1, source_target_pairs={{0,3},{1,0},{2,1},{3,2},{4,7},{5,4},{6,5},{7,6},{8,11},{9,8},{10,9... | collective-permute-start | bytes 1671176 | tf_op jit(solution)/shard_map/ppermute | solution.py:22
  119.3 1.6 fusion.21
  121.0 1.3 collective-permute-start.27
  123.1 2.0 %collective-permute-start.29 = (f32[4,17,16,128]{3,2,1,0:T(8,128)S(1)}, f32[4,17,16,128]{3,2,1,0:T(8,128)S(1)}, u32[]{:S(2)}, u32[]{:S(2)}) collective-permute-start(f32[4,17,16,128]{3,2,1,0:T(8,128)S(1)} %get-tuple-element.34), channel_id=1, source_target_pairs={{0,4},{16,20},{4,0},{20,16},{1,5},{17,21},{5,1},{21,17},{2,6},{18,... | collective-permute-start | bytes 1671176 | tf_op jit(solution)/shard_map/ppermute | solution.py:22
  125.2 4.8 %collective-permute-done.33 = f32[4,17,16,128]{3,2,1,0:T(8,128)S(1)} collective-permute-done((f32[4,17,16,128]{3,2,1,0:T(8,128)S(1)}, f32[4,17,16,128]{3,2,1,0:T(8,128)S(1)}, u32[]{:S(2)}, u32[]{:S(2)}) %collective-permute-start.33) | collective-permute-done | bytes 557088 | tf_op jit(solution)/shard_map/ppermute | solution.py:22
  130.0 3.8 %collective-permute-start.36 = (f32[2,17,16,128]{3,2,1,0:T(8,128)S(1)}, f32[2,17,16,128]{3,2,1,0:T(8,128)S(1)}, u32[]{:S(2)}, u32[]{:S(2)}) collective-permute-start(f32[2,17,16,128]{3,2,1,0:T(8,128)S(1)} %slice_add_fusion), channel_id=1, source_target_pairs={{0,3},{1,0},{2,1},{3,2},{4,7},{5,4},{6,5},{7,6},{8,11},{9,8},{10,9... | collective-permute-start | bytes 835592 | tf_op jit(solution)/shard_map/ppermute | solution.py:22
  133.9 2.7 %collective-permute-done.27 = f32[4,17,16,128]{3,2,1,0:T(8,128)S(1)} collective-permute-done((f32[4,17,16,128]{3,2,1,0:T(8,128)S(1)}, f32[4,17,16,128]{3,2,1,0:T(8,128)S(1)}, u32[]{:S(2)}, u32[]{:S(2)}) %collective-permute-start.27) | collective-permute-done | bytes 557088 | tf_op jit(solution)/shard_map/ppermute | solution.py:22
  136.6 11.6 %collective-permute-done.28 = f32[4,17,16,128]{3,2,1,0:T(8,128)S(1)} collective-permute-done((f32[4,17,16,128]{3,2,1,0:T(8,128)S(1)}, f32[4,17,16,128]{3,2,1,0:T(8,128)S(1)}, u32[]{:S(2)}, u32[]{:S(2)}) %collective-permute-start.28) | collective-permute-done | bytes 557088 | tf_op jit(solution)/shard_map/ppermute | solution.py:22
  148.4 1.6 collective-permute-start.30
  150.0 2.3 %collective-permute-start.31 = (f32[17,2,16,128]{3,2,0,1:T(8,128)S(1)}, f32[17,2,16,128]{3,2,0,1:T(8,128)S(1)}, u32[]{:S(2)}, u32[]{:S(2)}) collective-permute-start(f32[17,2,16,128]{3,2,0,1:T(8,128)S(1)} %pad_maximum_fusion.1), channel_id=1, source_target_pairs={{0,1},{1,2},{2,3},{3,0},{4,5},{5,6},{6,7},{7,4},{8,9},{9,10},{10,1... | collective-permute-start | bytes 835592 | tf_op jit(solution)/shard_map/ppermute | solution.py:22
  152.4 1.1 collective-permute-start.32
  153.6 0.9 collective-permute-start.37
  155.3 2.5 %collective-permute-done.30 = f32[17,2,16,128]{3,2,0,1:T(8,128)S(1)} collective-permute-done((f32[17,2,16,128]{3,2,0,1:T(8,128)S(1)}, f32[17,2,16,128]{3,2,0,1:T(8,128)S(1)}, u32[]{:S(2)}, u32[]{:S(2)}) %collective-permute-start.30) | collective-permute-done | bytes 278560 | tf_op jit(solution)/shard_map/ppermute | solution.py:22
  157.9 2.8 %collective-permute-done.31 = f32[17,2,16,128]{3,2,0,1:T(8,128)S(1)} collective-permute-done((f32[17,2,16,128]{3,2,0,1:T(8,128)S(1)}, f32[17,2,16,128]{3,2,0,1:T(8,128)S(1)}, u32[]{:S(2)}, u32[]{:S(2)}) %collective-permute-start.31) | collective-permute-done | bytes 278560 | tf_op jit(solution)/shard_map/ppermute | solution.py:22
  160.8 1.2 collective-permute-done.37
  162.1 1.8 %collective-permute-done.38 = f32[17,2,16,128]{3,2,0,1:T(8,128)S(1)} collective-permute-done((f32[17,2,16,128]{3,2,0,1:T(8,128)S(1)}, f32[17,2,16,128]{3,2,0,1:T(8,128)S(1)}, u32[]{:S(2)}, u32[]{:S(2)}) %collective-permute-start.38) | collective-permute-done | bytes 278560 | tf_op jit(solution)/shard_map/ppermute | solution.py:22
  163.9 1.7 collective-permute-done.39
  165.7 0.9 copy.16
  (95 shorter events, 9.9 us)
Async XLA Ops:
  6.5 102.8 %all-gather.2.cloned.1.call-start = ((), (), s32[]{:S(2)}) async-start(), calls=%async_computation | async-start | bytes 8912896 | tf_op jit(solution)/shard_map/all_gather | solution.py:195
  7.8 8.1 %collective-permute-start = (bf16[2,128,512]{2,1,0:T(8,128)(2,1)S(1)}, bf16[2,128,512]{2,1,0:T(8,128)(2,1)S(1)}, u32[]{:S(2)}, u32[]{:S(2)}) collective-permute-start(bf16[2,128,512]{2,1,0:T(8,128)(2,1)S(1)} %get-tuple-element.59), channel_id=1, source_target_pairs={{0,16},{16,0},{1,17},{17,1},{2,18},{18,2},{3,19},{19,3},{4,20},{20... | collective-permute-start | bytes 786440 | tf_op jit(solution)/shard_map/ppermute | solution.py:22
  8.7 13.1 %collective-permute-start.1 = (bf16[2,128,512]{2,1,0:T(8,128)(2,1)S(1)}, bf16[2,128,512]{2,1,0:T(8,128)(2,1)S(1)}, u32[]{:S(2)}, u32[]{:S(2)}) collective-permute-start(bf16[2,128,512]{2,1,0:T(8,128)(2,1)S(1)} %get-tuple-element.60.refs_0_), channel_id=1, source_target_pairs={{0,32},{32,64},{64,96},{96,128},{128,160},{160,192},{192,224},{224... | collective-permute-start | bytes 786440 | tf_op jit(solution)/shard_map/ppermute | solution.py:22
  10.6 11.2 %collective-permute-start.2 = (bf16[2,128,512]{2,1,0:T(8,128)(2,1)S(1)}, bf16[2,128,512]{2,1,0:T(8,128)(2,1)S(1)}, u32[]{:S(2)}, u32[]{:S(2)}) collective-permute-start(bf16[2,128,512]{2,1,0:T(8,128)(2,1)S(1)} %get-tuple-element.60.refs_0_), channel_id=1, source_target_pairs={{0,224},{32,0},{64,32},{96,64},{128,96},{160,128},{192,160},{224,1... | collective-permute-start | bytes 786440 | tf_op jit(solution)/shard_map/ppermute | solution.py:22
  15.9 12.6 %collective-permute-start.4 = (bf16[2,128,512]{2,1,0:T(8,128)(2,1)S(1)}, bf16[2,128,512]{2,1,0:T(8,128)(2,1)S(1)}, u32[]{:S(2)}, u32[]{:S(2)}) collective-permute-start(bf16[2,128,512]{2,1,0:T(8,128)(2,1)S(1)} %collective-permute-done.refs_1_), channel_id=1, source_target_pairs={{0,224},{32,0},{64,32},{96,64},{128,96},{160,128},{192,160},{224,1... | collective-permute-start | bytes 786440 | tf_op jit(solution)/shard_map/ppermute | solution.py:22
  21.8 10.5 %collective-permute-start.3 = (bf16[2,128,512]{2,1,0:T(8,128)(2,1)S(1)}, bf16[2,128,512]{2,1,0:T(8,128)(2,1)S(1)}, u32[]{:S(2)}, u32[]{:S(2)}) collective-permute-start(bf16[2,128,512]{2,1,0:T(8,128)(2,1)S(1)} %collective-permute-done.refs_1_), channel_id=1, source_target_pairs={{0,32},{32,64},{64,96},{96,128},{128,160},{160,192},{192,224},{224... | collective-permute-start | bytes 786440 | tf_op jit(solution)/shard_map/ppermute | solution.py:22
  21.8 16.1 %collective-permute-start.5 = (bf16[2,128,512]{2,1,0:T(8,128)(2,1)S(1)}, bf16[2,128,512]{2,1,0:T(8,128)(2,1)S(1)}, u32[]{:S(2)}, u32[]{:S(2)}) collective-permute-start(bf16[2,128,512]{2,1,0:T(8,128)(2,1)S(1)} %collective-permute-done.1.refs_0_), channel_id=1, source_target_pairs={{0,32},{32,64},{64,96},{96,128},{128,160},{160,192},{192,224},{224... | collective-permute-start | bytes 786440 | tf_op jit(solution)/shard_map/ppermute | solution.py:22
  21.8 16.1 %collective-permute-start.6 = (bf16[2,128,512]{2,1,0:T(8,128)(2,1)S(1)}, bf16[2,128,512]{2,1,0:T(8,128)(2,1)S(1)}, u32[]{:S(2)}, u32[]{:S(2)}) collective-permute-start(bf16[2,128,512]{2,1,0:T(8,128)(2,1)S(1)} %collective-permute-done.2.refs_1_), channel_id=1, source_target_pairs={{0,224},{32,0},{64,32},{96,64},{128,96},{160,128},{192,160},{224,1... | collective-permute-start | bytes 786440 | tf_op jit(solution)/shard_map/ppermute | solution.py:22
  28.5 12.6 %collective-permute-start.8 = (bf16[2,128,512]{2,1,0:T(8,128)(2,1)S(1)}, bf16[2,128,512]{2,1,0:T(8,128)(2,1)S(1)}, u32[]{:S(2)}, u32[]{:S(2)}) collective-permute-start(bf16[2,128,512]{2,1,0:T(8,128)(2,1)S(1)} %collective-permute-done.4.refs_3_), channel_id=1, source_target_pairs={{0,224},{32,0},{64,32},{96,64},{128,96},{160,128},{192,160},{224,1... | collective-permute-start | bytes 786440 | tf_op jit(solution)/shard_map/ppermute | solution.py:22
  32.2 11.2 %collective-permute-start.7 = (bf16[2,128,512]{2,1,0:T(8,128)(2,1)S(1)}, bf16[2,128,512]{2,1,0:T(8,128)(2,1)S(1)}, u32[]{:S(2)}, u32[]{:S(2)}) collective-permute-start(bf16[2,128,512]{2,1,0:T(8,128)(2,1)S(1)} %collective-permute-done.3.refs_2_), channel_id=1, source_target_pairs={{0,32},{32,64},{64,96},{96,128},{128,160},{160,192},{192,224},{224... | collective-permute-start | bytes 786440 | tf_op jit(solution)/shard_map/ppermute | solution.py:22
  32.2 14.2 %collective-permute-start.19 = (bf16[2,128,512]{2,1,0:T(8,128)(2,1)S(1)}, bf16[2,128,512]{2,1,0:T(8,128)(2,1)S(1)}, u32[]{:S(2)}, u32[]{:S(2)}) collective-permute-start(bf16[2,128,512]{2,1,0:T(8,128)(2,1)S(1)} %get-tuple-element.61), channel_id=1, source_target_pairs={{0,16},{16,0},{1,17},{17,1},{2,18},{18,2},{3,19},{19,3},{4,20},{20... | collective-permute-start | bytes 786440 | tf_op jit(solution)/shard_map/ppermute | solution.py:22
  37.9 11.2 %collective-permute-start.9 = (bf16[2,128,512]{2,1,0:T(8,128)(2,1)S(1)}, bf16[2,128,512]{2,1,0:T(8,128)(2,1)S(1)}, u32[]{:S(2)}, u32[]{:S(2)}) collective-permute-start(bf16[2,128,512]{2,1,0:T(8,128)(2,1)S(1)} %collective-permute-done.5.refs_0_), channel_id=1, source_target_pairs={{0,32},{32,64},{64,96},{96,128},{128,160},{160,192},{192,224},{224... | collective-permute-start | bytes 786440 | tf_op jit(solution)/shard_map/ppermute | solution.py:22
  37.9 11.2 %collective-permute-start.10 = (bf16[2,128,512]{2,1,0:T(8,128)(2,1)S(1)}, bf16[2,128,512]{2,1,0:T(8,128)(2,1)S(1)}, u32[]{:S(2)}, u32[]{:S(2)}) collective-permute-start(bf16[2,128,512]{2,1,0:T(8,128)(2,1)S(1)} %collective-permute-done.6.refs_1_), channel_id=1, source_target_pairs={{0,224},{32,0},{64,32},{96,64},{128,96},{160,128},{192,160},{224,1... | collective-permute-start | bytes 786440 | tf_op jit(solution)/shard_map/ppermute | solution.py:22
  41.1 8.0 %collective-permute-start.12 = (bf16[2,128,512]{2,1,0:T(8,128)(2,1)S(1)}, bf16[2,128,512]{2,1,0:T(8,128)(2,1)S(1)}, u32[]{:S(2)}, u32[]{:S(2)}) collective-permute-start(bf16[2,128,512]{2,1,0:T(8,128)(2,1)S(1)} %collective-permute-done.8.refs_3_), channel_id=1, source_target_pairs={{0,224},{32,0},{64,32},{96,64},{128,96},{160,128},{192,160},{224,1... | collective-permute-start | bytes 786440 | tf_op jit(solution)/shard_map/ppermute | solution.py:22
  43.5 8.9 %collective-permute-start.11 = (bf16[2,128,512]{2,1,0:T(8,128)(2,1)S(1)}, bf16[2,128,512]{2,1,0:T(8,128)(2,1)S(1)}, u32[]{:S(2)}, u32[]{:S(2)}) collective-permute-start(bf16[2,128,512]{2,1,0:T(8,128)(2,1)S(1)} %collective-permute-done.7.refs_2_), channel_id=1, source_target_pairs={{0,32},{32,64},{64,96},{96,128},{128,160},{160,192},{192,224},{224... | collective-permute-start | bytes 786440 | tf_op jit(solution)/shard_map/ppermute | solution.py:22
  53.2 9.2 %copy-start = (bf16[4,2,128,512]{3,2,1,0:T(8,128)(2,1)S(1)}, bf16[4,2,128,512]{3,2,1,0:T(8,128)(2,1)}, u32[]{:S(2)}) copy-start(bf16[4,2,128,512]{3,2,1,0:T(8,128)(2,1)} %shard_map.29.refs_3_.refs_1_) | copy-start | bytes 3145732
  53.2 9.7 %copy-start.1 = (bf16[4,2,128,512]{3,2,1,0:T(8,128)(2,1)S(1)}, bf16[4,2,128,512]{3,2,1,0:T(8,128)(2,1)}, u32[]{:S(2)}) copy-start(bf16[4,2,128,512]{3,2,1,0:T(8,128)(2,1)} %shard_map.30.refs_4_.refs_2_) | copy-start | bytes 3145732
  53.2 10.2 %copy-start.11 = (s32[32,17,2]{0,2,1:T(2,128)S(1)}, s32[32,17,2]{0,2,1:T(2,128)}, u32[]{:S(2)}) copy-start(s32[32,17,2]{0,2,1:T(2,128)} %param.3) | copy-start | bytes 13060
  53.2 7.7 %collective-permute-start.13 = (bf16[2,128,512]{2,1,0:T(8,128)(2,1)S(1)}, bf16[2,128,512]{2,1,0:T(8,128)(2,1)S(1)}, u32[]{:S(2)}, u32[]{:S(2)}) collective-permute-start(bf16[2,128,512]{2,1,0:T(8,128)(2,1)S(1)} %collective-permute-done.9.refs_0_.refs_5_), channel_id=1, source_target_pairs={{0,32},{32,64},{64,96},{96,128},{128,160},{160,192},{192,224},{224... | collective-permute-start | bytes 786440 | tf_op jit(solution)/shard_map/ppermute | solution.py:22
  53.3 7.6 %collective-permute-start.14 = (bf16[2,128,512]{2,1,0:T(8,128)(2,1)S(1)}, bf16[2,128,512]{2,1,0:T(8,128)(2,1)S(1)}, u32[]{:S(2)}, u32[]{:S(2)}) collective-permute-start(bf16[2,128,512]{2,1,0:T(8,128)(2,1)S(1)} %collective-permute-done.12.refs_3_.refs_8_), channel_id=1, source_target_pairs={{0,224},{32,0},{64,32},{96,64},{128,96},{160,128},{192,160},{224,1... | collective-permute-start | bytes 786440 | tf_op jit(solution)/shard_map/ppermute | solution.py:22
  62.1 8.1 %collective-permute-start.18 = (bf16[6,2,128,512]{3,2,1,0:T(8,128)(2,1)}, bf16[6,2,128,512]{3,2,1,0:T(8,128)(2,1)}, u32[]{:S(2)}, u32[]{:S(2)}) collective-permute-start(bf16[6,2,128,512]{3,2,1,0:T(8,128)(2,1)} %shard_map.31.refs_3_), channel_id=1, source_target_pairs={{0,8},{8,0},{1,9},{9,1},{2,10},{10,2},{3,11},{11,3},{4,12},{12,4},... | collective-permute-start | bytes 4718600 | tf_op jit(solution)/shard_map/ppermute | solution.py:22
  62.4 6.8 %collective-permute-start.16 = (bf16[4,2,128,512]{3,2,1,0:T(8,128)(2,1)S(1)}, bf16[4,2,128,512]{3,2,1,0:T(8,128)(2,1)S(1)}, u32[]{:S(2)}, u32[]{:S(2)}) collective-permute-start(bf16[4,2,128,512]{3,2,1,0:T(8,128)(2,1)S(1)} %copy-done), channel_id=1, source_target_pairs={{0,8},{8,0},{1,9},{9,1},{2,10},{10,2},{3,11},{11,3},{4,12},{12,4},... | collective-permute-start | bytes 3145736 | tf_op jit(solution)/shard_map/ppermute | solution.py:22
  62.9 7.0 %collective-permute-start.17 = (bf16[4,2,128,512]{3,2,1,0:T(8,128)(2,1)S(1)}, bf16[4,2,128,512]{3,2,1,0:T(8,128)(2,1)}, u32[]{:S(2)}, u32[]{:S(2)}) collective-permute-start(bf16[4,2,128,512]{3,2,1,0:T(8,128)(2,1)S(1)} %copy-done.1), channel_id=1, source_target_pairs={{0,8},{8,0},{1,9},{9,1},{2,10},{10,2},{3,11},{11,3},{4,12},{12,4},... | collective-permute-start | bytes 3145736 | tf_op jit(solution)/shard_map/ppermute | solution.py:22
  63.0 6.1 %collective-permute-start.15 = (bf16[2,2,128,512]{3,2,1,0:T(8,128)(2,1)}, bf16[2,2,128,512]{3,2,1,0:T(8,128)(2,1)}, u32[]{:S(2)}, u32[]{:S(2)}) collective-permute-start(bf16[2,2,128,512]{3,2,1,0:T(8,128)(2,1)} %shard_map.28.refs_2_.refs_0_), channel_id=1, source_target_pairs={{0,8},{8,0},{1,9},{9,1},{2,10},{10,2},{3,11},{11,3},{4,12},{12,4},... | collective-permute-start | bytes 1572872 | tf_op jit(solution)/shard_map/ppermute | solution.py:22
  77.4 15.5 %collective-permute-start.25 = (f32[4,17,16,128]{3,2,1,0:T(8,128)S(1)}, f32[4,17,16,128]{3,2,1,0:T(8,128)S(1)}, u32[]{:S(2)}, u32[]{:S(2)}) collective-permute-start(f32[4,17,16,128]{3,2,1,0:T(8,128)S(1)} %get-tuple-element.30), channel_id=1, source_target_pairs={{0,3},{1,0},{2,1},{3,2},{4,7},{5,4},{6,5},{7,6},{8,11},{9,8},{10,9... | collective-permute-start | bytes 1671176 | tf_op jit(solution)/shard_map/ppermute | solution.py:22
  80.6 16.8 %collective-permute-start.23 = (f32[4,17,16,128]{3,2,1,0:T(8,128)S(1)}, f32[4,17,16,128]{3,2,1,0:T(8,128)S(1)}, u32[]{:S(2)}, u32[]{:S(2)}) collective-permute-start(f32[4,17,16,128]{3,2,1,0:T(8,128)S(1)} %get-tuple-element.28), channel_id=1, source_target_pairs={{0,1},{1,2},{2,3},{3,0},{4,5},{5,6},{6,7},{7,4},{8,9},{9,10},{10,1... | collective-permute-start | bytes 1671176 | tf_op jit(solution)/shard_map/ppermute | solution.py:22
  80.6 17.9 %collective-permute-start.20 = (f32[4,17,16,128]{3,2,1,0:T(8,128)S(1)}, f32[4,17,16,128]{3,2,1,0:T(8,128)}, u32[]{:S(2)}, u32[]{:S(2)}) collective-permute-start(f32[4,17,16,128]{3,2,1,0:T(8,128)S(1)} %get-tuple-element.24), channel_id=1, source_target_pairs={{0,16},{16,4},{4,20},{20,0},{1,17},{17,5},{5,21},{21,1},{2,18},{18... | collective-permute-start | bytes 1671176 | tf_op jit(solution)/shard_map/ppermute | solution.py:22
  80.9 27.7 %collective-permute-start.21 = (f32[4,17,16,128]{3,2,1,0:T(8,128)S(1)}, f32[4,17,16,128]{3,2,1,0:T(8,128)}, u32[]{:S(2)}, u32[]{:S(2)}) collective-permute-start(f32[4,17,16,128]{3,2,1,0:T(8,128)S(1)} %get-tuple-element.25), channel_id=1, source_target_pairs={{0,20},{16,0},{4,16},{20,4},{1,21},{17,1},{5,17},{21,5},{2,22},{18... | collective-permute-start | bytes 1671176 | tf_op jit(solution)/shard_map/ppermute | solution.py:22
  82.7 25.9 %collective-permute-start.22 = (f32[4,17,16,128]{3,2,1,0:T(8,128)S(1)}, f32[4,17,16,128]{3,2,1,0:T(8,128)}, u32[]{:S(2)}, u32[]{:S(2)}) collective-permute-start(f32[4,17,16,128]{3,2,1,0:T(8,128)S(1)} %get-tuple-element.26), channel_id=1, source_target_pairs={{0,4},{16,20},{4,0},{20,16},{1,5},{17,21},{5,1},{21,17},{2,6},{18,... | collective-permute-start | bytes 1671176 | tf_op jit(solution)/shard_map/ppermute | solution.py:22
  93.7 14.8 %collective-permute-start.26 = (f32[2,17,16,128]{3,2,1,0:T(8,128)}, f32[2,17,16,128]{3,2,1,0:T(8,128)S(1)}, u32[]{:S(2)}, u32[]{:S(2)}) collective-permute-start(f32[2,17,16,128]{3,2,1,0:T(8,128)} %slice_add_fusion.2), channel_id=1, source_target_pairs={{0,3},{1,0},{2,1},{3,2},{4,7},{5,4},{6,5},{7,6},{8,11},{9,8},{10,9... | collective-permute-start | bytes 835592 | tf_op jit(solution)/shard_map/ppermute | solution.py:22
  98.3 10.3 %collective-permute-start.24 = (f32[2,17,16,128]{3,2,1,0:T(8,128)}, f32[2,17,16,128]{3,2,1,0:T(8,128)S(1)}, u32[]{:S(2)}, u32[]{:S(2)}) collective-permute-start(f32[2,17,16,128]{3,2,1,0:T(8,128)} %slice_add_fusion.3), channel_id=1, source_target_pairs={{0,1},{1,2},{2,3},{3,0},{4,5},{5,6},{6,7},{7,4},{8,9},{9,10},{10,1... | collective-permute-start | bytes 835592 | tf_op jit(solution)/shard_map/ppermute | solution.py:22
  116.3 8.8 %copy-start.3 = (f32[2,17,16,128]{3,2,1,0:T(8,128)S(1)}, f32[2,17,16,128]{3,2,1,0:T(8,128)}, u32[]{:S(2)}) copy-start(f32[2,17,16,128]{3,2,1,0:T(8,128)} %copy-done.2) | copy-start | bytes 835588
  116.3 8.8 %copy-start.5 = (f32[2,17,16,128]{3,2,1,0:T(8,128)S(1)}, f32[2,17,16,128]{3,2,1,0:T(8,128)}, u32[]{:S(2)}) copy-start(f32[2,17,16,128]{3,2,1,0:T(8,128)} %copy-done.4) | copy-start | bytes 835588
  116.3 8.8 %copy-start.8 = (f32[4,17,16,128]{3,2,1,0:T(8,128)S(1)}, f32[4,17,16,128]{3,2,1,0:T(8,128)}, u32[]{:S(2)}) copy-start(f32[4,17,16,128]{3,2,1,0:T(8,128)} %copy-done.7) | copy-start | bytes 1671172
  116.3 8.8 %copy-start.10 = (f32[4,17,16,128]{3,2,1,0:T(8,128)S(1)}, f32[4,17,16,128]{3,2,1,0:T(8,128)}, u32[]{:S(2)}) copy-start(f32[4,17,16,128]{3,2,1,0:T(8,128)} %copy-done.9) | copy-start | bytes 1671172
  116.3 13.7 %collective-permute-start.33 = (f32[4,17,16,128]{3,2,1,0:T(8,128)S(1)}, f32[4,17,16,128]{3,2,1,0:T(8,128)S(1)}, u32[]{:S(2)}, u32[]{:S(2)}) collective-permute-start(f32[4,17,16,128]{3,2,1,0:T(8,128)S(1)} %get-tuple-element.37), channel_id=1, source_target_pairs={{0,3},{1,0},{2,1},{3,2},{4,7},{5,4},{6,5},{7,6},{8,11},{9,8},{10,9... | collective-permute-start | bytes 1671176 | tf_op jit(solution)/shard_map/ppermute | solution.py:22
  119.3 14.4 %collective-permute-start.34 = (f32[4,17,16,128]{3,2,1,0:T(8,128)S(1)}, f32[4,17,16,128]{3,2,1,0:T(8,128)S(1)}, u32[]{:S(2)}, u32[]{:S(2)}) collective-permute-start(f32[4,17,16,128]{3,2,1,0:T(8,128)S(1)} %get-tuple-element.39), channel_id=1, source_target_pairs={{0,1},{1,2},{2,3},{3,0},{4,5},{5,6},{6,7},{7,4},{8,9},{9,10},{10,1... | collective-permute-start | bytes 1671176 | tf_op jit(solution)/shard_map/ppermute | solution.py:22
  121.0 15.6 %collective-permute-start.27 = (f32[4,17,16,128]{3,2,1,0:T(8,128)S(1)}, f32[4,17,16,128]{3,2,1,0:T(8,128)S(1)}, u32[]{:S(2)}, u32[]{:S(2)}) collective-permute-start(f32[4,17,16,128]{3,2,1,0:T(8,128)S(1)} %get-tuple-element.32), channel_id=1, source_target_pairs={{0,16},{16,4},{4,20},{20,0},{1,17},{17,5},{5,21},{21,1},{2,18},{18... | collective-permute-start | bytes 1671176 | tf_op jit(solution)/shard_map/ppermute | solution.py:22
  122.3 25.9 %collective-permute-start.28 = (f32[4,17,16,128]{3,2,1,0:T(8,128)S(1)}, f32[4,17,16,128]{3,2,1,0:T(8,128)S(1)}, u32[]{:S(2)}, u32[]{:S(2)}) collective-permute-start(f32[4,17,16,128]{3,2,1,0:T(8,128)S(1)} %get-tuple-element.33), channel_id=1, source_target_pairs={{0,20},{16,0},{4,16},{20,4},{1,21},{17,1},{5,17},{21,5},{2,22},{18... | collective-permute-start | bytes 1671176 | tf_op jit(solution)/shard_map/ppermute | solution.py:22
  123.1 25.1 %collective-permute-start.29 = (f32[4,17,16,128]{3,2,1,0:T(8,128)S(1)}, f32[4,17,16,128]{3,2,1,0:T(8,128)S(1)}, u32[]{:S(2)}, u32[]{:S(2)}) collective-permute-start(f32[4,17,16,128]{3,2,1,0:T(8,128)S(1)} %get-tuple-element.34), channel_id=1, source_target_pairs={{0,4},{16,20},{4,0},{20,16},{1,5},{17,21},{5,1},{21,17},{2,6},{18,... | collective-permute-start | bytes 1671176 | tf_op jit(solution)/shard_map/ppermute | solution.py:22
  130.0 23.4 %collective-permute-start.36 = (f32[2,17,16,128]{3,2,1,0:T(8,128)S(1)}, f32[2,17,16,128]{3,2,1,0:T(8,128)S(1)}, u32[]{:S(2)}, u32[]{:S(2)}) collective-permute-start(f32[2,17,16,128]{3,2,1,0:T(8,128)S(1)} %slice_add_fusion), channel_id=1, source_target_pairs={{0,3},{1,0},{2,1},{3,2},{4,7},{5,4},{6,5},{7,6},{8,11},{9,8},{10,9... | collective-permute-start | bytes 835592 | tf_op jit(solution)/shard_map/ppermute | solution.py:22
  133.8 19.6 %collective-permute-start.35 = (f32[2,17,16,128]{3,2,1,0:T(8,128)S(1)}, f32[2,17,16,128]{3,2,1,0:T(8,128)S(1)}, u32[]{:S(2)}, u32[]{:S(2)}) collective-permute-start(f32[2,17,16,128]{3,2,1,0:T(8,128)S(1)} %slice_add_fusion.1), channel_id=1, source_target_pairs={{0,1},{1,2},{2,3},{3,0},{4,5},{5,6},{6,7},{7,4},{8,9},{9,10},{10,1... | collective-permute-start | bytes 835592 | tf_op jit(solution)/shard_map/ppermute | solution.py:22
  148.4 9.5 %collective-permute-start.30 = (f32[17,2,16,128]{3,2,0,1:T(8,128)S(1)}, f32[17,2,16,128]{3,2,0,1:T(8,128)S(1)}, u32[]{:S(2)}, u32[]{:S(2)}) collective-permute-start(f32[17,2,16,128]{3,2,0,1:T(8,128)S(1)} %pad_maximum_fusion), channel_id=1, source_target_pairs={{0,2},{1,3},{2,0},{3,1},{4,6},{5,7},{6,4},{7,5},{8,10},{9,11},{10,... | collective-permute-start | bytes 835592 | tf_op jit(solution)/shard_map/ppermute | solution.py:22
  150.0 10.7 %collective-permute-start.31 = (f32[17,2,16,128]{3,2,0,1:T(8,128)S(1)}, f32[17,2,16,128]{3,2,0,1:T(8,128)S(1)}, u32[]{:S(2)}, u32[]{:S(2)}) collective-permute-start(f32[17,2,16,128]{3,2,0,1:T(8,128)S(1)} %pad_maximum_fusion.1), channel_id=1, source_target_pairs={{0,1},{1,2},{2,3},{3,0},{4,5},{5,6},{6,7},{7,4},{8,9},{9,10},{10,1... | collective-permute-start | bytes 835592 | tf_op jit(solution)/shard_map/ppermute | solution.py:22
  152.4 8.4 %collective-permute-start.32 = (f32[17,2,16,128]{3,2,0,1:T(8,128)S(1)}, f32[17,2,16,128]{3,2,0,1:T(8,128)S(1)}, u32[]{:S(2)}, u32[]{:S(2)}) collective-permute-start(f32[17,2,16,128]{3,2,0,1:T(8,128)S(1)} %pad_maximum_fusion.2), channel_id=1, source_target_pairs={{0,3},{1,0},{2,1},{3,2},{4,7},{5,4},{6,5},{7,6},{8,11},{9,8},{10,9... | collective-permute-start | bytes 835592 | tf_op jit(solution)/shard_map/ppermute | solution.py:22
  153.6 8.5 %collective-permute-start.37 = (f32[17,2,16,128]{3,2,0,1:T(8,128)S(1)}, f32[17,2,16,128]{3,2,0,1:T(8,128)S(1)}, u32[]{:S(2)}, u32[]{:S(2)}) collective-permute-start(f32[17,2,16,128]{3,2,0,1:T(8,128)S(1)} %pad_maximum_fusion.3), channel_id=1, source_target_pairs={{0,4},{16,20},{4,0},{20,16},{1,5},{17,21},{5,1},{21,17},{2,6},{18,... | collective-permute-start | bytes 835592 | tf_op jit(solution)/shard_map/ppermute | solution.py:22
  154.6 9.4 %collective-permute-start.38 = (f32[17,2,16,128]{3,2,0,1:T(8,128)S(1)}, f32[17,2,16,128]{3,2,0,1:T(8,128)S(1)}, u32[]{:S(2)}, u32[]{:S(2)}) collective-permute-start(f32[17,2,16,128]{3,2,0,1:T(8,128)S(1)} %pad_maximum_fusion.4), channel_id=1, source_target_pairs={{0,16},{16,4},{4,20},{20,0},{1,17},{17,5},{5,21},{21,1},{2,18},{18... | collective-permute-start | bytes 835592 | tf_op jit(solution)/shard_map/ppermute | solution.py:22
  157.9 7.8 %collective-permute-start.39 = (f32[17,2,16,128]{3,2,0,1:T(8,128)S(1)}, f32[17,2,16,128]{3,2,0,1:T(8,128)S(1)}, u32[]{:S(2)}, u32[]{:S(2)}) collective-permute-start(f32[17,2,16,128]{3,2,0,1:T(8,128)S(1)} %pad_maximum_fusion.5), channel_id=1, source_target_pairs={{0,20},{16,0},{4,16},{20,4},{1,21},{17,1},{5,17},{21,5},{2,22},{18... | collective-permute-start | bytes 835592 | tf_op jit(solution)/shard_map/ppermute | solution.py:22
  (5 other events, 8.8 us)
Sparse Core Ops, SparseCore 0:
  53.3 53.6 all-gather.1

commit v3 on v2

--- a/solution.py
+++ b/solution.py
@@ -85,29 +85,34 @@
     return near + [swap(v, "c") for v in near], late
 
 
-def tile_partials(slots, pos, stacks, after=()):
+def tile_partials(slots, pos, stacks, direct, after=()):
     n, m = len(stacks), len(after)
     starts = [sum(a.shape[0] for a in stacks[:i]) for i in range(n)]
-    parts = [jax.ShapeDtypeStruct((n2, K, 16, BR), jnp.float32) for n2 in [NY] * NX + [NX] * 3 + [NX // 2] * 2]
+    ring_sizes = [NX] * 3 + [NX // 2] * 2
+    re_sizes = [NY] * NX if direct else ring_sizes
+    parts = [jax.ShapeDtypeStruct((n2, K, 16, BR), jnp.float32) for n2 in re_sizes + ring_sizes]
 
     def kernel(slots, pos, *refs):
         chunks, outs = refs[:n], refs[n + m : n + m + len(parts)]
-        xs, gs, sem = refs[n + m + len(parts) :]
-        re_out = outs[:NX]
-        im_home, im_up, im_down, im_keep_up, im_keep_down = outs[NX:]
-
-        def put_im(dy, dx, j, v):
-            low = dx < 2
-            if dy == 0:
-                im_home[dx, j] = v
-            elif dy == 2:
-                (im_up if low else im_down)[dx % 2, j] = v
-            elif dy == 1:
-                (im_keep_up if low else im_up)[dx, j] = v
+        xs, sem = refs[n + m + len(parts) :]
+        re_out, im_out = outs[: len(re_sizes)], outs[len(re_sizes) :]
+
+        def put(refs, d1, d2, j, v):
+            if len(refs) == NX:
+                refs[d1][d2, j] = v
+                return
+            home, up, down, keep_up, keep_down = refs
+            low = d2 < 2
+            if d1 == 0:
+                home[d2, j] = v
+            elif d1 == 2:
+                (up if low else down)[d2 % 2, j] = v
+            elif d1 == 1:
+                (keep_up if low else up)[d2, j] = v
             elif low:
-                im_down[dx + 2, j] = v
+                down[d2 + 2, j] = v
             else:
-                im_keep_down[dx - 2, j] = v
+                keep_down[d2 - 2, j] = v
 
         loads = [
             pltpu.make_async_copy(chunks[i], xs.at[pl.ds(starts[i], stacks[i].shape[0])], sem.at[i]) for i in range(n)
@@ -122,24 +127,24 @@
             for dy in range(NY):
                 rows[dx, dy] = (((px + dx) % NX // 2) * NY + (py + dy) % NY) * 16
 
-        def block(s):
-            return xs[s].reshape(2 * BR, HS)
-
-        def tile(j, buf, xr):
+        def tile(j, xr):
             t = xr * K + j
-            u = block(slots[2 * t])
-            v = block(slots[2 * t + 1])
-            gs[buf] = lax.dot_general(u, v, (((1,), (1,)), ((), ())), preferred_element_type=jnp.float32)
-            for dx in (xr, xr + 2):
-                for dy in range(NY):
-                    top = pl.ds(pl.multiple_of(rows[dx, dy], 16), 16)
-                    low = pl.ds(pl.multiple_of(rows[dx, dy] + BR, 16), 16)
-                    re_out[dx][dy, j] = gs[buf, top, :BR] + gs[buf, low, BR:]
-                    put_im(dy, dx, j, gs[buf, low, :BR] - gs[buf, top, BR:])
+            row_block, col_block = slots[2 * t], slots[2 * t + 1]
+            groups = [(dx, dy) for dx in (xr, xr + 2) for dy in range(NY)]
+            u = [xs[row_block, part, pl.ds(pl.multiple_of(rows[g], 16), 16)] for part in range(2) for g in groups]
+            v = xs[col_block].reshape(2 * BR, HS)
+            g = lax.dot_general(
+                jnp.concatenate(u, 0), v, (((1,), (1,)), ((), ())), preferred_element_type=jnp.float32
+            )
+            re_tile = g[:BR, :BR] + g[BR:, BR:]
+            im_tile = g[BR:, :BR] - g[:BR, BR:]
+            for i, (dx, dy) in enumerate(groups):
+                put(re_out, dx, dy, j, re_tile[i * 16 : (i + 1) * 16])
+                put(im_out, dy, dx, j, im_tile[i * 16 : (i + 1) * 16])
 
         for j in range(K):
             for xr in range(NXL):
-                tile(j, (2 * j + xr) % 4, xr)
+                tile(j, xr)
 
     smem = pl.BlockSpec(memory_space=pltpu.SMEM)
     outs = pl.pallas_call(
@@ -149,25 +154,27 @@
         out_specs=[pl.BlockSpec(memory_space=pltpu.VMEM)] * len(parts),
         scratch_shapes=[
             pltpu.VMEM((NZ * NC * NXL, 2, BR, HS), jnp.bfloat16),
-            pltpu.VMEM((4, 2 * BR, 2 * BR), jnp.float32),
             pltpu.SemaphoreType.DMA((n,)),
         ],
         compiler_params=pltpu.CompilerParams(vmem_limit_bytes=24 * 1024 * 1024),
         cost_estimate=pl.CostEstimate(flops=2 * 34 * 256 * 256 * 512, bytes_accessed=13_000_000, transcendentals=0),
     )(slots.reshape(-1), pos, *in_hbm(stacks), *after)
-    return outs[:NX], outs[NX:]
-
-
-def reduce_far(re_parts, im_parts):
-    home, up, down, keep_up, keep_down = im_parts
-    got = [re_parts[0]] + [shift(re_parts[d], X_AXIS, NX, d) for d in (1, 3, 2)]
-    up, down = shift(up, "y", NY, 1), shift(down, "y", NY, -1)
-    last_up = shift(keep_up + up[:2], "y", NY, 1)
-    last_down = shift(keep_down + down[:2], "y", NY, -1)
-    re_sums = [got[0][d] + got[1][d] + got[2][d] + got[3][d] for d in range(NY)]
-    im_sums = [home[d] + down[2 + d] + last_up[d] for d in range(2)]
-    im_sums += [home[d] + up[d] + last_down[d - 2] for d in range(2, NX)]
-    return re_sums, im_sums, [*got[1:], last_up, last_down]
+    return outs[: len(re_sizes)], outs[len(re_sizes) :]
+
+
+def reduce_direct(parts, axis):
+    got = [parts[0]] + [shift(parts[d], axis, NX, d) for d in (1, 3, 2)]
+    return [got[0][d] + got[1][d] + got[2][d] + got[3][d] for d in range(NY)], got[1:]
+
+
+def reduce_ring(parts, axis):
+    home, up, down, keep_up, keep_down = parts
+    up, down = shift(up, axis, NX, 1), shift(down, axis, NX, -1)
+    last_up = shift(keep_up + up[:2], axis, NX, 1)
+    last_down = shift(keep_down + down[:2], axis, NX, -1)
+    sums = [home[d] + down[2 + d] + last_up[d] for d in range(2)]
+    sums += [home[d] + up[d] + last_down[d - 2] for d in range(2, NX)]
+    return sums, [last_up, last_down]
 
 
 def reduce_near(sums, axis):
@@ -194,11 +201,13 @@
     both = packed([own[1], swap(other[1], "xl")], after=late)
     whole = lax.all_gather(both, ("z", "c"), tiled=True)
 
-    re_parts, im_parts = tile_partials(slots_rel, pos, stacks, after=in_hbm([both]))
-    re_first, im_first, come = reduce_far(re_parts, im_parts)
-
-    re_parts, im_parts = tile_partials(slots_abs, pos, [whole], after=in_hbm(come))
-    re_second, im_second, _ = reduce_far(re_parts, im_parts)
+    re_parts, im_parts = tile_partials(slots_rel, pos, stacks, True, after=in_hbm([both]))
+    re_first, re_come = reduce_direct(re_parts, X_AXIS)
+    im_first, _ = reduce_ring(im_parts, "y")
+
+    re_parts, im_parts = tile_partials(slots_abs, pos, [whole], False, after=[*in_hbm(re_come), *im_first])
+    re_second, _ = reduce_ring(re_parts, X_AXIS)
+    im_second, _ = reduce_ring(im_parts, "y")
     re_sum = reduce_near((re_first, re_second), "y")
     im_sum = reduce_near((im_first, im_second), X_AXIS)
     return jnp.stack([re_sum, im_sum], 2)[None]

time: 174 us -> 171 us (0.983)
  waiting for transfers between devices: 74.9 us -> 66.7 us
  starting transfers between devices: 57.9 us -> 61.8 us
  other arithmetic: 4.14 us -> 7.75 us
    ppermute x40 -> x41, waiting for transfers between devices: 74.9 us -> 66.6 us  [shift(): lax.ppermute(x, axis, [(rank(i, axis), rank((i + step) % size, axis)) for...]
    ppermute x40 -> x41, starting transfers between devices: 57.9 us -> 61.8 us  [shift(): lax.ppermute(x, axis, [(rank(i, axis), rank((i + step) % size, axis)) for...]
    add x8 -> x11, other arithmetic: 3.68 us -> 7.23 us  [the longest x3 1.96 us: reduce_ring(): sums = [home[d] + down[2 + d] + last_up[d] for d in range(2)]]
  transfers between devices with their start and end apart: 41 -> 42, of which waited for: 19 -> 19; matrix products, arithmetic and copies ran while one was open for 3% -> 5% of each run, Pallas kernels for 7% -> 6%
where the time goes in v3:
time: 171 us
  waiting for transfers between devices  66.7 us (39%)
  starting transfers between devices  61.8 us (36%)
  Pallas kernels  18.1 us (11%)
  between operations  13.7 us (8%)
  other arithmetic  7.75 us (5%)
  local copies, waits for them, and re-layouts  3.06 us (2%)
    ppermute x41, waiting for transfers between devices, shift(): lax.ppermute(x, axis, [(rank(i, axis), rank((i + step) % size, axis)) for...  66.6 us
    ppermute x41, starting transfers between devices, shift(): lax.ppermute(x, axis, [(rank(i, axis), rank((i + step) % size, axis)) for...  61.8 us
    pallas_call x2, Pallas kernels, tile_partials(): pl.pallas_call(kernel, out_shape=parts, in_specs=[smem, smem] + [pl.Block...  13.2 us
    pallas_call x5, Pallas kernels, packed(): pl.pallas_call(kernel, out_shape=pltpu.HBM((n,) + arrays[0].shape, arrays...  4.94 us
  transfers between devices with their start and end apart: 42, of which 19 were waited for; matrix products, arithmetic and copies ran while one was open for 5% of the time, Pallas kernels for 6%

profile of v3, /device:TPU:6, one launch (start us, length us, event | category | flops | bytes accessed | tf_op | source)
XLA Modules:
  0.0 171.2 jit_solution(11580063430948560944)
XLA Ops:
  6.5 1.3 dynamic-slice_bitcast_fusion.2
  7.8 0.9 collective-permute-start
  8.7 1.9 %collective-permute-start.1 = (bf16[2,128,512]{2,1,0:T(8,128)(2,1)S(1)}, bf16[2,128,512]{2,1,0:T(8,128)(2,1)S(1)}, u32[]{:S(2)}, u32[]{:S(2)}) collective-permute-start(bf16[2,128,512]{2,1,0:T(8,128)(2,1)S(1)} %get-tuple-element.66.refs_0_), channel_id=1, source_target_pairs={{0,32},{32,64},{64,96},{96,128},{128,160},{160,192},{192,224},{224... | collective-permute-start | bytes 786440 | tf_op jit(solution)/shard_map/ppermute | solution.py:22
  10.6 3.9 %collective-permute-start.2 = (bf16[2,128,512]{2,1,0:T(8,128)(2,1)S(1)}, bf16[2,128,512]{2,1,0:T(8,128)(2,1)S(1)}, u32[]{:S(2)}, u32[]{:S(2)}) collective-permute-start(bf16[2,128,512]{2,1,0:T(8,128)(2,1)S(1)} %get-tuple-element.66.refs_0_), channel_id=1, source_target_pairs={{0,224},{32,0},{64,32},{96,64},{128,96},{160,128},{192,160},{224,1... | collective-permute-start | bytes 786440 | tf_op jit(solution)/shard_map/ppermute | solution.py:22
  14.6 1.4 collective-permute-done.refs_1_
  15.9 5.9 %collective-permute-start.4 = (bf16[2,128,512]{2,1,0:T(8,128)(2,1)S(1)}, bf16[2,128,512]{2,1,0:T(8,128)(2,1)S(1)}, u32[]{:S(2)}, u32[]{:S(2)}) collective-permute-start(bf16[2,128,512]{2,1,0:T(8,128)(2,1)S(1)} %collective-permute-done.refs_1_), channel_id=1, source_target_pairs={{0,224},{32,0},{64,32},{96,64},{128,96},{160,128},{192,160},{224,1... | collective-permute-start | bytes 786440 | tf_op jit(solution)/shard_map/ppermute | solution.py:22
  21.8 3.3 %collective-permute-start.6 = (bf16[2,128,512]{2,1,0:T(8,128)(2,1)S(1)}, bf16[2,128,512]{2,1,0:T(8,128)(2,1)S(1)}, u32[]{:S(2)}, u32[]{:S(2)}) collective-permute-start(bf16[2,128,512]{2,1,0:T(8,128)(2,1)S(1)} %collective-permute-done.2.refs_1_), channel_id=1, source_target_pairs={{0,224},{32,0},{64,32},{96,64},{128,96},{160,128},{192,160},{224,1... | collective-permute-start | bytes 786440 | tf_op jit(solution)/shard_map/ppermute | solution.py:22
  25.1 3.4 %collective-permute-done.4.refs_3_ = bf16[2,128,512]{2,1,0:T(8,128)(2,1)S(1)} collective-permute-done((bf16[2,128,512]{2,1,0:T(8,128)(2,1)S(1)}, bf16[2,128,512]{2,1,0:T(8,128)(2,1)S(1)}, u32[]{:S(2)}, u32[]{:S(2)}) %collective-permute-start.4) | collective-permute-done | bytes 262176 | tf_op jit(solution)/shard_map/ppermute | solution.py:22
  28.5 3.7 %collective-permute-start.8 = (bf16[2,128,512]{2,1,0:T(8,128)(2,1)S(1)}, bf16[2,128,512]{2,1,0:T(8,128)(2,1)S(1)}, u32[]{:S(2)}, u32[]{:S(2)}) collective-permute-start(bf16[2,128,512]{2,1,0:T(8,128)(2,1)S(1)} %collective-permute-done.4.refs_3_), channel_id=1, source_target_pairs={{0,224},{32,0},{64,32},{96,64},{128,96},{160,128},{192,160},{224,1... | collective-permute-start | bytes 786440 | tf_op jit(solution)/shard_map/ppermute | solution.py:22
  33.1 4.8 %collective-permute-done.5.refs_0_ = bf16[2,128,512]{2,1,0:T(8,128)(2,1)S(1)} collective-permute-done((bf16[2,128,512]{2,1,0:T(8,128)(2,1)S(1)}, bf16[2,128,512]{2,1,0:T(8,128)(2,1)S(1)}, u32[]{:S(2)}, u32[]{:S(2)}) %collective-permute-start.5) | collective-permute-done | bytes 262176 | tf_op jit(solution)/shard_map/ppermute | solution.py:22
  37.9 3.2 %collective-permute-start.10 = (bf16[2,128,512]{2,1,0:T(8,128)(2,1)S(1)}, bf16[2,128,512]{2,1,0:T(8,128)(2,1)S(1)}, u32[]{:S(2)}, u32[]{:S(2)}) collective-permute-start(bf16[2,128,512]{2,1,0:T(8,128)(2,1)S(1)} %collective-permute-done.6.refs_1_), channel_id=1, source_target_pairs={{0,224},{32,0},{64,32},{96,64},{128,96},{160,128},{192,160},{224,1... | collective-permute-start | bytes 786440 | tf_op jit(solution)/shard_map/ppermute | solution.py:22
  41.1 1.6 collective-permute-start.12
  44.3 1.1 shard_map.29.refs_3_.refs_1_
  45.4 1.0 shard_map.30.refs_4_.refs_2_
  46.4 2.7 %collective-permute-done.9.refs_0_.refs_5_ = bf16[2,128,512]{2,1,0:T(8,128)(2,1)S(1)} collective-permute-done((bf16[2,128,512]{2,1,0:T(8,128)(2,1)S(1)}, bf16[2,128,512]{2,1,0:T(8,128)(2,1)S(1)}, u32[]{:S(2)}, u32[]{:S(2)}) %collective-permute-start.9) | collective-permute-done | bytes 262176 | tf_op jit(solution)/shard_map/ppermute | solution.py:22
  49.1 3.3 %collective-permute-done.11.refs_2_.refs_7_ = bf16[2,128,512]{2,1,0:T(8,128)(2,1)S(1)} collective-permute-done((bf16[2,128,512]{2,1,0:T(8,128)(2,1)S(1)}, bf16[2,128,512]{2,1,0:T(8,128)(2,1)S(1)}, u32[]{:S(2)}, u32[]{:S(2)}) %collective-permute-start.11) | collective-permute-done | bytes 262176 | tf_op jit(solution)/shard_map/ppermute | solution.py:22
  53.3 3.2 %collective-permute-start.14 = (bf16[2,128,512]{2,1,0:T(8,128)(2,1)S(1)}, bf16[2,128,512]{2,1,0:T(8,128)(2,1)S(1)}, u32[]{:S(2)}, u32[]{:S(2)}) collective-permute-start(bf16[2,128,512]{2,1,0:T(8,128)(2,1)S(1)} %collective-permute-done.12.refs_3_.refs_8_), channel_id=1, source_target_pairs={{0,224},{32,0},{64,32},{96,64},{128,96},{160,128},{192,160},{224,1... | collective-permute-start | bytes 786440 | tf_op jit(solution)/shard_map/ppermute | solution.py:22
  56.6 4.3 %collective-permute-done.13.refs_4_ = bf16[2,128,512]{2,1,0:T(8,128)(2,1)S(1)} collective-permute-done((bf16[2,128,512]{2,1,0:T(8,128)(2,1)S(1)}, bf16[2,128,512]{2,1,0:T(8,128)(2,1)S(1)}, u32[]{:S(2)}, u32[]{:S(2)}) %collective-permute-start.13) | collective-permute-done | bytes 262176 | tf_op jit(solution)/shard_map/ppermute | solution.py:22
  60.9 1.2 shard_map.31.refs_3_
  63.9 5.3 %collective-permute-done.15.refs_4_ = bf16[2,2,128,512]{3,2,1,0:T(8,128)(2,1)S(1)} collective-permute-done((bf16[2,2,128,512]{3,2,1,0:T(8,128)(2,1)S(1)}, bf16[2,2,128,512]{3,2,1,0:T(8,128)(2,1)S(1)}, u32[]{:S(2)}, u32[]{:S(2)}) %collective-permute-start.15) | collective-permute-done | bytes 524320 | tf_op jit(solution)/shard_map/ppermute | solution.py:22
  69.2 0.9 collective-permute-done.17.refs_6_
  70.4 6.7 %shard_map.33 = (f32[4,17,16,128]{3,2,1,0:T(8,128)S(1)}, f32[4,17,16,128]{3,2,1,0:T(8,128)S(1)}, f32[4,17,16,128]{3,2,1,0:T(8,128)S(1)}, f32[4,17,16,128]{3,2,1,...) custom-call(s32[68]{0:T(128)S(1)} %reshape.526.slots, ...), custom_call_target="tpu_custom_call" | custom-call | flops 2281701376 | bytes 13000000 | tf_op jit(solution)/shard_map/pallas_call | solution.py:150
  77.1 3.1 %collective-permute-start.23 = (f32[4,17,16,128]{3,2,1,0:T(8,128)S(1)}, f32[4,17,16,128]{3,2,1,0:T(8,128)S(1)}, u32[]{:S(2)}, u32[]{:S(2)}) collective-permute-start(f32[4,17,16,128]{3,2,1,0:T(8,128)S(1)} %get-tuple-element.29), channel_id=1, source_target_pairs={{0,3},{1,0},{2,1},{3,2},{4,7},{5,4},{6,5},{7,6},{8,11},{9,8},{10,9... | collective-permute-start | bytes 1671176 | tf_op jit(solution)/shard_map/ppermute | solution.py:22
  80.7 1.5 collective-permute-start.21
  82.3 1.4 collective-permute-start.22
  83.7 9.0 %collective-permute-done.23 = f32[4,17,16,128]{3,2,1,0:T(8,128)S(1)} collective-permute-done((f32[4,17,16,128]{3,2,1,0:T(8,128)S(1)}, f32[4,17,16,128]{3,2,1,0:T(8,128)S(1)}, u32[]{:S(2)}, u32[]{:S(2)}) %collective-permute-start.23) | collective-permute-done | bytes 557088 | tf_op jit(solution)/shard_map/ppermute | solution.py:22
  93.4 3.7 %collective-permute-start.26 = (f32[2,17,16,128]{3,2,1,0:T(8,128)}, f32[2,17,16,128]{3,2,1,0:T(8,128)}, u32[]{:S(2)}, u32[]{:S(2)}) collective-permute-start(f32[2,17,16,128]{3,2,1,0:T(8,128)} %slice_add_fusion.4), channel_id=1, source_target_pairs={{0,3},{1,0},{2,1},{3,2},{4,7},{5,4},{6,5},{7,6},{8,11},{9,8},{10,9... | collective-permute-start | bytes 835592 | tf_op jit(solution)/shard_map/ppermute | solution.py:22
  98.3 4.9 %collective-permute-done.26 = f32[2,17,16,128]{3,2,1,0:T(8,128)} collective-permute-done((f32[2,17,16,128]{3,2,1,0:T(8,128)}, f32[2,17,16,128]{3,2,1,0:T(8,128)}, u32[]{:S(2)}, u32[]{:S(2)}) %collective-permute-start.26) | collective-permute-done | bytes 278560 | tf_op jit(solution)/shard_map/ppermute | solution.py:22
  103.2 1.9 %fusion.30 = (f32[17,1,16,128]{3,2,0,1:T(8,128)}, f32[17,1,16,128]{3,2,0,1:T(8,128)S(1)}, f32[17,16,128]{2,1,0:T(8,128)S(1)}, f32[17,16,128]{2,1,0:T(8,128)S(1)}) fusion(f32[2,17,16,128]{3,2,1,0:T(8,128)} %collective-permute-done.26, f32[4,17,16,128]{3,2,1,0:T(8,128)} %copy-done.5, f32[4,17,16,128]{3,2,1,0:T(8,128)S(1)} %get-tuple-element.28), kind=kLoop, calls=%fused_computation.111 | loop fusion | flops 139264 | bytes 1392640 | tf_op jit(solution)/shard_map/add | solution.py:176
  105.1 2.4 %collective-permute-done.25 = f32[2,17,16,128]{3,2,1,0:T(8,128)} collective-permute-done((f32[2,17,16,128]{3,2,1,0:T(8,128)}, f32[2,17,16,128]{3,2,1,0:T(8,128)}, u32[]{:S(2)}, u32[]{:S(2)}) %collective-permute-start.25) | collective-permute-done | bytes 278560 | tf_op jit(solution)/shard_map/ppermute | solution.py:22
  107.5 1.7 %fusion.26 = (f32[17,1,16,128]{3,2,0,1:T(8,128)}, f32[17,1,16,128]{3,2,0,1:T(8,128)}, f32[17,16,128]{2,1,0:T(8,128)S(1)}, f32[17,16,128]{2,1,0:T(8,128)S(1)}) fusion(f32[2,17,16,128]{3,2,1,0:T(8,128)} %collective-permute-done.25, f32[4,17,16,128]{3,2,1,0:T(8,128)S(1)} %copy-done.4, f32[4,17,16,128]{3,2,1,0:T(8,128)S(1)} %get-tuple-element.28), kind=kLoop, calls=%fused_computation.107 | loop fusion | flops 139264 | bytes 1392640 | tf_op jit(solution)/shard_map/add | solution.py:175
  109.3 6.5 %shard_map.34 = (f32[4,17,16,128]{3,2,1,0:T(8,128)S(1)}, f32[4,17,16,128]{3,2,1,0:T(8,128)S(1)}, f32[4,17,16,128]{3,2,1,0:T(8,128)S(1)}, f32[2,17,16,128]{3,2,1,...) custom-call(s32[68]{0:T(128)S(1)} %reshape.527.slots, ...), custom_call_target="tpu_custom_call" | custom-call | flops 2281701376 | bytes 13000000 | tf_op jit(solution)/shard_map/pallas_call | solution.py:150
  115.8 1.1 collective-permute-start.27
  116.9 2.4 %collective-permute-start.28 = (f32[4,17,16,128]{3,2,1,0:T(8,128)S(1)}, f32[4,17,16,128]{3,2,1,0:T(8,128)S(1)}, u32[]{:S(2)}, u32[]{:S(2)}) collective-permute-start(f32[4,17,16,128]{3,2,1,0:T(8,128)S(1)} %get-tuple-element.36), channel_id=1, source_target_pairs={{0,16},{16,4},{4,20},{20,0},{1,17},{17,5},{5,21},{21,1},{2,18},{18... | collective-permute-start | bytes 1671176 | tf_op jit(solution)/shard_map/ppermute | solution.py:22
  119.3 1.9 %collective-permute-start.34 = (f32[4,17,16,128]{3,2,1,0:T(8,128)S(1)}, f32[4,17,16,128]{3,2,1,0:T(8,128)S(1)}, u32[]{:S(2)}, u32[]{:S(2)}) collective-permute-start(f32[4,17,16,128]{3,2,1,0:T(8,128)S(1)} %get-tuple-element.39), channel_id=1, source_target_pairs={{0,3},{1,0},{2,1},{3,2},{4,7},{5,4},{6,5},{7,6},{8,11},{9,8},{10,9... | collective-permute-start | bytes 1671176 | tf_op jit(solution)/shard_map/ppermute | solution.py:22
  121.2 1.6 fusion.17
  123.0 7.2 %collective-permute-done.27 = f32[4,17,16,128]{3,2,1,0:T(8,128)S(1)} collective-permute-done((f32[4,17,16,128]{3,2,1,0:T(8,128)S(1)}, f32[4,17,16,128]{3,2,1,0:T(8,128)S(1)}, u32[]{:S(2)}, u32[]{:S(2)}) %collective-permute-start.27) | collective-permute-done | bytes 557088 | tf_op jit(solution)/shard_map/ppermute | solution.py:22
  130.5 3.3 %collective-permute-start.29 = (f32[2,17,16,128]{3,2,1,0:T(8,128)S(1)}, f32[2,17,16,128]{3,2,1,0:T(8,128)S(1)}, u32[]{:S(2)}, u32[]{:S(2)}) collective-permute-start(f32[2,17,16,128]{3,2,1,0:T(8,128)S(1)} %slice_add_fusion.3), channel_id=1, source_target_pairs={{0,16},{16,4},{4,20},{20,0},{1,17},{17,5},{5,21},{21,1},{2,18},{18... | collective-permute-start | bytes 835592 | tf_op jit(solution)/shard_map/ppermute | solution.py:22
  133.8 2.3 %collective-permute-start.37 = (f32[2,17,16,128]{3,2,1,0:T(8,128)S(1)}, f32[2,17,16,128]{3,2,1,0:T(8,128)S(1)}, u32[]{:S(2)}, u32[]{:S(2)}) collective-permute-start(f32[2,17,16,128]{3,2,1,0:T(8,128)S(1)} %slice_add_fusion), channel_id=1, source_target_pairs={{0,3},{1,0},{2,1},{3,2},{4,7},{5,4},{6,5},{7,6},{8,11},{9,8},{10,9... | collective-permute-start | bytes 835592 | tf_op jit(solution)/shard_map/ppermute | solution.py:22
  136.7 1.4 collective-permute-done.30
  138.3 3.8 %collective-permute-start.31 = (f32[17,2,16,128]{3,2,0,1:T(8,128)S(1)}, f32[17,2,16,128]{3,2,0,1:T(8,128)S(1)}, u32[]{:S(2)}, u32[]{:S(2)}) collective-permute-start(f32[17,2,16,128]{3,2,0,1:T(8,128)S(1)} %pad_maximum_fusion), channel_id=1, source_target_pairs={{0,2},{1,3},{2,0},{3,1},{4,6},{5,7},{6,4},{7,5},{8,10},{9,11},{10,... | collective-permute-start | bytes 835592 | tf_op jit(solution)/shard_map/ppermute | solution.py:22
  142.3 3.3 %collective-permute-start.33 = (f32[17,2,16,128]{3,2,0,1:T(8,128)S(1)}, f32[17,2,16,128]{3,2,0,1:T(8,128)S(1)}, u32[]{:S(2)}, u32[]{:S(2)}) collective-permute-start(f32[17,2,16,128]{3,2,0,1:T(8,128)S(1)} %pad_maximum_fusion.2), channel_id=1, source_target_pairs={{0,3},{1,0},{2,1},{3,2},{4,7},{5,4},{6,5},{7,6},{8,11},{9,8},{10,9... | collective-permute-start | bytes 835592 | tf_op jit(solution)/shard_map/ppermute | solution.py:22
  145.6 6.4 %collective-permute-done.36 = f32[2,17,16,128]{3,2,1,0:T(8,128)S(1)} collective-permute-done((f32[2,17,16,128]{3,2,1,0:T(8,128)S(1)}, f32[2,17,16,128]{3,2,1,0:T(8,128)S(1)}, u32[]{:S(2)}, u32[]{:S(2)}) %collective-permute-start.36) | collective-permute-done | bytes 278560 | tf_op jit(solution)/shard_map/ppermute | solution.py:22
  152.2 1.0 collective-permute-start.38
  153.1 1.5 collective-permute-start.39
  155.4 0.9 collective-permute-done.32
  156.4 4.0 %collective-permute-done.38 = f32[17,2,16,128]{3,2,0,1:T(8,128)S(1)} collective-permute-done((f32[17,2,16,128]{3,2,0,1:T(8,128)S(1)}, f32[17,2,16,128]{3,2,0,1:T(8,128)S(1)}, u32[]{:S(2)}, u32[]{:S(2)}) %collective-permute-start.38) | collective-permute-done | bytes 278560 | tf_op jit(solution)/shard_map/ppermute | solution.py:22
  160.4 2.9 %collective-permute-done.40 = f32[17,2,16,128]{3,2,0,1:T(8,128)S(1)} collective-permute-done((f32[17,2,16,128]{3,2,0,1:T(8,128)S(1)}, f32[17,2,16,128]{3,2,0,1:T(8,128)S(1)}, u32[]{:S(2)}, u32[]{:S(2)}) %collective-permute-start.40) | collective-permute-done | bytes 278560 | tf_op jit(solution)/shard_map/ppermute | solution.py:22
  (98 shorter events, 11.0 us)
Async XLA Ops:
  6.5 102.8 %all-gather.2.cloned.1.call-start = ((), (), s32[]{:S(2)}) async-start(), calls=%async_computation | async-start | bytes 8912896 | tf_op jit(solution)/shard_map/all_gather | solution.py:202
  7.8 8.1 %collective-permute-start = (bf16[2,128,512]{2,1,0:T(8,128)(2,1)S(1)}, bf16[2,128,512]{2,1,0:T(8,128)(2,1)S(1)}, u32[]{:S(2)}, u32[]{:S(2)}) collective-permute-start(bf16[2,128,512]{2,1,0:T(8,128)(2,1)S(1)} %get-tuple-element.65), channel_id=1, source_target_pairs={{0,16},{16,0},{1,17},{17,1},{2,18},{18,2},{3,19},{19,3},{4,20},{20... | collective-permute-start | bytes 786440 | tf_op jit(solution)/shard_map/ppermute | solution.py:22
  8.7 13.1 %collective-permute-start.1 = (bf16[2,128,512]{2,1,0:T(8,128)(2,1)S(1)}, bf16[2,128,512]{2,1,0:T(8,128)(2,1)S(1)}, u32[]{:S(2)}, u32[]{:S(2)}) collective-permute-start(bf16[2,128,512]{2,1,0:T(8,128)(2,1)S(1)} %get-tuple-element.66.refs_0_), channel_id=1, source_target_pairs={{0,32},{32,64},{64,96},{96,128},{128,160},{160,192},{192,224},{224... | collective-permute-start | bytes 786440 | tf_op jit(solution)/shard_map/ppermute | solution.py:22
  10.6 11.2 %collective-permute-start.2 = (bf16[2,128,512]{2,1,0:T(8,128)(2,1)S(1)}, bf16[2,128,512]{2,1,0:T(8,128)(2,1)S(1)}, u32[]{:S(2)}, u32[]{:S(2)}) collective-permute-start(bf16[2,128,512]{2,1,0:T(8,128)(2,1)S(1)} %get-tuple-element.66.refs_0_), channel_id=1, source_target_pairs={{0,224},{32,0},{64,32},{96,64},{128,96},{160,128},{192,160},{224,1... | collective-permute-start | bytes 786440 | tf_op jit(solution)/shard_map/ppermute | solution.py:22
  15.9 12.6 %collective-permute-start.4 = (bf16[2,128,512]{2,1,0:T(8,128)(2,1)S(1)}, bf16[2,128,512]{2,1,0:T(8,128)(2,1)S(1)}, u32[]{:S(2)}, u32[]{:S(2)}) collective-permute-start(bf16[2,128,512]{2,1,0:T(8,128)(2,1)S(1)} %collective-permute-done.refs_1_), channel_id=1, source_target_pairs={{0,224},{32,0},{64,32},{96,64},{128,96},{160,128},{192,160},{224,1... | collective-permute-start | bytes 786440 | tf_op jit(solution)/shard_map/ppermute | solution.py:22
  21.8 10.5 %collective-permute-start.3 = (bf16[2,128,512]{2,1,0:T(8,128)(2,1)S(1)}, bf16[2,128,512]{2,1,0:T(8,128)(2,1)S(1)}, u32[]{:S(2)}, u32[]{:S(2)}) collective-permute-start(bf16[2,128,512]{2,1,0:T(8,128)(2,1)S(1)} %collective-permute-done.refs_1_), channel_id=1, source_target_pairs={{0,32},{32,64},{64,96},{96,128},{128,160},{160,192},{192,224},{224... | collective-permute-start | bytes 786440 | tf_op jit(solution)/shard_map/ppermute | solution.py:22
  21.8 16.1 %collective-permute-start.5 = (bf16[2,128,512]{2,1,0:T(8,128)(2,1)S(1)}, bf16[2,128,512]{2,1,0:T(8,128)(2,1)S(1)}, u32[]{:S(2)}, u32[]{:S(2)}) collective-permute-start(bf16[2,128,512]{2,1,0:T(8,128)(2,1)S(1)} %collective-permute-done.1.refs_0_), channel_id=1, source_target_pairs={{0,32},{32,64},{64,96},{96,128},{128,160},{160,192},{192,224},{224... | collective-permute-start | bytes 786440 | tf_op jit(solution)/shard_map/ppermute | solution.py:22
  21.8 16.1 %collective-permute-start.6 = (bf16[2,128,512]{2,1,0:T(8,128)(2,1)S(1)}, bf16[2,128,512]{2,1,0:T(8,128)(2,1)S(1)}, u32[]{:S(2)}, u32[]{:S(2)}) collective-permute-start(bf16[2,128,512]{2,1,0:T(8,128)(2,1)S(1)} %collective-permute-done.2.refs_1_), channel_id=1, source_target_pairs={{0,224},{32,0},{64,32},{96,64},{128,96},{160,128},{192,160},{224,1... | collective-permute-start | bytes 786440 | tf_op jit(solution)/shard_map/ppermute | solution.py:22
  28.5 12.6 %collective-permute-start.8 = (bf16[2,128,512]{2,1,0:T(8,128)(2,1)S(1)}, bf16[2,128,512]{2,1,0:T(8,128)(2,1)S(1)}, u32[]{:S(2)}, u32[]{:S(2)}) collective-permute-start(bf16[2,128,512]{2,1,0:T(8,128)(2,1)S(1)} %collective-permute-done.4.refs_3_), channel_id=1, source_target_pairs={{0,224},{32,0},{64,32},{96,64},{128,96},{160,128},{192,160},{224,1... | collective-permute-start | bytes 786440 | tf_op jit(solution)/shard_map/ppermute | solution.py:22
  32.2 11.2 %collective-permute-start.7 = (bf16[2,128,512]{2,1,0:T(8,128)(2,1)S(1)}, bf16[2,128,512]{2,1,0:T(8,128)(2,1)S(1)}, u32[]{:S(2)}, u32[]{:S(2)}) collective-permute-start(bf16[2,128,512]{2,1,0:T(8,128)(2,1)S(1)} %collective-permute-done.3.refs_2_), channel_id=1, source_target_pairs={{0,32},{32,64},{64,96},{96,128},{128,160},{160,192},{192,224},{224... | collective-permute-start | bytes 786440 | tf_op jit(solution)/shard_map/ppermute | solution.py:22
  32.2 14.2 %collective-permute-start.19 = (bf16[2,128,512]{2,1,0:T(8,128)(2,1)S(1)}, bf16[2,128,512]{2,1,0:T(8,128)(2,1)S(1)}, u32[]{:S(2)}, u32[]{:S(2)}) collective-permute-start(bf16[2,128,512]{2,1,0:T(8,128)(2,1)S(1)} %get-tuple-element.67), channel_id=1, source_target_pairs={{0,16},{16,0},{1,17},{17,1},{2,18},{18,2},{3,19},{19,3},{4,20},{20... | collective-permute-start | bytes 786440 | tf_op jit(solution)/shard_map/ppermute | solution.py:22
  37.9 11.2 %collective-permute-start.9 = (bf16[2,128,512]{2,1,0:T(8,128)(2,1)S(1)}, bf16[2,128,512]{2,1,0:T(8,128)(2,1)S(1)}, u32[]{:S(2)}, u32[]{:S(2)}) collective-permute-start(bf16[2,128,512]{2,1,0:T(8,128)(2,1)S(1)} %collective-permute-done.5.refs_0_), channel_id=1, source_target_pairs={{0,32},{32,64},{64,96},{96,128},{128,160},{160,192},{192,224},{224... | collective-permute-start | bytes 786440 | tf_op jit(solution)/shard_map/ppermute | solution.py:22
  37.9 11.2 %collective-permute-start.10 = (bf16[2,128,512]{2,1,0:T(8,128)(2,1)S(1)}, bf16[2,128,512]{2,1,0:T(8,128)(2,1)S(1)}, u32[]{:S(2)}, u32[]{:S(2)}) collective-permute-start(bf16[2,128,512]{2,1,0:T(8,128)(2,1)S(1)} %collective-permute-done.6.refs_1_), channel_id=1, source_target_pairs={{0,224},{32,0},{64,32},{96,64},{128,96},{160,128},{192,160},{224,1... | collective-permute-start | bytes 786440 | tf_op jit(solution)/shard_map/ppermute | solution.py:22
  41.1 8.0 %collective-permute-start.12 = (bf16[2,128,512]{2,1,0:T(8,128)(2,1)S(1)}, bf16[2,128,512]{2,1,0:T(8,128)(2,1)S(1)}, u32[]{:S(2)}, u32[]{:S(2)}) collective-permute-start(bf16[2,128,512]{2,1,0:T(8,128)(2,1)S(1)} %collective-permute-done.8.refs_3_), channel_id=1, source_target_pairs={{0,224},{32,0},{64,32},{96,64},{128,96},{160,128},{192,160},{224,1... | collective-permute-start | bytes 786440 | tf_op jit(solution)/shard_map/ppermute | solution.py:22
  43.5 8.9 %collective-permute-start.11 = (bf16[2,128,512]{2,1,0:T(8,128)(2,1)S(1)}, bf16[2,128,512]{2,1,0:T(8,128)(2,1)S(1)}, u32[]{:S(2)}, u32[]{:S(2)}) collective-permute-start(bf16[2,128,512]{2,1,0:T(8,128)(2,1)S(1)} %collective-permute-done.7.refs_2_), channel_id=1, source_target_pairs={{0,32},{32,64},{64,96},{96,128},{128,160},{160,192},{192,224},{224... | collective-permute-start | bytes 786440 | tf_op jit(solution)/shard_map/ppermute | solution.py:22
  53.2 9.8 %copy-start.1 = (bf16[2,2,128,512]{3,2,1,0:T(8,128)(2,1)S(1)}, bf16[2,2,128,512]{3,2,1,0:T(8,128)(2,1)}, u32[]{:S(2)}) copy-start(bf16[2,2,128,512]{3,2,1,0:T(8,128)(2,1)} %shard_map.28.refs_2_.refs_0_) | copy-start | bytes 1572868
  53.2 10.2 %copy-start.10 = (s32[32,17,2]{0,2,1:T(2,128)S(1)}, s32[32,17,2]{0,2,1:T(2,128)}, u32[]{:S(2)}) copy-start(s32[32,17,2]{0,2,1:T(2,128)} %param.3) | copy-start | bytes 13060
  53.2 7.7 %collective-permute-start.13 = (bf16[2,128,512]{2,1,0:T(8,128)(2,1)S(1)}, bf16[2,128,512]{2,1,0:T(8,128)(2,1)S(1)}, u32[]{:S(2)}, u32[]{:S(2)}) collective-permute-start(bf16[2,128,512]{2,1,0:T(8,128)(2,1)S(1)} %collective-permute-done.9.refs_0_.refs_5_), channel_id=1, source_target_pairs={{0,32},{32,64},{64,96},{96,128},{128,160},{160,192},{192,224},{224... | collective-permute-start | bytes 786440 | tf_op jit(solution)/shard_map/ppermute | solution.py:22
  53.3 7.6 %collective-permute-start.14 = (bf16[2,128,512]{2,1,0:T(8,128)(2,1)S(1)}, bf16[2,128,512]{2,1,0:T(8,128)(2,1)S(1)}, u32[]{:S(2)}, u32[]{:S(2)}) collective-permute-start(bf16[2,128,512]{2,1,0:T(8,128)(2,1)S(1)} %collective-permute-done.12.refs_3_.refs_8_), channel_id=1, source_target_pairs={{0,224},{32,0},{64,32},{96,64},{128,96},{160,128},{192,160},{224,1... | collective-permute-start | bytes 786440 | tf_op jit(solution)/shard_map/ppermute | solution.py:22
  62.1 8.2 %collective-permute-start.18 = (bf16[6,2,128,512]{3,2,1,0:T(8,128)(2,1)}, bf16[6,2,128,512]{3,2,1,0:T(8,128)(2,1)}, u32[]{:S(2)}, u32[]{:S(2)}) collective-permute-start(bf16[6,2,128,512]{3,2,1,0:T(8,128)(2,1)} %shard_map.31.refs_3_), channel_id=1, source_target_pairs={{0,8},{8,0},{1,9},{9,1},{2,10},{10,2},{3,11},{11,3},{4,12},{12,4},... | collective-permute-start | bytes 4718600 | tf_op jit(solution)/shard_map/ppermute | solution.py:22
  62.4 6.8 %collective-permute-start.16 = (bf16[4,2,128,512]{3,2,1,0:T(8,128)(2,1)S(1)}, bf16[4,2,128,512]{3,2,1,0:T(8,128)(2,1)S(1)}, u32[]{:S(2)}, u32[]{:S(2)}) collective-permute-start(bf16[4,2,128,512]{3,2,1,0:T(8,128)(2,1)S(1)} %copy-done), channel_id=1, source_target_pairs={{0,8},{8,0},{1,9},{9,1},{2,10},{10,2},{3,11},{11,3},{4,12},{12,4},... | collective-permute-start | bytes 3145736 | tf_op jit(solution)/shard_map/ppermute | solution.py:22
  62.9 7.2 %collective-permute-start.17 = (bf16[4,2,128,512]{3,2,1,0:T(8,128)(2,1)}, bf16[4,2,128,512]{3,2,1,0:T(8,128)(2,1)}, u32[]{:S(2)}, u32[]{:S(2)}) collective-permute-start(bf16[4,2,128,512]{3,2,1,0:T(8,128)(2,1)} %shard_map.30.refs_4_.refs_2_), channel_id=1, source_target_pairs={{0,8},{8,0},{1,9},{9,1},{2,10},{10,2},{3,11},{11,3},{4,12},{12,4},... | collective-permute-start | bytes 3145736 | tf_op jit(solution)/shard_map/ppermute | solution.py:22
  63.0 6.2 %collective-permute-start.15 = (bf16[2,2,128,512]{3,2,1,0:T(8,128)(2,1)S(1)}, bf16[2,2,128,512]{3,2,1,0:T(8,128)(2,1)S(1)}, u32[]{:S(2)}, u32[]{:S(2)}) collective-permute-start(bf16[2,2,128,512]{3,2,1,0:T(8,128)(2,1)S(1)} %copy-done.1), channel_id=1, source_target_pairs={{0,8},{8,0},{1,9},{9,1},{2,10},{10,2},{3,11},{11,3},{4,12},{12,4},... | collective-permute-start | bytes 1572872 | tf_op jit(solution)/shard_map/ppermute | solution.py:22
  77.1 15.5 %collective-permute-start.23 = (f32[4,17,16,128]{3,2,1,0:T(8,128)S(1)}, f32[4,17,16,128]{3,2,1,0:T(8,128)S(1)}, u32[]{:S(2)}, u32[]{:S(2)}) collective-permute-start(f32[4,17,16,128]{3,2,1,0:T(8,128)S(1)} %get-tuple-element.29), channel_id=1, source_target_pairs={{0,3},{1,0},{2,1},{3,2},{4,7},{5,4},{6,5},{7,6},{8,11},{9,8},{10,9... | collective-permute-start | bytes 1671176 | tf_op jit(solution)/shard_map/ppermute | solution.py:22
  80.2 16.9 %collective-permute-start.24 = (f32[4,17,16,128]{3,2,1,0:T(8,128)S(1)}, f32[4,17,16,128]{3,2,1,0:T(8,128)S(1)}, u32[]{:S(2)}, u32[]{:S(2)}) collective-permute-start(f32[4,17,16,128]{3,2,1,0:T(8,128)S(1)} %get-tuple-element.31), channel_id=1, source_target_pairs={{0,1},{1,2},{2,3},{3,0},{4,5},{5,6},{6,7},{7,4},{8,9},{9,10},{10,1... | collective-permute-start | bytes 1671176 | tf_op jit(solution)/shard_map/ppermute | solution.py:22
  80.2 29.0 %collective-permute-start.20 = (f32[4,17,16,128]{3,2,1,0:T(8,128)S(1)}, f32[4,17,16,128]{3,2,1,0:T(8,128)}, u32[]{:S(2)}, u32[]{:S(2)}) collective-permute-start(f32[4,17,16,128]{3,2,1,0:T(8,128)S(1)} %get-tuple-element.25), channel_id=1, source_target_pairs={{0,16},{16,4},{4,20},{20,0},{1,17},{17,5},{5,21},{21,1},{2,18},{18... | collective-permute-start | bytes 1671176 | tf_op jit(solution)/shard_map/ppermute | solution.py:22
  80.7 28.6 %collective-permute-start.21 = (f32[4,17,16,128]{3,2,1,0:T(8,128)S(1)}, f32[4,17,16,128]{3,2,1,0:T(8,128)}, u32[]{:S(2)}, u32[]{:S(2)}) collective-permute-start(f32[4,17,16,128]{3,2,1,0:T(8,128)S(1)} %get-tuple-element.26), channel_id=1, source_target_pairs={{0,20},{16,0},{4,16},{20,4},{1,21},{17,1},{5,17},{21,5},{2,22},{18... | collective-permute-start | bytes 1671176 | tf_op jit(solution)/shard_map/ppermute | solution.py:22
  82.3 27.0 %collective-permute-start.22 = (f32[4,17,16,128]{3,2,1,0:T(8,128)S(1)}, f32[4,17,16,128]{3,2,1,0:T(8,128)}, u32[]{:S(2)}, u32[]{:S(2)}) collective-permute-start(f32[4,17,16,128]{3,2,1,0:T(8,128)S(1)} %get-tuple-element.27), channel_id=1, source_target_pairs={{0,4},{16,20},{4,0},{20,16},{1,5},{17,21},{5,1},{21,17},{2,6},{18,... | collective-permute-start | bytes 1671176 | tf_op jit(solution)/shard_map/ppermute | solution.py:22
  92.6 10.6 %copy-start.3 = (f32[4,17,16,128]{3,2,1,0:T(8,128)}, f32[4,17,16,128]{3,2,1,0:T(8,128)S(1)}, u32[]{:S(2)}) copy-start(f32[4,17,16,128]{3,2,1,0:T(8,128)S(1)} %collective-permute-done.23) | copy-start | bytes 1671172
  93.4 9.8 %collective-permute-start.26 = (f32[2,17,16,128]{3,2,1,0:T(8,128)}, f32[2,17,16,128]{3,2,1,0:T(8,128)}, u32[]{:S(2)}, u32[]{:S(2)}) collective-permute-start(f32[2,17,16,128]{3,2,1,0:T(8,128)} %slice_add_fusion.4), channel_id=1, source_target_pairs={{0,3},{1,0},{2,1},{3,2},{4,7},{5,4},{6,5},{7,6},{8,11},{9,8},{10,9... | collective-permute-start | bytes 835592 | tf_op jit(solution)/shard_map/ppermute | solution.py:22
  98.1 9.5 %collective-permute-start.25 = (f32[2,17,16,128]{3,2,1,0:T(8,128)}, f32[2,17,16,128]{3,2,1,0:T(8,128)}, u32[]{:S(2)}, u32[]{:S(2)}) collective-permute-start(f32[2,17,16,128]{3,2,1,0:T(8,128)} %slice_add_fusion.5), channel_id=1, source_target_pairs={{0,1},{1,2},{2,3},{3,0},{4,5},{5,6},{6,7},{7,4},{8,9},{9,10},{10,1... | collective-permute-start | bytes 835592 | tf_op jit(solution)/shard_map/ppermute | solution.py:22
  115.8 14.5 %collective-permute-start.27 = (f32[4,17,16,128]{3,2,1,0:T(8,128)S(1)}, f32[4,17,16,128]{3,2,1,0:T(8,128)S(1)}, u32[]{:S(2)}, u32[]{:S(2)}) collective-permute-start(f32[4,17,16,128]{3,2,1,0:T(8,128)S(1)} %get-tuple-element.34), channel_id=1, source_target_pairs={{0,20},{16,0},{4,16},{20,4},{1,21},{17,1},{5,17},{21,5},{2,22},{18... | collective-permute-start | bytes 1671176 | tf_op jit(solution)/shard_map/ppermute | solution.py:22
  116.9 13.5 %collective-permute-start.28 = (f32[4,17,16,128]{3,2,1,0:T(8,128)S(1)}, f32[4,17,16,128]{3,2,1,0:T(8,128)S(1)}, u32[]{:S(2)}, u32[]{:S(2)}) collective-permute-start(f32[4,17,16,128]{3,2,1,0:T(8,128)S(1)} %get-tuple-element.36), channel_id=1, source_target_pairs={{0,16},{16,4},{4,20},{20,0},{1,17},{17,5},{5,21},{21,1},{2,18},{18... | collective-permute-start | bytes 1671176 | tf_op jit(solution)/shard_map/ppermute | solution.py:22
  119.3 14.4 %collective-permute-start.34 = (f32[4,17,16,128]{3,2,1,0:T(8,128)S(1)}, f32[4,17,16,128]{3,2,1,0:T(8,128)S(1)}, u32[]{:S(2)}, u32[]{:S(2)}) collective-permute-start(f32[4,17,16,128]{3,2,1,0:T(8,128)S(1)} %get-tuple-element.39), channel_id=1, source_target_pairs={{0,3},{1,0},{2,1},{3,2},{4,7},{5,4},{6,5},{7,6},{8,11},{9,8},{10,9... | collective-permute-start | bytes 1671176 | tf_op jit(solution)/shard_map/ppermute | solution.py:22
  122.9 13.7 %collective-permute-start.35 = (f32[4,17,16,128]{3,2,1,0:T(8,128)S(1)}, f32[4,17,16,128]{3,2,1,0:T(8,128)S(1)}, u32[]{:S(2)}, u32[]{:S(2)}) collective-permute-start(f32[4,17,16,128]{3,2,1,0:T(8,128)S(1)} %get-tuple-element.41), channel_id=1, source_target_pairs={{0,1},{1,2},{2,3},{3,0},{4,5},{5,6},{6,7},{7,4},{8,9},{9,10},{10,1... | collective-permute-start | bytes 1671176 | tf_op jit(solution)/shard_map/ppermute | solution.py:22
  130.3 7.8 %collective-permute-start.30 = (f32[2,17,16,128]{3,2,1,0:T(8,128)S(1)}, f32[2,17,16,128]{3,2,1,0:T(8,128)S(1)}, u32[]{:S(2)}, u32[]{:S(2)}) collective-permute-start(f32[2,17,16,128]{3,2,1,0:T(8,128)S(1)} %slice_add_fusion.2), channel_id=1, source_target_pairs={{0,20},{16,0},{4,16},{20,4},{1,21},{17,1},{5,17},{21,5},{2,22},{18... | collective-permute-start | bytes 835592 | tf_op jit(solution)/shard_map/ppermute | solution.py:22
  130.5 7.7 %collective-permute-start.29 = (f32[2,17,16,128]{3,2,1,0:T(8,128)S(1)}, f32[2,17,16,128]{3,2,1,0:T(8,128)S(1)}, u32[]{:S(2)}, u32[]{:S(2)}) collective-permute-start(f32[2,17,16,128]{3,2,1,0:T(8,128)S(1)} %slice_add_fusion.3), channel_id=1, source_target_pairs={{0,16},{16,4},{4,20},{20,0},{1,17},{17,5},{5,21},{21,1},{2,18},{18... | collective-permute-start | bytes 835592 | tf_op jit(solution)/shard_map/ppermute | solution.py:22
  133.8 11.8 %collective-permute-start.37 = (f32[2,17,16,128]{3,2,1,0:T(8,128)S(1)}, f32[2,17,16,128]{3,2,1,0:T(8,128)S(1)}, u32[]{:S(2)}, u32[]{:S(2)}) collective-permute-start(f32[2,17,16,128]{3,2,1,0:T(8,128)S(1)} %slice_add_fusion), channel_id=1, source_target_pairs={{0,3},{1,0},{2,1},{3,2},{4,7},{5,4},{6,5},{7,6},{8,11},{9,8},{10,9... | collective-permute-start | bytes 835592 | tf_op jit(solution)/shard_map/ppermute | solution.py:22
  136.7 15.3 %collective-permute-start.36 = (f32[2,17,16,128]{3,2,1,0:T(8,128)S(1)}, f32[2,17,16,128]{3,2,1,0:T(8,128)S(1)}, u32[]{:S(2)}, u32[]{:S(2)}) collective-permute-start(f32[2,17,16,128]{3,2,1,0:T(8,128)S(1)} %slice_add_fusion.1), channel_id=1, source_target_pairs={{0,1},{1,2},{2,3},{3,0},{4,5},{5,6},{6,7},{7,4},{8,9},{9,10},{10,1... | collective-permute-start | bytes 835592 | tf_op jit(solution)/shard_map/ppermute | solution.py:22
  138.3 16.4 %collective-permute-start.31 = (f32[17,2,16,128]{3,2,0,1:T(8,128)S(1)}, f32[17,2,16,128]{3,2,0,1:T(8,128)S(1)}, u32[]{:S(2)}, u32[]{:S(2)}) collective-permute-start(f32[17,2,16,128]{3,2,0,1:T(8,128)S(1)} %pad_maximum_fusion), channel_id=1, source_target_pairs={{0,2},{1,3},{2,0},{3,1},{4,6},{5,7},{6,4},{7,5},{8,10},{9,11},{10,... | collective-permute-start | bytes 835592 | tf_op jit(solution)/shard_map/ppermute | solution.py:22
  142.1 10.0 %copy-start.6 = (f32[17,1,16,128]{3,2,0,1:T(8,128)S(1)}, f32[17,1,16,128]{3,2,0,1:T(8,128)}, u32[]{:S(2)}) copy-start(f32[17,1,16,128]{3,2,0,1:T(8,128)} %get-tuple-element.59) | copy-start | bytes 417796
  142.1 14.2 %collective-permute-start.32 = (f32[17,2,16,128]{3,2,0,1:T(8,128)S(1)}, f32[17,2,16,128]{3,2,0,1:T(8,128)S(1)}, u32[]{:S(2)}, u32[]{:S(2)}) collective-permute-start(f32[17,2,16,128]{3,2,0,1:T(8,128)S(1)} %pad_maximum_fusion.1), channel_id=1, source_target_pairs={{0,1},{1,2},{2,3},{3,0},{4,5},{5,6},{6,7},{7,4},{8,9},{9,10},{10,1... | collective-permute-start | bytes 835592 | tf_op jit(solution)/shard_map/ppermute | solution.py:22
  142.2 10.9 %copy-start.7 = (f32[17,1,16,128]{3,2,0,1:T(8,128)S(1)}, f32[17,1,16,128]{3,2,0,1:T(8,128)}, u32[]{:S(2)}) copy-start(f32[17,1,16,128]{3,2,0,1:T(8,128)} %get-tuple-element.54) | copy-start | bytes 417796
  142.3 14.0 %collective-permute-start.33 = (f32[17,2,16,128]{3,2,0,1:T(8,128)S(1)}, f32[17,2,16,128]{3,2,0,1:T(8,128)S(1)}, u32[]{:S(2)}, u32[]{:S(2)}) collective-permute-start(f32[17,2,16,128]{3,2,0,1:T(8,128)S(1)} %pad_maximum_fusion.2), channel_id=1, source_target_pairs={{0,3},{1,0},{2,1},{3,2},{4,7},{5,4},{6,5},{7,6},{8,11},{9,8},{10,9... | collective-permute-start | bytes 835592 | tf_op jit(solution)/shard_map/ppermute | solution.py:22
  152.1 11.2 %copy-start.8 = (f32[17,1,16,128]{3,2,0,1:T(8,128)S(1)}, f32[17,1,16,128]{3,2,0,1:T(8,128)}, u32[]{:S(2)}) copy-start(f32[17,1,16,128]{3,2,0,1:T(8,128)} %get-tuple-element.53) | copy-start | bytes 417796
  152.2 8.2 %collective-permute-start.38 = (f32[17,2,16,128]{3,2,0,1:T(8,128)S(1)}, f32[17,2,16,128]{3,2,0,1:T(8,128)S(1)}, u32[]{:S(2)}, u32[]{:S(2)}) collective-permute-start(f32[17,2,16,128]{3,2,0,1:T(8,128)S(1)} %pad_maximum_fusion.3), channel_id=1, source_target_pairs={{0,4},{16,20},{4,0},{20,16},{1,5},{17,21},{5,1},{21,17},{2,6},{18,... | collective-permute-start | bytes 835592 | tf_op jit(solution)/shard_map/ppermute | solution.py:22
  153.1 7.2 %collective-permute-start.39 = (f32[17,2,16,128]{3,2,0,1:T(8,128)S(1)}, f32[17,2,16,128]{3,2,0,1:T(8,128)S(1)}, u32[]{:S(2)}, u32[]{:S(2)}) collective-permute-start(f32[17,2,16,128]{3,2,0,1:T(8,128)S(1)} %pad_maximum_fusion.4), channel_id=1, source_target_pairs={{0,16},{16,4},{4,20},{20,0},{1,17},{17,5},{5,21},{21,1},{2,18},{18... | collective-permute-start | bytes 835592 | tf_op jit(solution)/shard_map/ppermute | solution.py:22
  154.7 8.6 %collective-permute-start.40 = (f32[17,2,16,128]{3,2,0,1:T(8,128)S(1)}, f32[17,2,16,128]{3,2,0,1:T(8,128)S(1)}, u32[]{:S(2)}, u32[]{:S(2)}) collective-permute-start(f32[17,2,16,128]{3,2,0,1:T(8,128)S(1)} %pad_maximum_fusion.5), channel_id=1, source_target_pairs={{0,20},{16,0},{4,16},{20,4},{1,21},{17,1},{5,17},{21,5},{2,22},{18... | collective-permute-start | bytes 835592 | tf_op jit(solution)/shard_map/ppermute | solution.py:22
  (5 other events, 16.5 us)
Sparse Core Ops, SparseCore 0:
  53.3 53.6 all-gather.1

commit v4 on v3

--- a/solution.py
+++ b/solution.py
@@ -205,7 +205,7 @@
     re_first, re_come = reduce_direct(re_parts, X_AXIS)
     im_first, _ = reduce_ring(im_parts, "y")
 
-    re_parts, im_parts = tile_partials(slots_abs, pos, [whole], False, after=[*in_hbm(re_come), *im_first])
+    re_parts, im_parts = tile_partials(slots_abs, pos, [whole], False, after=[*in_hbm(re_come), *im_first[2:]])
     re_second, _ = reduce_ring(re_parts, X_AXIS)
     im_second, _ = reduce_ring(im_parts, "y")
     re_sum = reduce_near((re_first, re_second), "y")

time: 171 us -> 171 us (level)
    add x1 -> x0, other arithmetic: 1.88 us -> none  [reduce_ring(): sums += [home[d] + up[d] + last_down[d - 2] for d in range(2, NX)]]
  transfers between devices with their start and end apart: 42 -> 42, of which waited for: 19 -> 19; matrix products, arithmetic and copies ran while one was open for 5% -> 4% of each run, Pallas kernels for 6% -> 6%
where the time goes in v4:
time: 171 us
  waiting for transfers between devices  67.9 us (40%)
  starting transfers between devices  61.9 us (36%)
  Pallas kernels  18.2 us (11%)
  between operations  13.7 us (8%)
  other arithmetic  6.15 us (4%)
  local copies, waits for them, and re-layouts  3.09 us (2%)
    ppermute x41, waiting for transfers between devices, shift(): lax.ppermute(x, axis, [(rank(i, axis), rank((i + step) % size, axis)) for...  67.9 us
    ppermute x41, starting transfers between devices, shift(): lax.ppermute(x, axis, [(rank(i, axis), rank((i + step) % size, axis)) for...  61.9 us
    pallas_call x2, Pallas kernels, tile_partials(): pl.pallas_call(kernel, out_shape=parts, in_specs=[smem, smem] + [pl.Block...  13.2 us
    pallas_call x5, Pallas kernels, packed(): pl.pallas_call(kernel, out_shape=pltpu.HBM((n,) + arrays[0].shape, arrays...  4.94 us
  transfers between devices with their start and end apart: 42, of which 19 were waited for; matrix products, arithmetic and copies ran while one was open for 4% of the time, Pallas kernels for 6%

profile of v4, /device:TPU:6, one launch (start us, length us, event | category | flops | bytes accessed | tf_op | source)
XLA Modules:
  0.0 170.9 jit_solution(12511988342037207367)
XLA Ops:
  6.5 1.3 dynamic-slice_bitcast_fusion.2
  7.8 0.9 collective-permute-start
  8.7 1.9 %collective-permute-start.1 = (bf16[2,128,512]{2,1,0:T(8,128)(2,1)S(1)}, bf16[2,128,512]{2,1,0:T(8,128)(2,1)S(1)}, u32[]{:S(2)}, u32[]{:S(2)}) collective-permute-start(bf16[2,128,512]{2,1,0:T(8,128)(2,1)S(1)} %get-tuple-element.64.refs_0_), channel_id=1, source_target_pairs={{0,32},{32,64},{64,96},{96,128},{128,160},{160,192},{192,224},{224... | collective-permute-start | bytes 786440 | tf_op jit(solution)/shard_map/ppermute | solution.py:22
  10.6 3.9 %collective-permute-start.2 = (bf16[2,128,512]{2,1,0:T(8,128)(2,1)S(1)}, bf16[2,128,512]{2,1,0:T(8,128)(2,1)S(1)}, u32[]{:S(2)}, u32[]{:S(2)}) collective-permute-start(bf16[2,128,512]{2,1,0:T(8,128)(2,1)S(1)} %get-tuple-element.64.refs_0_), channel_id=1, source_target_pairs={{0,224},{32,0},{64,32},{96,64},{128,96},{160,128},{192,160},{224,1... | collective-permute-start | bytes 786440 | tf_op jit(solution)/shard_map/ppermute | solution.py:22
  14.6 1.4 collective-permute-done.refs_1_
  15.9 5.9 %collective-permute-start.4 = (bf16[2,128,512]{2,1,0:T(8,128)(2,1)S(1)}, bf16[2,128,512]{2,1,0:T(8,128)(2,1)S(1)}, u32[]{:S(2)}, u32[]{:S(2)}) collective-permute-start(bf16[2,128,512]{2,1,0:T(8,128)(2,1)S(1)} %collective-permute-done.refs_1_), channel_id=1, source_target_pairs={{0,224},{32,0},{64,32},{96,64},{128,96},{160,128},{192,160},{224,1... | collective-permute-start | bytes 786440 | tf_op jit(solution)/shard_map/ppermute | solution.py:22
  21.8 3.3 %collective-permute-start.6 = (bf16[2,128,512]{2,1,0:T(8,128)(2,1)S(1)}, bf16[2,128,512]{2,1,0:T(8,128)(2,1)S(1)}, u32[]{:S(2)}, u32[]{:S(2)}) collective-permute-start(bf16[2,128,512]{2,1,0:T(8,128)(2,1)S(1)} %collective-permute-done.2.refs_1_), channel_id=1, source_target_pairs={{0,224},{32,0},{64,32},{96,64},{128,96},{160,128},{192,160},{224,1... | collective-permute-start | bytes 786440 | tf_op jit(solution)/shard_map/ppermute | solution.py:22
  25.1 3.4 %collective-permute-done.4.refs_3_ = bf16[2,128,512]{2,1,0:T(8,128)(2,1)S(1)} collective-permute-done((bf16[2,128,512]{2,1,0:T(8,128)(2,1)S(1)}, bf16[2,128,512]{2,1,0:T(8,128)(2,1)S(1)}, u32[]{:S(2)}, u32[]{:S(2)}) %collective-permute-start.4) | collective-permute-done | bytes 262176 | tf_op jit(solution)/shard_map/ppermute | solution.py:22
  28.5 3.7 %collective-permute-start.8 = (bf16[2,128,512]{2,1,0:T(8,128)(2,1)S(1)}, bf16[2,128,512]{2,1,0:T(8,128)(2,1)S(1)}, u32[]{:S(2)}, u32[]{:S(2)}) collective-permute-start(bf16[2,128,512]{2,1,0:T(8,128)(2,1)S(1)} %collective-permute-done.4.refs_3_), channel_id=1, source_target_pairs={{0,224},{32,0},{64,32},{96,64},{128,96},{160,128},{192,160},{224,1... | collective-permute-start | bytes 786440 | tf_op jit(solution)/shard_map/ppermute | solution.py:22
  32.2 0.8 collective-permute-start.19
  33.1 4.8 %collective-permute-done.5.refs_0_ = bf16[2,128,512]{2,1,0:T(8,128)(2,1)S(1)} collective-permute-done((bf16[2,128,512]{2,1,0:T(8,128)(2,1)S(1)}, bf16[2,128,512]{2,1,0:T(8,128)(2,1)S(1)}, u32[]{:S(2)}, u32[]{:S(2)}) %collective-permute-start.5) | collective-permute-done | bytes 262176 | tf_op jit(solution)/shard_map/ppermute | solution.py:22
  37.9 3.2 %collective-permute-start.10 = (bf16[2,128,512]{2,1,0:T(8,128)(2,1)S(1)}, bf16[2,128,512]{2,1,0:T(8,128)(2,1)S(1)}, u32[]{:S(2)}, u32[]{:S(2)}) collective-permute-start(bf16[2,128,512]{2,1,0:T(8,128)(2,1)S(1)} %collective-permute-done.6.refs_1_), channel_id=1, source_target_pairs={{0,224},{32,0},{64,32},{96,64},{128,96},{160,128},{192,160},{224,1... | collective-permute-start | bytes 786440 | tf_op jit(solution)/shard_map/ppermute | solution.py:22
  41.1 1.6 collective-permute-start.12
  44.3 1.1 shard_map.29.refs_3_.refs_1_
  45.4 1.0 shard_map.30.refs_4_.refs_2_
  46.4 2.7 %collective-permute-done.9.refs_0_.refs_5_ = bf16[2,128,512]{2,1,0:T(8,128)(2,1)S(1)} collective-permute-done((bf16[2,128,512]{2,1,0:T(8,128)(2,1)S(1)}, bf16[2,128,512]{2,1,0:T(8,128)(2,1)S(1)}, u32[]{:S(2)}, u32[]{:S(2)}) %collective-permute-start.9) | collective-permute-done | bytes 262176 | tf_op jit(solution)/shard_map/ppermute | solution.py:22
  49.1 3.3 %collective-permute-done.11.refs_2_.refs_7_ = bf16[2,128,512]{2,1,0:T(8,128)(2,1)S(1)} collective-permute-done((bf16[2,128,512]{2,1,0:T(8,128)(2,1)S(1)}, bf16[2,128,512]{2,1,0:T(8,128)(2,1)S(1)}, u32[]{:S(2)}, u32[]{:S(2)}) %collective-permute-start.11) | collective-permute-done | bytes 262176 | tf_op jit(solution)/shard_map/ppermute | solution.py:22
  53.3 3.2 %collective-permute-start.14 = (bf16[2,128,512]{2,1,0:T(8,128)(2,1)S(1)}, bf16[2,128,512]{2,1,0:T(8,128)(2,1)S(1)}, u32[]{:S(2)}, u32[]{:S(2)}) collective-permute-start(bf16[2,128,512]{2,1,0:T(8,128)(2,1)S(1)} %collective-permute-done.12.refs_3_.refs_8_), channel_id=1, source_target_pairs={{0,224},{32,0},{64,32},{96,64},{128,96},{160,128},{192,160},{224,1... | collective-permute-start | bytes 786440 | tf_op jit(solution)/shard_map/ppermute | solution.py:22
  56.6 4.3 %collective-permute-done.13.refs_4_ = bf16[2,128,512]{2,1,0:T(8,128)(2,1)S(1)} collective-permute-done((bf16[2,128,512]{2,1,0:T(8,128)(2,1)S(1)}, bf16[2,128,512]{2,1,0:T(8,128)(2,1)S(1)}, u32[]{:S(2)}, u32[]{:S(2)}) %collective-permute-start.13) | collective-permute-done | bytes 262176 | tf_op jit(solution)/shard_map/ppermute | solution.py:22
  60.9 1.2 shard_map.31.refs_3_
  63.9 5.3 %collective-permute-done.15.refs_4_ = bf16[2,2,128,512]{3,2,1,0:T(8,128)(2,1)} collective-permute-done((bf16[2,2,128,512]{3,2,1,0:T(8,128)(2,1)}, bf16[2,2,128,512]{3,2,1,0:T(8,128)(2,1)}, u32[]{:S(2)}, u32[]{:S(2)}) %collective-permute-start.15) | collective-permute-done | bytes 524320 | tf_op jit(solution)/shard_map/ppermute | solution.py:22
  70.2 6.8 %shard_map.33 = (f32[4,17,16,128]{3,2,1,0:T(8,128)S(1)}, f32[4,17,16,128]{3,2,1,0:T(8,128)S(1)}, f32[4,17,16,128]{3,2,1,0:T(8,128)S(1)}, f32[4,17,16,128]{3,2,1,...) custom-call(s32[68]{0:T(128)S(1)} %reshape.522.slots, ...), custom_call_target="tpu_custom_call" | custom-call | flops 2281701376 | bytes 13000000 | tf_op jit(solution)/shard_map/pallas_call | solution.py:150
  77.0 3.2 %collective-permute-start.24 = (f32[4,17,16,128]{3,2,1,0:T(8,128)S(1)}, f32[4,17,16,128]{3,2,1,0:T(8,128)S(1)}, u32[]{:S(2)}, u32[]{:S(2)}) collective-permute-start(f32[4,17,16,128]{3,2,1,0:T(8,128)S(1)} %get-tuple-element.31), channel_id=1, source_target_pairs={{0,3},{1,0},{2,1},{3,2},{4,7},{5,4},{6,5},{7,6},{8,11},{9,8},{10,9... | collective-permute-start | bytes 1671176 | tf_op jit(solution)/shard_map/ppermute | solution.py:22
  80.5 1.7 %collective-permute-start.21 = (f32[4,17,16,128]{3,2,1,0:T(8,128)S(1)}, f32[4,17,16,128]{3,2,1,0:T(8,128)}, u32[]{:S(2)}, u32[]{:S(2)}) collective-permute-start(f32[4,17,16,128]{3,2,1,0:T(8,128)S(1)} %get-tuple-element.26), channel_id=1, source_target_pairs={{0,20},{16,0},{4,16},{20,4},{1,21},{17,1},{5,17},{21,5},{2,22},{18... | collective-permute-start | bytes 1671176 | tf_op jit(solution)/shard_map/ppermute | solution.py:22
  82.2 1.2 collective-permute-start.22
  83.4 9.0 %collective-permute-done.24 = f32[4,17,16,128]{3,2,1,0:T(8,128)S(1)} collective-permute-done((f32[4,17,16,128]{3,2,1,0:T(8,128)S(1)}, f32[4,17,16,128]{3,2,1,0:T(8,128)S(1)}, u32[]{:S(2)}, u32[]{:S(2)}) %collective-permute-start.24) | collective-permute-done | bytes 557088 | tf_op jit(solution)/shard_map/ppermute | solution.py:22
  93.3 3.7 %collective-permute-start.25 = (f32[2,17,16,128]{3,2,1,0:T(8,128)}, f32[2,17,16,128]{3,2,1,0:T(8,128)S(1)}, u32[]{:S(2)}, u32[]{:S(2)}) collective-permute-start(f32[2,17,16,128]{3,2,1,0:T(8,128)} %slice_add_fusion.5), channel_id=1, source_target_pairs={{0,3},{1,0},{2,1},{3,2},{4,7},{5,4},{6,5},{7,6},{8,11},{9,8},{10,9... | collective-permute-start | bytes 835592 | tf_op jit(solution)/shard_map/ppermute | solution.py:22
  97.0 0.8 slice_add_fusion.2
  98.2 4.7 %collective-permute-done.25 = f32[2,17,16,128]{3,2,1,0:T(8,128)S(1)} collective-permute-done((f32[2,17,16,128]{3,2,1,0:T(8,128)}, f32[2,17,16,128]{3,2,1,0:T(8,128)S(1)}, u32[]{:S(2)}, u32[]{:S(2)}) %collective-permute-start.25) | collective-permute-done | bytes 278560 | tf_op jit(solution)/shard_map/ppermute | solution.py:22
  102.9 4.1 %collective-permute-done.33 = f32[2,17,16,128]{3,2,1,0:T(8,128)S(1)} collective-permute-done((f32[2,17,16,128]{3,2,1,0:T(8,128)}, f32[2,17,16,128]{3,2,1,0:T(8,128)S(1)}, u32[]{:S(2)}, u32[]{:S(2)}) %collective-permute-start.33) | collective-permute-done | bytes 278560 | tf_op jit(solution)/shard_map/ppermute | solution.py:22
  107.1 2.1 %fusion.11 = (f32[17,1,16,128]{3,2,0,1:T(8,128)}, f32[17,1,16,128]{3,2,0,1:T(8,128)}, f32[17,16,128]{2,1,0:T(8,128)S(1)}, f32[17,16,128]{2,1,0:T(8,128)S(1)}, f3...) fusion(f32[2,17,16,128]{3,2,1,0:T(8,128)S(1)} %collective-permute-done.33, f32[4,17,16,128]{3,2,1,0:T(8,128)} %copy-done.3, ...), kind=kLoop, calls=%fused_computation.41 | loop fusion | flops 278528 | bytes 2506752 | tf_op jit(solution)/shard_map/add | solution.py:175
  109.2 6.5 %shard_map.34 = (f32[4,17,16,128]{3,2,1,0:T(8,128)S(1)}, f32[4,17,16,128]{3,2,1,0:T(8,128)S(1)}, f32[4,17,16,128]{3,2,1,0:T(8,128)S(1)}, f32[2,17,16,128]{3,2,1,...) custom-call(s32[68]{0:T(128)S(1)} %reshape.523.slots, ...), custom_call_target="tpu_custom_call" | custom-call | flops 2281701376 | bytes 13000000 | tf_op jit(solution)/shard_map/pallas_call | solution.py:150
  115.7 1.1 collective-permute-start.26
  116.8 2.4 %collective-permute-start.27 = (f32[4,17,16,128]{3,2,1,0:T(8,128)S(1)}, f32[4,17,16,128]{3,2,1,0:T(8,128)S(1)}, u32[]{:S(2)}, u32[]{:S(2)}) collective-permute-start(f32[4,17,16,128]{3,2,1,0:T(8,128)S(1)} %get-tuple-element.35), channel_id=1, source_target_pairs={{0,16},{16,4},{4,20},{20,0},{1,17},{17,5},{5,21},{21,1},{2,18},{18... | collective-permute-start | bytes 1671176 | tf_op jit(solution)/shard_map/ppermute | solution.py:22
  119.2 1.9 %collective-permute-start.34 = (f32[4,17,16,128]{3,2,1,0:T(8,128)S(1)}, f32[4,17,16,128]{3,2,1,0:T(8,128)S(1)}, u32[]{:S(2)}, u32[]{:S(2)}) collective-permute-start(f32[4,17,16,128]{3,2,1,0:T(8,128)S(1)} %get-tuple-element.39), channel_id=1, source_target_pairs={{0,3},{1,0},{2,1},{3,2},{4,7},{5,4},{6,5},{7,6},{8,11},{9,8},{10,9... | collective-permute-start | bytes 1671176 | tf_op jit(solution)/shard_map/ppermute | solution.py:22
  121.1 1.6 fusion.19
  122.9 7.2 %collective-permute-done.26 = f32[4,17,16,128]{3,2,1,0:T(8,128)S(1)} collective-permute-done((f32[4,17,16,128]{3,2,1,0:T(8,128)S(1)}, f32[4,17,16,128]{3,2,1,0:T(8,128)S(1)}, u32[]{:S(2)}, u32[]{:S(2)}) %collective-permute-start.26) | collective-permute-done | bytes 557088 | tf_op jit(solution)/shard_map/ppermute | solution.py:22
  130.3 3.3 %collective-permute-start.28 = (f32[2,17,16,128]{3,2,1,0:T(8,128)S(1)}, f32[2,17,16,128]{3,2,1,0:T(8,128)S(1)}, u32[]{:S(2)}, u32[]{:S(2)}) collective-permute-start(f32[2,17,16,128]{3,2,1,0:T(8,128)S(1)} %slice_add_fusion.4), channel_id=1, source_target_pairs={{0,16},{16,4},{4,20},{20,0},{1,17},{17,5},{5,21},{21,1},{2,18},{18... | collective-permute-start | bytes 835592 | tf_op jit(solution)/shard_map/ppermute | solution.py:22
  133.7 2.4 %collective-permute-start.37 = (f32[2,17,16,128]{3,2,1,0:T(8,128)S(1)}, f32[2,17,16,128]{3,2,1,0:T(8,128)S(1)}, u32[]{:S(2)}, u32[]{:S(2)}) collective-permute-start(f32[2,17,16,128]{3,2,1,0:T(8,128)S(1)} %slice_add_fusion), channel_id=1, source_target_pairs={{0,3},{1,0},{2,1},{3,2},{4,7},{5,4},{6,5},{7,6},{8,11},{9,8},{10,9... | collective-permute-start | bytes 835592 | tf_op jit(solution)/shard_map/ppermute | solution.py:22
  136.8 1.3 collective-permute-done.29
  138.2 4.1 %collective-permute-start.30 = (f32[17,2,16,128]{3,2,0,1:T(8,128)S(1)}, f32[17,2,16,128]{3,2,0,1:T(8,128)S(1)}, u32[]{:S(2)}, u32[]{:S(2)}) collective-permute-start(f32[17,2,16,128]{3,2,0,1:T(8,128)S(1)} %pad_maximum_fusion), channel_id=1, source_target_pairs={{0,2},{1,3},{2,0},{3,1},{4,6},{5,7},{6,4},{7,5},{8,10},{9,11},{10,... | collective-permute-start | bytes 835592 | tf_op jit(solution)/shard_map/ppermute | solution.py:22
  142.5 3.3 %collective-permute-start.32 = (f32[17,2,16,128]{3,2,0,1:T(8,128)S(1)}, f32[17,2,16,128]{3,2,0,1:T(8,128)S(1)}, u32[]{:S(2)}, u32[]{:S(2)}) collective-permute-start(f32[17,2,16,128]{3,2,0,1:T(8,128)S(1)} %pad_maximum_fusion.2), channel_id=1, source_target_pairs={{0,3},{1,0},{2,1},{3,2},{4,7},{5,4},{6,5},{7,6},{8,11},{9,8},{10,9... | collective-permute-start | bytes 835592 | tf_op jit(solution)/shard_map/ppermute | solution.py:22
  145.8 6.1 %collective-permute-done.36 = f32[2,17,16,128]{3,2,1,0:T(8,128)S(1)} collective-permute-done((f32[2,17,16,128]{3,2,1,0:T(8,128)S(1)}, f32[2,17,16,128]{3,2,1,0:T(8,128)S(1)}, u32[]{:S(2)}, u32[]{:S(2)}) %collective-permute-start.36) | collective-permute-done | bytes 278560 | tf_op jit(solution)/shard_map/ppermute | solution.py:22
  152.3 2.4 %collective-permute-start.39 = (f32[17,2,16,128]{3,2,0,1:T(8,128)S(1)}, f32[17,2,16,128]{3,2,0,1:T(8,128)S(1)}, u32[]{:S(2)}, u32[]{:S(2)}) collective-permute-start(f32[17,2,16,128]{3,2,0,1:T(8,128)S(1)} %pad_maximum_fusion.4), channel_id=1, source_target_pairs={{0,16},{16,4},{4,20},{20,0},{1,17},{17,5},{5,21},{21,1},{2,18},{18... | collective-permute-start | bytes 835592 | tf_op jit(solution)/shard_map/ppermute | solution.py:22
  154.8 1.6 collective-permute-done.31
  156.5 3.7 %collective-permute-done.38 = f32[17,2,16,128]{3,2,0,1:T(8,128)S(1)} collective-permute-done((f32[17,2,16,128]{3,2,0,1:T(8,128)S(1)}, f32[17,2,16,128]{3,2,0,1:T(8,128)S(1)}, u32[]{:S(2)}, u32[]{:S(2)}) %collective-permute-start.38) | collective-permute-done | bytes 278560 | tf_op jit(solution)/shard_map/ppermute | solution.py:22
  160.2 2.9 %collective-permute-done.40 = f32[17,2,16,128]{3,2,0,1:T(8,128)S(1)} collective-permute-done((f32[17,2,16,128]{3,2,0,1:T(8,128)S(1)}, f32[17,2,16,128]{3,2,0,1:T(8,128)S(1)}, u32[]{:S(2)}, u32[]{:S(2)}) %collective-permute-start.40) | collective-permute-done | bytes 278560 | tf_op jit(solution)/shard_map/ppermute | solution.py:22
  163.2 0.9 copy.16
  (97 shorter events, 8.8 us)
Async XLA Ops:
  6.5 102.6 %all-gather.2.cloned.1.call-start = ((), (), s32[]{:S(2)}) async-start(), calls=%async_computation | async-start | bytes 8912896 | tf_op jit(solution)/shard_map/all_gather | solution.py:202
  7.8 8.1 %collective-permute-start = (bf16[2,128,512]{2,1,0:T(8,128)(2,1)S(1)}, bf16[2,128,512]{2,1,0:T(8,128)(2,1)S(1)}, u32[]{:S(2)}, u32[]{:S(2)}) collective-permute-start(bf16[2,128,512]{2,1,0:T(8,128)(2,1)S(1)} %get-tuple-element.63), channel_id=1, source_target_pairs={{0,16},{16,0},{1,17},{17,1},{2,18},{18,2},{3,19},{19,3},{4,20},{20... | collective-permute-start | bytes 786440 | tf_op jit(solution)/shard_map/ppermute | solution.py:22
  8.7 13.1 %collective-permute-start.1 = (bf16[2,128,512]{2,1,0:T(8,128)(2,1)S(1)}, bf16[2,128,512]{2,1,0:T(8,128)(2,1)S(1)}, u32[]{:S(2)}, u32[]{:S(2)}) collective-permute-start(bf16[2,128,512]{2,1,0:T(8,128)(2,1)S(1)} %get-tuple-element.64.refs_0_), channel_id=1, source_target_pairs={{0,32},{32,64},{64,96},{96,128},{128,160},{160,192},{192,224},{224... | collective-permute-start | bytes 786440 | tf_op jit(solution)/shard_map/ppermute | solution.py:22
  10.6 11.2 %collective-permute-start.2 = (bf16[2,128,512]{2,1,0:T(8,128)(2,1)S(1)}, bf16[2,128,512]{2,1,0:T(8,128)(2,1)S(1)}, u32[]{:S(2)}, u32[]{:S(2)}) collective-permute-start(bf16[2,128,512]{2,1,0:T(8,128)(2,1)S(1)} %get-tuple-element.64.refs_0_), channel_id=1, source_target_pairs={{0,224},{32,0},{64,32},{96,64},{128,96},{160,128},{192,160},{224,1... | collective-permute-start | bytes 786440 | tf_op jit(solution)/shard_map/ppermute | solution.py:22
  15.9 12.6 %collective-permute-start.4 = (bf16[2,128,512]{2,1,0:T(8,128)(2,1)S(1)}, bf16[2,128,512]{2,1,0:T(8,128)(2,1)S(1)}, u32[]{:S(2)}, u32[]{:S(2)}) collective-permute-start(bf16[2,128,512]{2,1,0:T(8,128)(2,1)S(1)} %collective-permute-done.refs_1_), channel_id=1, source_target_pairs={{0,224},{32,0},{64,32},{96,64},{128,96},{160,128},{192,160},{224,1... | collective-permute-start | bytes 786440 | tf_op jit(solution)/shard_map/ppermute | solution.py:22
  21.8 10.5 %collective-permute-start.3 = (bf16[2,128,512]{2,1,0:T(8,128)(2,1)S(1)}, bf16[2,128,512]{2,1,0:T(8,128)(2,1)S(1)}, u32[]{:S(2)}, u32[]{:S(2)}) collective-permute-start(bf16[2,128,512]{2,1,0:T(8,128)(2,1)S(1)} %collective-permute-done.refs_1_), channel_id=1, source_target_pairs={{0,32},{32,64},{64,96},{96,128},{128,160},{160,192},{192,224},{224... | collective-permute-start | bytes 786440 | tf_op jit(solution)/shard_map/ppermute | solution.py:22
  21.8 16.1 %collective-permute-start.5 = (bf16[2,128,512]{2,1,0:T(8,128)(2,1)S(1)}, bf16[2,128,512]{2,1,0:T(8,128)(2,1)S(1)}, u32[]{:S(2)}, u32[]{:S(2)}) collective-permute-start(bf16[2,128,512]{2,1,0:T(8,128)(2,1)S(1)} %collective-permute-done.1.refs_0_), channel_id=1, source_target_pairs={{0,32},{32,64},{64,96},{96,128},{128,160},{160,192},{192,224},{224... | collective-permute-start | bytes 786440 | tf_op jit(solution)/shard_map/ppermute | solution.py:22
  21.8 16.1 %collective-permute-start.6 = (bf16[2,128,512]{2,1,0:T(8,128)(2,1)S(1)}, bf16[2,128,512]{2,1,0:T(8,128)(2,1)S(1)}, u32[]{:S(2)}, u32[]{:S(2)}) collective-permute-start(bf16[2,128,512]{2,1,0:T(8,128)(2,1)S(1)} %collective-permute-done.2.refs_1_), channel_id=1, source_target_pairs={{0,224},{32,0},{64,32},{96,64},{128,96},{160,128},{192,160},{224,1... | collective-permute-start | bytes 786440 | tf_op jit(solution)/shard_map/ppermute | solution.py:22
  28.5 12.6 %collective-permute-start.8 = (bf16[2,128,512]{2,1,0:T(8,128)(2,1)S(1)}, bf16[2,128,512]{2,1,0:T(8,128)(2,1)S(1)}, u32[]{:S(2)}, u32[]{:S(2)}) collective-permute-start(bf16[2,128,512]{2,1,0:T(8,128)(2,1)S(1)} %collective-permute-done.4.refs_3_), channel_id=1, source_target_pairs={{0,224},{32,0},{64,32},{96,64},{128,96},{160,128},{192,160},{224,1... | collective-permute-start | bytes 786440 | tf_op jit(solution)/shard_map/ppermute | solution.py:22
  32.2 11.2 %collective-permute-start.7 = (bf16[2,128,512]{2,1,0:T(8,128)(2,1)S(1)}, bf16[2,128,512]{2,1,0:T(8,128)(2,1)S(1)}, u32[]{:S(2)}, u32[]{:S(2)}) collective-permute-start(bf16[2,128,512]{2,1,0:T(8,128)(2,1)S(1)} %collective-permute-done.3.refs_2_), channel_id=1, source_target_pairs={{0,32},{32,64},{64,96},{96,128},{128,160},{160,192},{192,224},{224... | collective-permute-start | bytes 786440 | tf_op jit(solution)/shard_map/ppermute | solution.py:22
  32.2 14.2 %collective-permute-start.19 = (bf16[2,128,512]{2,1,0:T(8,128)(2,1)S(1)}, bf16[2,128,512]{2,1,0:T(8,128)(2,1)S(1)}, u32[]{:S(2)}, u32[]{:S(2)}) collective-permute-start(bf16[2,128,512]{2,1,0:T(8,128)(2,1)S(1)} %get-tuple-element.65), channel_id=1, source_target_pairs={{0,16},{16,0},{1,17},{17,1},{2,18},{18,2},{3,19},{19,3},{4,20},{20... | collective-permute-start | bytes 786440 | tf_op jit(solution)/shard_map/ppermute | solution.py:22
  37.9 11.2 %collective-permute-start.9 = (bf16[2,128,512]{2,1,0:T(8,128)(2,1)S(1)}, bf16[2,128,512]{2,1,0:T(8,128)(2,1)S(1)}, u32[]{:S(2)}, u32[]{:S(2)}) collective-permute-start(bf16[2,128,512]{2,1,0:T(8,128)(2,1)S(1)} %collective-permute-done.5.refs_0_), channel_id=1, source_target_pairs={{0,32},{32,64},{64,96},{96,128},{128,160},{160,192},{192,224},{224... | collective-permute-start | bytes 786440 | tf_op jit(solution)/shard_map/ppermute | solution.py:22
  37.9 11.2 %collective-permute-start.10 = (bf16[2,128,512]{2,1,0:T(8,128)(2,1)S(1)}, bf16[2,128,512]{2,1,0:T(8,128)(2,1)S(1)}, u32[]{:S(2)}, u32[]{:S(2)}) collective-permute-start(bf16[2,128,512]{2,1,0:T(8,128)(2,1)S(1)} %collective-permute-done.6.refs_1_), channel_id=1, source_target_pairs={{0,224},{32,0},{64,32},{96,64},{128,96},{160,128},{192,160},{224,1... | collective-permute-start | bytes 786440 | tf_op jit(solution)/shard_map/ppermute | solution.py:22
  41.1 8.0 %collective-permute-start.12 = (bf16[2,128,512]{2,1,0:T(8,128)(2,1)S(1)}, bf16[2,128,512]{2,1,0:T(8,128)(2,1)S(1)}, u32[]{:S(2)}, u32[]{:S(2)}) collective-permute-start(bf16[2,128,512]{2,1,0:T(8,128)(2,1)S(1)} %collective-permute-done.8.refs_3_), channel_id=1, source_target_pairs={{0,224},{32,0},{64,32},{96,64},{128,96},{160,128},{192,160},{224,1... | collective-permute-start | bytes 786440 | tf_op jit(solution)/shard_map/ppermute | solution.py:22
  43.5 8.9 %collective-permute-start.11 = (bf16[2,128,512]{2,1,0:T(8,128)(2,1)S(1)}, bf16[2,128,512]{2,1,0:T(8,128)(2,1)S(1)}, u32[]{:S(2)}, u32[]{:S(2)}) collective-permute-start(bf16[2,128,512]{2,1,0:T(8,128)(2,1)S(1)} %collective-permute-done.7.refs_2_), channel_id=1, source_target_pairs={{0,32},{32,64},{64,96},{96,128},{128,160},{160,192},{192,224},{224... | collective-permute-start | bytes 786440 | tf_op jit(solution)/shard_map/ppermute | solution.py:22
  53.2 9.2 %copy-start = (bf16[4,2,128,512]{3,2,1,0:T(8,128)(2,1)S(1)}, bf16[4,2,128,512]{3,2,1,0:T(8,128)(2,1)}, u32[]{:S(2)}) copy-start(bf16[4,2,128,512]{3,2,1,0:T(8,128)(2,1)} %shard_map.29.refs_3_.refs_1_) | copy-start | bytes 3145732
  53.2 9.7 %copy-start.1 = (bf16[4,2,128,512]{3,2,1,0:T(8,128)(2,1)S(1)}, bf16[4,2,128,512]{3,2,1,0:T(8,128)(2,1)}, u32[]{:S(2)}) copy-start(bf16[4,2,128,512]{3,2,1,0:T(8,128)(2,1)} %shard_map.30.refs_4_.refs_2_) | copy-start | bytes 3145732
  53.2 10.2 %copy-start.10 = (s32[32,17,2]{0,2,1:T(2,128)S(1)}, s32[32,17,2]{0,2,1:T(2,128)}, u32[]{:S(2)}) copy-start(s32[32,17,2]{0,2,1:T(2,128)} %param.3) | copy-start | bytes 13060
  53.2 7.7 %collective-permute-start.13 = (bf16[2,128,512]{2,1,0:T(8,128)(2,1)S(1)}, bf16[2,128,512]{2,1,0:T(8,128)(2,1)S(1)}, u32[]{:S(2)}, u32[]{:S(2)}) collective-permute-start(bf16[2,128,512]{2,1,0:T(8,128)(2,1)S(1)} %collective-permute-done.9.refs_0_.refs_5_), channel_id=1, source_target_pairs={{0,32},{32,64},{64,96},{96,128},{128,160},{160,192},{192,224},{224... | collective-permute-start | bytes 786440 | tf_op jit(solution)/shard_map/ppermute | solution.py:22
  53.3 7.6 %collective-permute-start.14 = (bf16[2,128,512]{2,1,0:T(8,128)(2,1)S(1)}, bf16[2,128,512]{2,1,0:T(8,128)(2,1)S(1)}, u32[]{:S(2)}, u32[]{:S(2)}) collective-permute-start(bf16[2,128,512]{2,1,0:T(8,128)(2,1)S(1)} %collective-permute-done.12.refs_3_.refs_8_), channel_id=1, source_target_pairs={{0,224},{32,0},{64,32},{96,64},{128,96},{160,128},{192,160},{224,1... | collective-permute-start | bytes 786440 | tf_op jit(solution)/shard_map/ppermute | solution.py:22
  62.1 8.1 %collective-permute-start.18 = (bf16[6,2,128,512]{3,2,1,0:T(8,128)(2,1)}, bf16[6,2,128,512]{3,2,1,0:T(8,128)(2,1)}, u32[]{:S(2)}, u32[]{:S(2)}) collective-permute-start(bf16[6,2,128,512]{3,2,1,0:T(8,128)(2,1)} %shard_map.31.refs_3_), channel_id=1, source_target_pairs={{0,8},{8,0},{1,9},{9,1},{2,10},{10,2},{3,11},{11,3},{4,12},{12,4},... | collective-permute-start | bytes 4718600 | tf_op jit(solution)/shard_map/ppermute | solution.py:22
  62.4 6.8 %collective-permute-start.16 = (bf16[4,2,128,512]{3,2,1,0:T(8,128)(2,1)S(1)}, bf16[4,2,128,512]{3,2,1,0:T(8,128)(2,1)S(1)}, u32[]{:S(2)}, u32[]{:S(2)}) collective-permute-start(bf16[4,2,128,512]{3,2,1,0:T(8,128)(2,1)S(1)} %copy-done), channel_id=1, source_target_pairs={{0,8},{8,0},{1,9},{9,1},{2,10},{10,2},{3,11},{11,3},{4,12},{12,4},... | collective-permute-start | bytes 3145736 | tf_op jit(solution)/shard_map/ppermute | solution.py:22
  62.9 7.0 %collective-permute-start.17 = (bf16[4,2,128,512]{3,2,1,0:T(8,128)(2,1)S(1)}, bf16[4,2,128,512]{3,2,1,0:T(8,128)(2,1)}, u32[]{:S(2)}, u32[]{:S(2)}) collective-permute-start(bf16[4,2,128,512]{3,2,1,0:T(8,128)(2,1)S(1)} %copy-done.1), channel_id=1, source_target_pairs={{0,8},{8,0},{1,9},{9,1},{2,10},{10,2},{3,11},{11,3},{4,12},{12,4},... | collective-permute-start | bytes 3145736 | tf_op jit(solution)/shard_map/ppermute | solution.py:22
  63.0 6.1 %collective-permute-start.15 = (bf16[2,2,128,512]{3,2,1,0:T(8,128)(2,1)}, bf16[2,2,128,512]{3,2,1,0:T(8,128)(2,1)}, u32[]{:S(2)}, u32[]{:S(2)}) collective-permute-start(bf16[2,2,128,512]{3,2,1,0:T(8,128)(2,1)} %shard_map.28.refs_2_.refs_0_), channel_id=1, source_target_pairs={{0,8},{8,0},{1,9},{9,1},{2,10},{10,2},{3,11},{11,3},{4,12},{12,4},... | collective-permute-start | bytes 1572872 | tf_op jit(solution)/shard_map/ppermute | solution.py:22
  77.0 15.5 %collective-permute-start.24 = (f32[4,17,16,128]{3,2,1,0:T(8,128)S(1)}, f32[4,17,16,128]{3,2,1,0:T(8,128)S(1)}, u32[]{:S(2)}, u32[]{:S(2)}) collective-permute-start(f32[4,17,16,128]{3,2,1,0:T(8,128)S(1)} %get-tuple-element.31), channel_id=1, source_target_pairs={{0,3},{1,0},{2,1},{3,2},{4,7},{5,4},{6,5},{7,6},{8,11},{9,8},{10,9... | collective-permute-start | bytes 1671176 | tf_op jit(solution)/shard_map/ppermute | solution.py:22
  80.2 16.8 %collective-permute-start.23 = (f32[4,17,16,128]{3,2,1,0:T(8,128)S(1)}, f32[4,17,16,128]{3,2,1,0:T(8,128)S(1)}, u32[]{:S(2)}, u32[]{:S(2)}) collective-permute-start(f32[4,17,16,128]{3,2,1,0:T(8,128)S(1)} %get-tuple-element.29), channel_id=1, source_target_pairs={{0,1},{1,2},{2,3},{3,0},{4,5},{5,6},{6,7},{7,4},{8,9},{9,10},{10,1... | collective-permute-start | bytes 1671176 | tf_op jit(solution)/shard_map/ppermute | solution.py:22
  80.2 28.9 %collective-permute-start.20 = (f32[4,17,16,128]{3,2,1,0:T(8,128)S(1)}, f32[4,17,16,128]{3,2,1,0:T(8,128)}, u32[]{:S(2)}, u32[]{:S(2)}) collective-permute-start(f32[4,17,16,128]{3,2,1,0:T(8,128)S(1)} %get-tuple-element.25), channel_id=1, source_target_pairs={{0,16},{16,4},{4,20},{20,0},{1,17},{17,5},{5,21},{21,1},{2,18},{18... | collective-permute-start | bytes 1671176 | tf_op jit(solution)/shard_map/ppermute | solution.py:22
  80.5 28.6 %collective-permute-start.21 = (f32[4,17,16,128]{3,2,1,0:T(8,128)S(1)}, f32[4,17,16,128]{3,2,1,0:T(8,128)}, u32[]{:S(2)}, u32[]{:S(2)}) collective-permute-start(f32[4,17,16,128]{3,2,1,0:T(8,128)S(1)} %get-tuple-element.26), channel_id=1, source_target_pairs={{0,20},{16,0},{4,16},{20,4},{1,21},{17,1},{5,17},{21,5},{2,22},{18... | collective-permute-start | bytes 1671176 | tf_op jit(solution)/shard_map/ppermute | solution.py:22
  82.2 26.9 %collective-permute-start.22 = (f32[4,17,16,128]{3,2,1,0:T(8,128)S(1)}, f32[4,17,16,128]{3,2,1,0:T(8,128)}, u32[]{:S(2)}, u32[]{:S(2)}) collective-permute-start(f32[4,17,16,128]{3,2,1,0:T(8,128)S(1)} %get-tuple-element.27), channel_id=1, source_target_pairs={{0,4},{16,20},{4,0},{20,16},{1,5},{17,21},{5,1},{21,17},{2,6},{18,... | collective-permute-start | bytes 1671176 | tf_op jit(solution)/shard_map/ppermute | solution.py:22
  93.3 9.6 %collective-permute-start.25 = (f32[2,17,16,128]{3,2,1,0:T(8,128)}, f32[2,17,16,128]{3,2,1,0:T(8,128)S(1)}, u32[]{:S(2)}, u32[]{:S(2)}) collective-permute-start(f32[2,17,16,128]{3,2,1,0:T(8,128)} %slice_add_fusion.5), channel_id=1, source_target_pairs={{0,3},{1,0},{2,1},{3,2},{4,7},{5,4},{6,5},{7,6},{8,11},{9,8},{10,9... | collective-permute-start | bytes 835592 | tf_op jit(solution)/shard_map/ppermute | solution.py:22
  97.8 9.2 %collective-permute-start.33 = (f32[2,17,16,128]{3,2,1,0:T(8,128)}, f32[2,17,16,128]{3,2,1,0:T(8,128)S(1)}, u32[]{:S(2)}, u32[]{:S(2)}) collective-permute-start(f32[2,17,16,128]{3,2,1,0:T(8,128)} %slice_add_fusion.2), channel_id=1, source_target_pairs={{0,1},{1,2},{2,3},{3,0},{4,5},{5,6},{6,7},{7,4},{8,9},{9,10},{10,1... | collective-permute-start | bytes 835592 | tf_op jit(solution)/shard_map/ppermute | solution.py:22
  115.7 14.5 %collective-permute-start.26 = (f32[4,17,16,128]{3,2,1,0:T(8,128)S(1)}, f32[4,17,16,128]{3,2,1,0:T(8,128)S(1)}, u32[]{:S(2)}, u32[]{:S(2)}) collective-permute-start(f32[4,17,16,128]{3,2,1,0:T(8,128)S(1)} %get-tuple-element.33), channel_id=1, source_target_pairs={{0,20},{16,0},{4,16},{20,4},{1,21},{17,1},{5,17},{21,5},{2,22},{18... | collective-permute-start | bytes 1671176 | tf_op jit(solution)/shard_map/ppermute | solution.py:22
  116.8 13.5 %collective-permute-start.27 = (f32[4,17,16,128]{3,2,1,0:T(8,128)S(1)}, f32[4,17,16,128]{3,2,1,0:T(8,128)S(1)}, u32[]{:S(2)}, u32[]{:S(2)}) collective-permute-start(f32[4,17,16,128]{3,2,1,0:T(8,128)S(1)} %get-tuple-element.35), channel_id=1, source_target_pairs={{0,16},{16,4},{4,20},{20,0},{1,17},{17,5},{5,21},{21,1},{2,18},{18... | collective-permute-start | bytes 1671176 | tf_op jit(solution)/shard_map/ppermute | solution.py:22
  119.2 14.4 %collective-permute-start.34 = (f32[4,17,16,128]{3,2,1,0:T(8,128)S(1)}, f32[4,17,16,128]{3,2,1,0:T(8,128)S(1)}, u32[]{:S(2)}, u32[]{:S(2)}) collective-permute-start(f32[4,17,16,128]{3,2,1,0:T(8,128)S(1)} %get-tuple-element.39), channel_id=1, source_target_pairs={{0,3},{1,0},{2,1},{3,2},{4,7},{5,4},{6,5},{7,6},{8,11},{9,8},{10,9... | collective-permute-start | bytes 1671176 | tf_op jit(solution)/shard_map/ppermute | solution.py:22
  122.7 13.9 %collective-permute-start.35 = (f32[4,17,16,128]{3,2,1,0:T(8,128)S(1)}, f32[4,17,16,128]{3,2,1,0:T(8,128)S(1)}, u32[]{:S(2)}, u32[]{:S(2)}) collective-permute-start(f32[4,17,16,128]{3,2,1,0:T(8,128)S(1)} %get-tuple-element.41), channel_id=1, source_target_pairs={{0,1},{1,2},{2,3},{3,0},{4,5},{5,6},{6,7},{7,4},{8,9},{9,10},{10,1... | collective-permute-start | bytes 1671176 | tf_op jit(solution)/shard_map/ppermute | solution.py:22
  130.2 7.8 %collective-permute-start.29 = (f32[2,17,16,128]{3,2,1,0:T(8,128)S(1)}, f32[2,17,16,128]{3,2,1,0:T(8,128)S(1)}, u32[]{:S(2)}, u32[]{:S(2)}) collective-permute-start(f32[2,17,16,128]{3,2,1,0:T(8,128)S(1)} %slice_add_fusion.3), channel_id=1, source_target_pairs={{0,20},{16,0},{4,16},{20,4},{1,21},{17,1},{5,17},{21,5},{2,22},{18... | collective-permute-start | bytes 835592 | tf_op jit(solution)/shard_map/ppermute | solution.py:22
  130.3 7.7 %collective-permute-start.28 = (f32[2,17,16,128]{3,2,1,0:T(8,128)S(1)}, f32[2,17,16,128]{3,2,1,0:T(8,128)S(1)}, u32[]{:S(2)}, u32[]{:S(2)}) collective-permute-start(f32[2,17,16,128]{3,2,1,0:T(8,128)S(1)} %slice_add_fusion.4), channel_id=1, source_target_pairs={{0,16},{16,4},{4,20},{20,0},{1,17},{17,5},{5,21},{21,1},{2,18},{18... | collective-permute-start | bytes 835592 | tf_op jit(solution)/shard_map/ppermute | solution.py:22
  133.7 12.1 %collective-permute-start.37 = (f32[2,17,16,128]{3,2,1,0:T(8,128)S(1)}, f32[2,17,16,128]{3,2,1,0:T(8,128)S(1)}, u32[]{:S(2)}, u32[]{:S(2)}) collective-permute-start(f32[2,17,16,128]{3,2,1,0:T(8,128)S(1)} %slice_add_fusion), channel_id=1, source_target_pairs={{0,3},{1,0},{2,1},{3,2},{4,7},{5,4},{6,5},{7,6},{8,11},{9,8},{10,9... | collective-permute-start | bytes 835592 | tf_op jit(solution)/shard_map/ppermute | solution.py:22
  136.7 15.2 %collective-permute-start.36 = (f32[2,17,16,128]{3,2,1,0:T(8,128)S(1)}, f32[2,17,16,128]{3,2,1,0:T(8,128)S(1)}, u32[]{:S(2)}, u32[]{:S(2)}) collective-permute-start(f32[2,17,16,128]{3,2,1,0:T(8,128)S(1)} %slice_add_fusion.1), channel_id=1, source_target_pairs={{0,1},{1,2},{2,3},{3,0},{4,5},{5,6},{6,7},{7,4},{8,9},{9,10},{10,1... | collective-permute-start | bytes 835592 | tf_op jit(solution)/shard_map/ppermute | solution.py:22
  138.2 16.5 %collective-permute-start.30 = (f32[17,2,16,128]{3,2,0,1:T(8,128)S(1)}, f32[17,2,16,128]{3,2,0,1:T(8,128)S(1)}, u32[]{:S(2)}, u32[]{:S(2)}) collective-permute-start(f32[17,2,16,128]{3,2,0,1:T(8,128)S(1)} %pad_maximum_fusion), channel_id=1, source_target_pairs={{0,2},{1,3},{2,0},{3,1},{4,6},{5,7},{6,4},{7,5},{8,10},{9,11},{10,... | collective-permute-start | bytes 835592 | tf_op jit(solution)/shard_map/ppermute | solution.py:22
  142.3 9.6 %copy-start.7 = (f32[17,1,16,128]{3,2,0,1:T(8,128)S(1)}, f32[17,1,16,128]{3,2,0,1:T(8,128)}, u32[]{:S(2)}) copy-start(f32[17,1,16,128]{3,2,0,1:T(8,128)} %get-tuple-element.72) | copy-start | bytes 417796
  142.3 14.1 %collective-permute-start.31 = (f32[17,2,16,128]{3,2,0,1:T(8,128)S(1)}, f32[17,2,16,128]{3,2,0,1:T(8,128)S(1)}, u32[]{:S(2)}, u32[]{:S(2)}) collective-permute-start(f32[17,2,16,128]{3,2,0,1:T(8,128)S(1)} %pad_maximum_fusion.1), channel_id=1, source_target_pairs={{0,1},{1,2},{2,3},{3,0},{4,5},{5,6},{6,7},{7,4},{8,9},{9,10},{10,1... | collective-permute-start | bytes 835592 | tf_op jit(solution)/shard_map/ppermute | solution.py:22
  142.4 9.8 %copy-start.6 = (f32[17,1,16,128]{3,2,0,1:T(8,128)S(1)}, f32[17,1,16,128]{3,2,0,1:T(8,128)}, u32[]{:S(2)}) copy-start(f32[17,1,16,128]{3,2,0,1:T(8,128)} %get-tuple-element.54) | copy-start | bytes 417796
  142.5 14.0 %collective-permute-start.32 = (f32[17,2,16,128]{3,2,0,1:T(8,128)S(1)}, f32[17,2,16,128]{3,2,0,1:T(8,128)S(1)}, u32[]{:S(2)}, u32[]{:S(2)}) collective-permute-start(f32[17,2,16,128]{3,2,0,1:T(8,128)S(1)} %pad_maximum_fusion.2), channel_id=1, source_target_pairs={{0,3},{1,0},{2,1},{3,2},{4,7},{5,4},{6,5},{7,6},{8,11},{9,8},{10,9... | collective-permute-start | bytes 835592 | tf_op jit(solution)/shard_map/ppermute | solution.py:22
  151.9 11.2 %copy-start.8 = (f32[17,1,16,128]{3,2,0,1:T(8,128)S(1)}, f32[17,1,16,128]{3,2,0,1:T(8,128)}, u32[]{:S(2)}) copy-start(f32[17,1,16,128]{3,2,0,1:T(8,128)} %get-tuple-element.53) | copy-start | bytes 417796
  152.0 8.2 %collective-permute-start.38 = (f32[17,2,16,128]{3,2,0,1:T(8,128)S(1)}, f32[17,2,16,128]{3,2,0,1:T(8,128)S(1)}, u32[]{:S(2)}, u32[]{:S(2)}) collective-permute-start(f32[17,2,16,128]{3,2,0,1:T(8,128)S(1)} %pad_maximum_fusion.3), channel_id=1, source_target_pairs={{0,4},{16,20},{4,0},{20,16},{1,5},{17,21},{5,1},{21,17},{2,6},{18,... | collective-permute-start | bytes 835592 | tf_op jit(solution)/shard_map/ppermute | solution.py:22
  152.3 7.9 %collective-permute-start.39 = (f32[17,2,16,128]{3,2,0,1:T(8,128)S(1)}, f32[17,2,16,128]{3,2,0,1:T(8,128)S(1)}, u32[]{:S(2)}, u32[]{:S(2)}) collective-permute-start(f32[17,2,16,128]{3,2,0,1:T(8,128)S(1)} %pad_maximum_fusion.4), channel_id=1, source_target_pairs={{0,16},{16,4},{4,20},{20,0},{1,17},{17,5},{5,21},{21,1},{2,18},{18... | collective-permute-start | bytes 835592 | tf_op jit(solution)/shard_map/ppermute | solution.py:22
  154.7 8.4 %collective-permute-start.40 = (f32[17,2,16,128]{3,2,0,1:T(8,128)S(1)}, f32[17,2,16,128]{3,2,0,1:T(8,128)S(1)}, u32[]{:S(2)}, u32[]{:S(2)}) collective-permute-start(f32[17,2,16,128]{3,2,0,1:T(8,128)S(1)} %pad_maximum_fusion.5), channel_id=1, source_target_pairs={{0,20},{16,0},{4,16},{20,4},{1,21},{17,1},{5,17},{21,5},{2,22},{18... | collective-permute-start | bytes 835592 | tf_op jit(solution)/shard_map/ppermute | solution.py:22
  (5 other events, 14.3 us)
Sparse Core Ops, SparseCore 0:
  53.3 53.6 all-gather.1

commit v5 on v3

--- a/solution.py
+++ b/solution.py
@@ -180,7 +180,26 @@
 def reduce_near(sums, axis):
     both = [jnp.stack([f[d] for f in sums], 1) for d in range(NY)]
     got = [both[0]] + [shift(both[d], axis, NY, d) for d in (2, 1, 3)]
-    return got[0] + got[1] + got[2] + got[3]
+    return got
+
+
+def assemble(re_got, im_got):
+    def kernel(*refs):
+        out = refs[-1]
+        for i, got in enumerate((refs[:NY], refs[NY : 2 * NY])):
+            for j in range(K):
+                for f in range(2):
+                    out[0, j, f, i] = (got[0][j, f] + got[1][j, f]) + (got[2][j, f] + got[3][j, f])
+
+    vmem = pl.BlockSpec(memory_space=pltpu.VMEM)
+    return pl.pallas_call(
+        kernel,
+        out_shape=jax.ShapeDtypeStruct((1, K, 2, 2, 16, BR), jnp.float32),
+        in_specs=[vmem] * (2 * NY),
+        out_specs=vmem,
+        compiler_params=pltpu.CompilerParams(vmem_limit_bytes=8 * 1024 * 1024),
+        cost_estimate=pl.CostEstimate(flops=500_000, bytes_accessed=3_000_000, transcendentals=0),
+    )(*re_got, *im_got)
 
 
 def body(traces, tile_table):
@@ -208,9 +227,9 @@
     re_parts, im_parts = tile_partials(slots_abs, pos, [whole], False, after=[*in_hbm(re_come), *im_first])
     re_second, _ = reduce_ring(re_parts, X_AXIS)
     im_second, _ = reduce_ring(im_parts, "y")
-    re_sum = reduce_near((re_first, re_second), "y")
-    im_sum = reduce_near((im_first, im_second), X_AXIS)
-    return jnp.stack([re_sum, im_sum], 2)[None]
+    re_got = reduce_near((re_first, re_second), "y")
+    im_got = reduce_near((im_first, im_second), X_AXIS)
+    return assemble(re_got, im_got)
 
 
 def solution(mesh):

time: 171 us -> 169 us (0.988); the launches traced: 171 us -> 167 us
  waiting for transfers between devices: 66.7 us -> 63.5 us
    ppermute x41, waiting for transfers between devices: 66.6 us -> 63.5 us  [shift(): lax.ppermute(x, axis, [(rank(i, axis), rank((i + step) % size, axis)) for...]
  transfers between devices with their start and end apart: 42 -> 42, of which waited for: 19 -> 19; matrix products, arithmetic and copies ran while one was open for 5% -> 5% of each run, Pallas kernels for 6% -> 7%
where the time goes in v5:
time: 169 us; the launch traced here: 167 us
  waiting for transfers between devices  63.5 us (38%)
  starting transfers between devices  60.7 us (36%)
  Pallas kernels  19 us (11%)
  between operations  13.8 us (8%)
  other arithmetic  7.57 us (4%)
  local copies, waits for them, and re-layouts  2.29 us (1%)
    ppermute x41, waiting for transfers between devices, shift(): lax.ppermute(x, axis, [(rank(i, axis), rank((i + step) % size, axis)) for...  63.5 us
    ppermute x41, starting transfers between devices, shift(): lax.ppermute(x, axis, [(rank(i, axis), rank((i + step) % size, axis)) for...  60.7 us
    pallas_call x2, Pallas kernels, tile_partials(): pl.pallas_call(kernel, out_shape=parts, in_specs=[smem, smem] + [pl.Block...  13.2 us
    pallas_call x5, Pallas kernels, packed(): pl.pallas_call(kernel, out_shape=pltpu.HBM((n,) + arrays[0].shape, arrays...  4.94 us
  transfers between devices with their start and end apart: 42, of which 19 were waited for; matrix products, arithmetic and copies ran while one was open for 5% of the time, Pallas kernels for 7%

profile of v5, /device:TPU:6, one launch (start us, length us, event | category | flops | bytes accessed | tf_op | source)
XLA Modules:
  0.0 166.9 jit_solution(14986205351765048050)
XLA Ops:
  6.5 1.3 dynamic-slice_bitcast_fusion.2
  7.8 0.9 collective-permute-start
  8.7 1.9 %collective-permute-start.1 = (bf16[2,128,512]{2,1,0:T(8,128)(2,1)S(1)}, bf16[2,128,512]{2,1,0:T(8,128)(2,1)S(1)}, u32[]{:S(2)}, u32[]{:S(2)}) collective-permute-start(bf16[2,128,512]{2,1,0:T(8,128)(2,1)S(1)} %get-tuple-element.66.refs_0_), channel_id=1, source_target_pairs={{0,32},{32,64},{64,96},{96,128},{128,160},{160,192},{192,224},{224... | collective-permute-start | bytes 786440 | tf_op jit(solution)/shard_map/ppermute | solution.py:22
  10.6 3.9 %collective-permute-start.2 = (bf16[2,128,512]{2,1,0:T(8,128)(2,1)S(1)}, bf16[2,128,512]{2,1,0:T(8,128)(2,1)S(1)}, u32[]{:S(2)}, u32[]{:S(2)}) collective-permute-start(bf16[2,128,512]{2,1,0:T(8,128)(2,1)S(1)} %get-tuple-element.66.refs_0_), channel_id=1, source_target_pairs={{0,224},{32,0},{64,32},{96,64},{128,96},{160,128},{192,160},{224,1... | collective-permute-start | bytes 786440 | tf_op jit(solution)/shard_map/ppermute | solution.py:22
  14.6 1.4 collective-permute-done.refs_1_
  15.9 5.9 %collective-permute-start.4 = (bf16[2,128,512]{2,1,0:T(8,128)(2,1)S(1)}, bf16[2,128,512]{2,1,0:T(8,128)(2,1)S(1)}, u32[]{:S(2)}, u32[]{:S(2)}) collective-permute-start(bf16[2,128,512]{2,1,0:T(8,128)(2,1)S(1)} %collective-permute-done.refs_1_), channel_id=1, source_target_pairs={{0,224},{32,0},{64,32},{96,64},{128,96},{160,128},{192,160},{224,1... | collective-permute-start | bytes 786440 | tf_op jit(solution)/shard_map/ppermute | solution.py:22
  21.8 3.3 %collective-permute-start.6 = (bf16[2,128,512]{2,1,0:T(8,128)(2,1)S(1)}, bf16[2,128,512]{2,1,0:T(8,128)(2,1)S(1)}, u32[]{:S(2)}, u32[]{:S(2)}) collective-permute-start(bf16[2,128,512]{2,1,0:T(8,128)(2,1)S(1)} %collective-permute-done.2.refs_1_), channel_id=1, source_target_pairs={{0,224},{32,0},{64,32},{96,64},{128,96},{160,128},{192,160},{224,1... | collective-permute-start | bytes 786440 | tf_op jit(solution)/shard_map/ppermute | solution.py:22
  25.1 3.4 %collective-permute-done.4.refs_3_ = bf16[2,128,512]{2,1,0:T(8,128)(2,1)S(1)} collective-permute-done((bf16[2,128,512]{2,1,0:T(8,128)(2,1)S(1)}, bf16[2,128,512]{2,1,0:T(8,128)(2,1)S(1)}, u32[]{:S(2)}, u32[]{:S(2)}) %collective-permute-start.4) | collective-permute-done | bytes 262176 | tf_op jit(solution)/shard_map/ppermute | solution.py:22
  28.5 3.7 %collective-permute-start.8 = (bf16[2,128,512]{2,1,0:T(8,128)(2,1)S(1)}, bf16[2,128,512]{2,1,0:T(8,128)(2,1)S(1)}, u32[]{:S(2)}, u32[]{:S(2)}) collective-permute-start(bf16[2,128,512]{2,1,0:T(8,128)(2,1)S(1)} %collective-permute-done.4.refs_3_), channel_id=1, source_target_pairs={{0,224},{32,0},{64,32},{96,64},{128,96},{160,128},{192,160},{224,1... | collective-permute-start | bytes 786440 | tf_op jit(solution)/shard_map/ppermute | solution.py:22
  32.2 0.8 collective-permute-start.19
  33.1 4.8 %collective-permute-done.5.refs_0_ = bf16[2,128,512]{2,1,0:T(8,128)(2,1)S(1)} collective-permute-done((bf16[2,128,512]{2,1,0:T(8,128)(2,1)S(1)}, bf16[2,128,512]{2,1,0:T(8,128)(2,1)S(1)}, u32[]{:S(2)}, u32[]{:S(2)}) %collective-permute-start.5) | collective-permute-done | bytes 262176 | tf_op jit(solution)/shard_map/ppermute | solution.py:22
  37.9 3.2 %collective-permute-start.10 = (bf16[2,128,512]{2,1,0:T(8,128)(2,1)S(1)}, bf16[2,128,512]{2,1,0:T(8,128)(2,1)S(1)}, u32[]{:S(2)}, u32[]{:S(2)}) collective-permute-start(bf16[2,128,512]{2,1,0:T(8,128)(2,1)S(1)} %collective-permute-done.6.refs_1_), channel_id=1, source_target_pairs={{0,224},{32,0},{64,32},{96,64},{128,96},{160,128},{192,160},{224,1... | collective-permute-start | bytes 786440 | tf_op jit(solution)/shard_map/ppermute | solution.py:22
  41.1 1.6 collective-permute-start.12
  44.3 1.1 shard_map.29.refs_3_.refs_1_
  45.4 1.0 shard_map.30.refs_4_.refs_2_
  46.4 2.7 %collective-permute-done.9.refs_0_.refs_5_ = bf16[2,128,512]{2,1,0:T(8,128)(2,1)S(1)} collective-permute-done((bf16[2,128,512]{2,1,0:T(8,128)(2,1)S(1)}, bf16[2,128,512]{2,1,0:T(8,128)(2,1)S(1)}, u32[]{:S(2)}, u32[]{:S(2)}) %collective-permute-start.9) | collective-permute-done | bytes 262176 | tf_op jit(solution)/shard_map/ppermute | solution.py:22
  49.1 3.3 %collective-permute-done.11.refs_2_.refs_7_ = bf16[2,128,512]{2,1,0:T(8,128)(2,1)S(1)} collective-permute-done((bf16[2,128,512]{2,1,0:T(8,128)(2,1)S(1)}, bf16[2,128,512]{2,1,0:T(8,128)(2,1)S(1)}, u32[]{:S(2)}, u32[]{:S(2)}) %collective-permute-start.11) | collective-permute-done | bytes 262176 | tf_op jit(solution)/shard_map/ppermute | solution.py:22
  53.3 3.2 %collective-permute-start.14 = (bf16[2,128,512]{2,1,0:T(8,128)(2,1)S(1)}, bf16[2,128,512]{2,1,0:T(8,128)(2,1)S(1)}, u32[]{:S(2)}, u32[]{:S(2)}) collective-permute-start(bf16[2,128,512]{2,1,0:T(8,128)(2,1)S(1)} %collective-permute-done.12.refs_3_.refs_8_), channel_id=1, source_target_pairs={{0,224},{32,0},{64,32},{96,64},{128,96},{160,128},{192,160},{224,1... | collective-permute-start | bytes 786440 | tf_op jit(solution)/shard_map/ppermute | solution.py:22
  56.6 4.3 %collective-permute-done.13.refs_4_ = bf16[2,128,512]{2,1,0:T(8,128)(2,1)S(1)} collective-permute-done((bf16[2,128,512]{2,1,0:T(8,128)(2,1)S(1)}, bf16[2,128,512]{2,1,0:T(8,128)(2,1)S(1)}, u32[]{:S(2)}, u32[]{:S(2)}) %collective-permute-start.13) | collective-permute-done | bytes 262176 | tf_op jit(solution)/shard_map/ppermute | solution.py:22
  60.9 1.2 shard_map.31.refs_3_
  63.9 5.3 %collective-permute-done.15.refs_4_ = bf16[2,2,128,512]{3,2,1,0:T(8,128)(2,1)S(1)} collective-permute-done((bf16[2,2,128,512]{3,2,1,0:T(8,128)(2,1)S(1)}, bf16[2,2,128,512]{3,2,1,0:T(8,128)(2,1)S(1)}, u32[]{:S(2)}, u32[]{:S(2)}) %collective-permute-start.15) | collective-permute-done | bytes 524320 | tf_op jit(solution)/shard_map/ppermute | solution.py:22
  69.2 0.9 collective-permute-done.17.refs_6_
  70.4 6.7 %shard_map.33 = (f32[4,17,16,128]{3,2,1,0:T(8,128)S(1)}, f32[4,17,16,128]{3,2,1,0:T(8,128)S(1)}, f32[4,17,16,128]{3,2,1,0:T(8,128)S(1)}, f32[4,17,16,128]{3,2,1,...) custom-call(s32[68]{0:T(128)S(1)} %reshape.526.slots, ...), custom_call_target="tpu_custom_call" | custom-call | flops 2281701376 | bytes 13000000 | tf_op jit(solution)/shard_map/pallas_call | solution.py:150
  77.1 3.1 %collective-permute-start.23 = (f32[4,17,16,128]{3,2,1,0:T(8,128)S(1)}, f32[4,17,16,128]{3,2,1,0:T(8,128)S(1)}, u32[]{:S(2)}, u32[]{:S(2)}) collective-permute-start(f32[4,17,16,128]{3,2,1,0:T(8,128)S(1)} %get-tuple-element.29), channel_id=1, source_target_pairs={{0,3},{1,0},{2,1},{3,2},{4,7},{5,4},{6,5},{7,6},{8,11},{9,8},{10,9... | collective-permute-start | bytes 1671176 | tf_op jit(solution)/shard_map/ppermute | solution.py:22
  80.7 1.5 collective-permute-start.21
  82.3 1.4 collective-permute-start.22
  83.7 9.0 %collective-permute-done.23 = f32[4,17,16,128]{3,2,1,0:T(8,128)S(1)} collective-permute-done((f32[4,17,16,128]{3,2,1,0:T(8,128)S(1)}, f32[4,17,16,128]{3,2,1,0:T(8,128)S(1)}, u32[]{:S(2)}, u32[]{:S(2)}) %collective-permute-start.23) | collective-permute-done | bytes 557088 | tf_op jit(solution)/shard_map/ppermute | solution.py:22
  93.4 3.7 %collective-permute-start.26 = (f32[2,17,16,128]{3,2,1,0:T(8,128)}, f32[2,17,16,128]{3,2,1,0:T(8,128)}, u32[]{:S(2)}, u32[]{:S(2)}) collective-permute-start(f32[2,17,16,128]{3,2,1,0:T(8,128)} %slice_add_fusion.4), channel_id=1, source_target_pairs={{0,3},{1,0},{2,1},{3,2},{4,7},{5,4},{6,5},{7,6},{8,11},{9,8},{10,9... | collective-permute-start | bytes 835592 | tf_op jit(solution)/shard_map/ppermute | solution.py:22
  97.1 0.8 slice_add_fusion.5
  98.3 4.9 %collective-permute-done.26 = f32[2,17,16,128]{3,2,1,0:T(8,128)} collective-permute-done((f32[2,17,16,128]{3,2,1,0:T(8,128)}, f32[2,17,16,128]{3,2,1,0:T(8,128)}, u32[]{:S(2)}, u32[]{:S(2)}) %collective-permute-start.26) | collective-permute-done | bytes 278560 | tf_op jit(solution)/shard_map/ppermute | solution.py:22
  103.2 1.9 %fusion.26 = (f32[17,1,16,128]{3,2,1,0:T(8,128)}, f32[17,1,16,128]{3,2,0,1:T(8,128)}, f32[17,16,128]{2,1,0:T(8,128)S(1)}, f32[17,16,128]{2,1,0:T(8,128)S(1)}) fusion(f32[2,17,16,128]{3,2,1,0:T(8,128)} %collective-permute-done.26, f32[4,17,16,128]{3,2,1,0:T(8,128)} %copy-done.5, f32[4,17,16,128]{3,2,1,0:T(8,128)S(1)} %get-tuple-element.28), kind=kLoop, calls=%fused_computation.106 | loop fusion | flops 139264 | bytes 1392640 | tf_op jit(solution)/shard_map/add | solution.py:176
  105.1 2.4 %collective-permute-done.25 = f32[2,17,16,128]{3,2,1,0:T(8,128)} collective-permute-done((f32[2,17,16,128]{3,2,1,0:T(8,128)}, f32[2,17,16,128]{3,2,1,0:T(8,128)}, u32[]{:S(2)}, u32[]{:S(2)}) %collective-permute-start.25) | collective-permute-done | bytes 278560 | tf_op jit(solution)/shard_map/ppermute | solution.py:22
  107.5 1.7 %fusion.22 = (f32[17,1,16,128]{3,2,0,1:T(8,128)}, f32[17,1,16,128]{3,2,0,1:T(8,128)S(1)}, f32[17,16,128]{2,1,0:T(8,128)S(1)}, f32[17,16,128]{2,1,0:T(8,128)S(1)}) fusion(f32[2,17,16,128]{3,2,1,0:T(8,128)} %collective-permute-done.25, f32[4,17,16,128]{3,2,1,0:T(8,128)S(1)} %copy-done.4, f32[4,17,16,128]{3,2,1,0:T(8,128)S(1)} %get-tuple-element.28), kind=kLoop, calls=%fused_computation.102 | loop fusion | flops 139264 | bytes 1392640 | tf_op jit(solution)/shard_map/add | solution.py:175
  109.2 6.5 %shard_map.34 = (f32[4,17,16,128]{3,2,1,0:T(8,128)S(1)}, f32[4,17,16,128]{3,2,1,0:T(8,128)S(1)}, f32[4,17,16,128]{3,2,1,0:T(8,128)S(1)}, f32[2,17,16,128]{3,2,1,...) custom-call(s32[68]{0:T(128)S(1)} %reshape.527.slots, ...), custom_call_target="tpu_custom_call" | custom-call | flops 2281701376 | bytes 13000000 | tf_op jit(solution)/shard_map/pallas_call | solution.py:150
  116.0 3.2 %collective-permute-start.34 = (f32[4,17,16,128]{3,2,1,0:T(8,128)S(1)}, f32[4,17,16,128]{3,2,1,0:T(8,128)S(1)}, u32[]{:S(2)}, u32[]{:S(2)}) collective-permute-start(f32[4,17,16,128]{3,2,1,0:T(8,128)S(1)} %get-tuple-element.39), channel_id=1, source_target_pairs={{0,3},{1,0},{2,1},{3,2},{4,7},{5,4},{6,5},{7,6},{8,11},{9,8},{10,9... | collective-permute-start | bytes 1671176 | tf_op jit(solution)/shard_map/ppermute | solution.py:22
  119.7 1.6 fusion.5
  121.4 1.6 collective-permute-start.27
  123.0 7.2 %collective-permute-done.35 = f32[4,17,16,128]{3,2,1,0:T(8,128)S(1)} collective-permute-done((f32[4,17,16,128]{3,2,1,0:T(8,128)S(1)}, f32[4,17,16,128]{3,2,1,0:T(8,128)S(1)}, u32[]{:S(2)}, u32[]{:S(2)}) %collective-permute-start.35) | collective-permute-done | bytes 557088 | tf_op jit(solution)/shard_map/ppermute | solution.py:22
  130.4 3.3 %collective-permute-start.37 = (f32[2,17,16,128]{3,2,1,0:T(8,128)S(1)}, f32[2,17,16,128]{3,2,1,0:T(8,128)S(1)}, u32[]{:S(2)}, u32[]{:S(2)}) collective-permute-start(f32[2,17,16,128]{3,2,1,0:T(8,128)S(1)} %slice_add_fusion), channel_id=1, source_target_pairs={{0,3},{1,0},{2,1},{3,2},{4,7},{5,4},{6,5},{7,6},{8,11},{9,8},{10,9... | collective-permute-start | bytes 835592 | tf_op jit(solution)/shard_map/ppermute | solution.py:22
  133.7 1.2 collective-permute-start.29
  136.0 2.1 %collective-permute-done.36 = f32[2,17,16,128]{3,2,1,0:T(8,128)S(1)} collective-permute-done((f32[2,17,16,128]{3,2,1,0:T(8,128)S(1)}, f32[2,17,16,128]{3,2,1,0:T(8,128)S(1)}, u32[]{:S(2)}, u32[]{:S(2)}) %collective-permute-start.36) | collective-permute-done | bytes 278560 | tf_op jit(solution)/shard_map/ppermute | solution.py:22
  138.2 0.9 collective-permute-start.40
  139.2 2.5 %collective-permute-start.39 = (f32[17,2,16,128]{3,2,0,1:T(8,128)S(1)}, f32[17,2,16,128]{3,2,0,1:T(8,128)S(1)}, u32[]{:S(2)}, u32[]{:S(2)}) collective-permute-start(f32[17,2,16,128]{3,2,0,1:T(8,128)S(1)} %pad_maximum_fusion.6), channel_id=1, source_target_pairs={{0,16},{16,4},{4,20},{20,0},{1,17},{17,5},{5,21},{21,1},{2,18},{18... | collective-permute-start | bytes 835592 | tf_op jit(solution)/shard_map/ppermute | solution.py:22
  142.0 4.5 %collective-permute-done.30 = f32[2,17,16,128]{3,2,1,0:T(8,128)S(1)} collective-permute-done((f32[2,17,16,128]{3,2,1,0:T(8,128)S(1)}, f32[2,17,16,128]{3,2,1,0:T(8,128)S(1)}, u32[]{:S(2)}, u32[]{:S(2)}) %collective-permute-start.30) | collective-permute-done | bytes 278560 | tf_op jit(solution)/shard_map/ppermute | solution.py:22
  146.7 4.9 %collective-permute-start.31 = (f32[17,2,16,128]{3,2,0,1:T(8,128)S(1)}, f32[17,2,16,128]{3,2,0,1:T(8,128)S(1)}, u32[]{:S(2)}, u32[]{:S(2)}) collective-permute-start(f32[17,2,16,128]{3,2,0,1:T(8,128)S(1)} %pad_maximum_fusion.1), channel_id=1, source_target_pairs={{0,2},{1,3},{2,0},{3,1},{4,6},{5,7},{6,4},{7,5},{8,10},{9,11},{10,... | collective-permute-start | bytes 835592 | tf_op jit(solution)/shard_map/ppermute | solution.py:22
  151.7 1.2 collective-permute-start.33
  154.6 4.4 %collective-permute-done.31 = f32[17,2,16,128]{3,2,0,1:T(8,128)S(1)} collective-permute-done((f32[17,2,16,128]{3,2,0,1:T(8,128)S(1)}, f32[17,2,16,128]{3,2,0,1:T(8,128)S(1)}, u32[]{:S(2)}, u32[]{:S(2)}) %collective-permute-start.31) | collective-permute-done | bytes 278560 | tf_op jit(solution)/shard_map/ppermute | solution.py:22
  159.1 0.9 shard_map.35
  (103 shorter events, 10.7 us)
Async XLA Ops:
  6.5 102.7 %all-gather.2.cloned.1.call-start = ((), (), s32[]{:S(2)}) async-start(), calls=%async_computation | async-start | bytes 8912896 | tf_op jit(solution)/shard_map/all_gather | solution.py:221
  7.8 8.1 %collective-permute-start = (bf16[2,128,512]{2,1,0:T(8,128)(2,1)S(1)}, bf16[2,128,512]{2,1,0:T(8,128)(2,1)S(1)}, u32[]{:S(2)}, u32[]{:S(2)}) collective-permute-start(bf16[2,128,512]{2,1,0:T(8,128)(2,1)S(1)} %get-tuple-element.65), channel_id=1, source_target_pairs={{0,16},{16,0},{1,17},{17,1},{2,18},{18,2},{3,19},{19,3},{4,20},{20... | collective-permute-start | bytes 786440 | tf_op jit(solution)/shard_map/ppermute | solution.py:22
  8.7 13.1 %collective-permute-start.1 = (bf16[2,128,512]{2,1,0:T(8,128)(2,1)S(1)}, bf16[2,128,512]{2,1,0:T(8,128)(2,1)S(1)}, u32[]{:S(2)}, u32[]{:S(2)}) collective-permute-start(bf16[2,128,512]{2,1,0:T(8,128)(2,1)S(1)} %get-tuple-element.66.refs_0_), channel_id=1, source_target_pairs={{0,32},{32,64},{64,96},{96,128},{128,160},{160,192},{192,224},{224... | collective-permute-start | bytes 786440 | tf_op jit(solution)/shard_map/ppermute | solution.py:22
  10.6 11.2 %collective-permute-start.2 = (bf16[2,128,512]{2,1,0:T(8,128)(2,1)S(1)}, bf16[2,128,512]{2,1,0:T(8,128)(2,1)S(1)}, u32[]{:S(2)}, u32[]{:S(2)}) collective-permute-start(bf16[2,128,512]{2,1,0:T(8,128)(2,1)S(1)} %get-tuple-element.66.refs_0_), channel_id=1, source_target_pairs={{0,224},{32,0},{64,32},{96,64},{128,96},{160,128},{192,160},{224,1... | collective-permute-start | bytes 786440 | tf_op jit(solution)/shard_map/ppermute | solution.py:22
  15.9 12.6 %collective-permute-start.4 = (bf16[2,128,512]{2,1,0:T(8,128)(2,1)S(1)}, bf16[2,128,512]{2,1,0:T(8,128)(2,1)S(1)}, u32[]{:S(2)}, u32[]{:S(2)}) collective-permute-start(bf16[2,128,512]{2,1,0:T(8,128)(2,1)S(1)} %collective-permute-done.refs_1_), channel_id=1, source_target_pairs={{0,224},{32,0},{64,32},{96,64},{128,96},{160,128},{192,160},{224,1... | collective-permute-start | bytes 786440 | tf_op jit(solution)/shard_map/ppermute | solution.py:22
  21.8 10.5 %collective-permute-start.3 = (bf16[2,128,512]{2,1,0:T(8,128)(2,1)S(1)}, bf16[2,128,512]{2,1,0:T(8,128)(2,1)S(1)}, u32[]{:S(2)}, u32[]{:S(2)}) collective-permute-start(bf16[2,128,512]{2,1,0:T(8,128)(2,1)S(1)} %collective-permute-done.refs_1_), channel_id=1, source_target_pairs={{0,32},{32,64},{64,96},{96,128},{128,160},{160,192},{192,224},{224... | collective-permute-start | bytes 786440 | tf_op jit(solution)/shard_map/ppermute | solution.py:22
  21.8 16.1 %collective-permute-start.5 = (bf16[2,128,512]{2,1,0:T(8,128)(2,1)S(1)}, bf16[2,128,512]{2,1,0:T(8,128)(2,1)S(1)}, u32[]{:S(2)}, u32[]{:S(2)}) collective-permute-start(bf16[2,128,512]{2,1,0:T(8,128)(2,1)S(1)} %collective-permute-done.1.refs_0_), channel_id=1, source_target_pairs={{0,32},{32,64},{64,96},{96,128},{128,160},{160,192},{192,224},{224... | collective-permute-start | bytes 786440 | tf_op jit(solution)/shard_map/ppermute | solution.py:22
  21.8 16.1 %collective-permute-start.6 = (bf16[2,128,512]{2,1,0:T(8,128)(2,1)S(1)}, bf16[2,128,512]{2,1,0:T(8,128)(2,1)S(1)}, u32[]{:S(2)}, u32[]{:S(2)}) collective-permute-start(bf16[2,128,512]{2,1,0:T(8,128)(2,1)S(1)} %collective-permute-done.2.refs_1_), channel_id=1, source_target_pairs={{0,224},{32,0},{64,32},{96,64},{128,96},{160,128},{192,160},{224,1... | collective-permute-start | bytes 786440 | tf_op jit(solution)/shard_map/ppermute | solution.py:22
  28.5 12.6 %collective-permute-start.8 = (bf16[2,128,512]{2,1,0:T(8,128)(2,1)S(1)}, bf16[2,128,512]{2,1,0:T(8,128)(2,1)S(1)}, u32[]{:S(2)}, u32[]{:S(2)}) collective-permute-start(bf16[2,128,512]{2,1,0:T(8,128)(2,1)S(1)} %collective-permute-done.4.refs_3_), channel_id=1, source_target_pairs={{0,224},{32,0},{64,32},{96,64},{128,96},{160,128},{192,160},{224,1... | collective-permute-start | bytes 786440 | tf_op jit(solution)/shard_map/ppermute | solution.py:22
  32.2 11.2 %collective-permute-start.7 = (bf16[2,128,512]{2,1,0:T(8,128)(2,1)S(1)}, bf16[2,128,512]{2,1,0:T(8,128)(2,1)S(1)}, u32[]{:S(2)}, u32[]{:S(2)}) collective-permute-start(bf16[2,128,512]{2,1,0:T(8,128)(2,1)S(1)} %collective-permute-done.3.refs_2_), channel_id=1, source_target_pairs={{0,32},{32,64},{64,96},{96,128},{128,160},{160,192},{192,224},{224... | collective-permute-start | bytes 786440 | tf_op jit(solution)/shard_map/ppermute | solution.py:22
  32.2 14.2 %collective-permute-start.19 = (bf16[2,128,512]{2,1,0:T(8,128)(2,1)S(1)}, bf16[2,128,512]{2,1,0:T(8,128)(2,1)S(1)}, u32[]{:S(2)}, u32[]{:S(2)}) collective-permute-start(bf16[2,128,512]{2,1,0:T(8,128)(2,1)S(1)} %get-tuple-element.67), channel_id=1, source_target_pairs={{0,16},{16,0},{1,17},{17,1},{2,18},{18,2},{3,19},{19,3},{4,20},{20... | collective-permute-start | bytes 786440 | tf_op jit(solution)/shard_map/ppermute | solution.py:22
  37.9 11.2 %collective-permute-start.9 = (bf16[2,128,512]{2,1,0:T(8,128)(2,1)S(1)}, bf16[2,128,512]{2,1,0:T(8,128)(2,1)S(1)}, u32[]{:S(2)}, u32[]{:S(2)}) collective-permute-start(bf16[2,128,512]{2,1,0:T(8,128)(2,1)S(1)} %collective-permute-done.5.refs_0_), channel_id=1, source_target_pairs={{0,32},{32,64},{64,96},{96,128},{128,160},{160,192},{192,224},{224... | collective-permute-start | bytes 786440 | tf_op jit(solution)/shard_map/ppermute | solution.py:22
  37.9 11.2 %collective-permute-start.10 = (bf16[2,128,512]{2,1,0:T(8,128)(2,1)S(1)}, bf16[2,128,512]{2,1,0:T(8,128)(2,1)S(1)}, u32[]{:S(2)}, u32[]{:S(2)}) collective-permute-start(bf16[2,128,512]{2,1,0:T(8,128)(2,1)S(1)} %collective-permute-done.6.refs_1_), channel_id=1, source_target_pairs={{0,224},{32,0},{64,32},{96,64},{128,96},{160,128},{192,160},{224,1... | collective-permute-start | bytes 786440 | tf_op jit(solution)/shard_map/ppermute | solution.py:22
  41.1 8.0 %collective-permute-start.12 = (bf16[2,128,512]{2,1,0:T(8,128)(2,1)S(1)}, bf16[2,128,512]{2,1,0:T(8,128)(2,1)S(1)}, u32[]{:S(2)}, u32[]{:S(2)}) collective-permute-start(bf16[2,128,512]{2,1,0:T(8,128)(2,1)S(1)} %collective-permute-done.8.refs_3_), channel_id=1, source_target_pairs={{0,224},{32,0},{64,32},{96,64},{128,96},{160,128},{192,160},{224,1... | collective-permute-start | bytes 786440 | tf_op jit(solution)/shard_map/ppermute | solution.py:22
  43.5 8.9 %collective-permute-start.11 = (bf16[2,128,512]{2,1,0:T(8,128)(2,1)S(1)}, bf16[2,128,512]{2,1,0:T(8,128)(2,1)S(1)}, u32[]{:S(2)}, u32[]{:S(2)}) collective-permute-start(bf16[2,128,512]{2,1,0:T(8,128)(2,1)S(1)} %collective-permute-done.7.refs_2_), channel_id=1, source_target_pairs={{0,32},{32,64},{64,96},{96,128},{128,160},{160,192},{192,224},{224... | collective-permute-start | bytes 786440 | tf_op jit(solution)/shard_map/ppermute | solution.py:22
  53.2 9.2 %copy-start = (bf16[4,2,128,512]{3,2,1,0:T(8,128)(2,1)S(1)}, bf16[4,2,128,512]{3,2,1,0:T(8,128)(2,1)}, u32[]{:S(2)}) copy-start(bf16[4,2,128,512]{3,2,1,0:T(8,128)(2,1)} %shard_map.29.refs_3_.refs_1_) | copy-start | bytes 3145732
  53.2 9.8 %copy-start.1 = (bf16[2,2,128,512]{3,2,1,0:T(8,128)(2,1)S(1)}, bf16[2,2,128,512]{3,2,1,0:T(8,128)(2,1)}, u32[]{:S(2)}) copy-start(bf16[2,2,128,512]{3,2,1,0:T(8,128)(2,1)} %shard_map.28.refs_2_.refs_0_) | copy-start | bytes 1572868
  53.2 10.2 %copy-start.10 = (s32[32,17,2]{0,2,1:T(2,128)S(1)}, s32[32,17,2]{0,2,1:T(2,128)}, u32[]{:S(2)}) copy-start(s32[32,17,2]{0,2,1:T(2,128)} %param.3) | copy-start | bytes 13060
  53.2 7.7 %collective-permute-start.13 = (bf16[2,128,512]{2,1,0:T(8,128)(2,1)S(1)}, bf16[2,128,512]{2,1,0:T(8,128)(2,1)S(1)}, u32[]{:S(2)}, u32[]{:S(2)}) collective-permute-start(bf16[2,128,512]{2,1,0:T(8,128)(2,1)S(1)} %collective-permute-done.9.refs_0_.refs_5_), channel_id=1, source_target_pairs={{0,32},{32,64},{64,96},{96,128},{128,160},{160,192},{192,224},{224... | collective-permute-start | bytes 786440 | tf_op jit(solution)/shard_map/ppermute | solution.py:22
  53.3 7.6 %collective-permute-start.14 = (bf16[2,128,512]{2,1,0:T(8,128)(2,1)S(1)}, bf16[2,128,512]{2,1,0:T(8,128)(2,1)S(1)}, u32[]{:S(2)}, u32[]{:S(2)}) collective-permute-start(bf16[2,128,512]{2,1,0:T(8,128)(2,1)S(1)} %collective-permute-done.12.refs_3_.refs_8_), channel_id=1, source_target_pairs={{0,224},{32,0},{64,32},{96,64},{128,96},{160,128},{192,160},{224,1... | collective-permute-start | bytes 786440 | tf_op jit(solution)/shard_map/ppermute | solution.py:22
  62.1 8.2 %collective-permute-start.18 = (bf16[6,2,128,512]{3,2,1,0:T(8,128)(2,1)}, bf16[6,2,128,512]{3,2,1,0:T(8,128)(2,1)}, u32[]{:S(2)}, u32[]{:S(2)}) collective-permute-start(bf16[6,2,128,512]{3,2,1,0:T(8,128)(2,1)} %shard_map.31.refs_3_), channel_id=1, source_target_pairs={{0,8},{8,0},{1,9},{9,1},{2,10},{10,2},{3,11},{11,3},{4,12},{12,4},... | collective-permute-start | bytes 4718600 | tf_op jit(solution)/shard_map/ppermute | solution.py:22
  62.4 6.8 %collective-permute-start.16 = (bf16[4,2,128,512]{3,2,1,0:T(8,128)(2,1)S(1)}, bf16[4,2,128,512]{3,2,1,0:T(8,128)(2,1)S(1)}, u32[]{:S(2)}, u32[]{:S(2)}) collective-permute-start(bf16[4,2,128,512]{3,2,1,0:T(8,128)(2,1)S(1)} %copy-done), channel_id=1, source_target_pairs={{0,8},{8,0},{1,9},{9,1},{2,10},{10,2},{3,11},{11,3},{4,12},{12,4},... | collective-permute-start | bytes 3145736 | tf_op jit(solution)/shard_map/ppermute | solution.py:22
  62.9 7.2 %collective-permute-start.17 = (bf16[4,2,128,512]{3,2,1,0:T(8,128)(2,1)}, bf16[4,2,128,512]{3,2,1,0:T(8,128)(2,1)}, u32[]{:S(2)}, u32[]{:S(2)}) collective-permute-start(bf16[4,2,128,512]{3,2,1,0:T(8,128)(2,1)} %shard_map.30.refs_4_.refs_2_), channel_id=1, source_target_pairs={{0,8},{8,0},{1,9},{9,1},{2,10},{10,2},{3,11},{11,3},{4,12},{12,4},... | collective-permute-start | bytes 3145736 | tf_op jit(solution)/shard_map/ppermute | solution.py:22
  63.0 6.2 %collective-permute-start.15 = (bf16[2,2,128,512]{3,2,1,0:T(8,128)(2,1)S(1)}, bf16[2,2,128,512]{3,2,1,0:T(8,128)(2,1)S(1)}, u32[]{:S(2)}, u32[]{:S(2)}) collective-permute-start(bf16[2,2,128,512]{3,2,1,0:T(8,128)(2,1)S(1)} %copy-done.1), channel_id=1, source_target_pairs={{0,8},{8,0},{1,9},{9,1},{2,10},{10,2},{3,11},{11,3},{4,12},{12,4},... | collective-permute-start | bytes 1572872 | tf_op jit(solution)/shard_map/ppermute | solution.py:22
  77.1 15.5 %collective-permute-start.23 = (f32[4,17,16,128]{3,2,1,0:T(8,128)S(1)}, f32[4,17,16,128]{3,2,1,0:T(8,128)S(1)}, u32[]{:S(2)}, u32[]{:S(2)}) collective-permute-start(f32[4,17,16,128]{3,2,1,0:T(8,128)S(1)} %get-tuple-element.29), channel_id=1, source_target_pairs={{0,3},{1,0},{2,1},{3,2},{4,7},{5,4},{6,5},{7,6},{8,11},{9,8},{10,9... | collective-permute-start | bytes 1671176 | tf_op jit(solution)/shard_map/ppermute | solution.py:22
  80.2 16.9 %collective-permute-start.24 = (f32[4,17,16,128]{3,2,1,0:T(8,128)S(1)}, f32[4,17,16,128]{3,2,1,0:T(8,128)S(1)}, u32[]{:S(2)}, u32[]{:S(2)}) collective-permute-start(f32[4,17,16,128]{3,2,1,0:T(8,128)S(1)} %get-tuple-element.31), channel_id=1, source_target_pairs={{0,1},{1,2},{2,3},{3,0},{4,5},{5,6},{6,7},{7,4},{8,9},{9,10},{10,1... | collective-permute-start | bytes 1671176 | tf_op jit(solution)/shard_map/ppermute | solution.py:22
  80.2 29.0 %collective-permute-start.20 = (f32[4,17,16,128]{3,2,1,0:T(8,128)S(1)}, f32[4,17,16,128]{3,2,1,0:T(8,128)}, u32[]{:S(2)}, u32[]{:S(2)}) collective-permute-start(f32[4,17,16,128]{3,2,1,0:T(8,128)S(1)} %get-tuple-element.25), channel_id=1, source_target_pairs={{0,16},{16,4},{4,20},{20,0},{1,17},{17,5},{5,21},{21,1},{2,18},{18... | collective-permute-start | bytes 1671176 | tf_op jit(solution)/shard_map/ppermute | solution.py:22
  80.7 28.5 %collective-permute-start.21 = (f32[4,17,16,128]{3,2,1,0:T(8,128)S(1)}, f32[4,17,16,128]{3,2,1,0:T(8,128)}, u32[]{:S(2)}, u32[]{:S(2)}) collective-permute-start(f32[4,17,16,128]{3,2,1,0:T(8,128)S(1)} %get-tuple-element.26), channel_id=1, source_target_pairs={{0,20},{16,0},{4,16},{20,4},{1,21},{17,1},{5,17},{21,5},{2,22},{18... | collective-permute-start | bytes 1671176 | tf_op jit(solution)/shard_map/ppermute | solution.py:22
  82.3 26.9 %collective-permute-start.22 = (f32[4,17,16,128]{3,2,1,0:T(8,128)S(1)}, f32[4,17,16,128]{3,2,1,0:T(8,128)}, u32[]{:S(2)}, u32[]{:S(2)}) collective-permute-start(f32[4,17,16,128]{3,2,1,0:T(8,128)S(1)} %get-tuple-element.27), channel_id=1, source_target_pairs={{0,4},{16,20},{4,0},{20,16},{1,5},{17,21},{5,1},{21,17},{2,6},{18,... | collective-permute-start | bytes 1671176 | tf_op jit(solution)/shard_map/ppermute | solution.py:22
  92.6 10.6 %copy-start.3 = (f32[4,17,16,128]{3,2,1,0:T(8,128)}, f32[4,17,16,128]{3,2,1,0:T(8,128)S(1)}, u32[]{:S(2)}) copy-start(f32[4,17,16,128]{3,2,1,0:T(8,128)S(1)} %collective-permute-done.23) | copy-start | bytes 1671172
  93.4 9.8 %collective-permute-start.26 = (f32[2,17,16,128]{3,2,1,0:T(8,128)}, f32[2,17,16,128]{3,2,1,0:T(8,128)}, u32[]{:S(2)}, u32[]{:S(2)}) collective-permute-start(f32[2,17,16,128]{3,2,1,0:T(8,128)} %slice_add_fusion.4), channel_id=1, source_target_pairs={{0,3},{1,0},{2,1},{3,2},{4,7},{5,4},{6,5},{7,6},{8,11},{9,8},{10,9... | collective-permute-start | bytes 835592 | tf_op jit(solution)/shard_map/ppermute | solution.py:22
  98.0 9.5 %collective-permute-start.25 = (f32[2,17,16,128]{3,2,1,0:T(8,128)}, f32[2,17,16,128]{3,2,1,0:T(8,128)}, u32[]{:S(2)}, u32[]{:S(2)}) collective-permute-start(f32[2,17,16,128]{3,2,1,0:T(8,128)} %slice_add_fusion.5), channel_id=1, source_target_pairs={{0,1},{1,2},{2,3},{3,0},{4,5},{5,6},{6,7},{7,4},{8,9},{9,10},{10,1... | collective-permute-start | bytes 835592 | tf_op jit(solution)/shard_map/ppermute | solution.py:22
  103.2 4.3 %copy-start.4 = (f32[4,17,16,128]{3,2,1,0:T(8,128)S(1)}, f32[4,17,16,128]{3,2,1,0:T(8,128)}, u32[]{:S(2)}) copy-start(f32[4,17,16,128]{3,2,1,0:T(8,128)} %copy-done.3) | copy-start | bytes 1671172
  115.7 14.5 %collective-permute-start.35 = (f32[4,17,16,128]{3,2,1,0:T(8,128)S(1)}, f32[4,17,16,128]{3,2,1,0:T(8,128)S(1)}, u32[]{:S(2)}, u32[]{:S(2)}) collective-permute-start(f32[4,17,16,128]{3,2,1,0:T(8,128)S(1)} %get-tuple-element.41), channel_id=1, source_target_pairs={{0,1},{1,2},{2,3},{3,0},{4,5},{5,6},{6,7},{7,4},{8,9},{9,10},{10,1... | collective-permute-start | bytes 1671176 | tf_op jit(solution)/shard_map/ppermute | solution.py:22
  116.0 14.3 %collective-permute-start.34 = (f32[4,17,16,128]{3,2,1,0:T(8,128)S(1)}, f32[4,17,16,128]{3,2,1,0:T(8,128)S(1)}, u32[]{:S(2)}, u32[]{:S(2)}) collective-permute-start(f32[4,17,16,128]{3,2,1,0:T(8,128)S(1)} %get-tuple-element.39), channel_id=1, source_target_pairs={{0,3},{1,0},{2,1},{3,2},{4,7},{5,4},{6,5},{7,6},{8,11},{9,8},{10,9... | collective-permute-start | bytes 1671176 | tf_op jit(solution)/shard_map/ppermute | solution.py:22
  119.2 14.4 %collective-permute-start.28 = (f32[4,17,16,128]{3,2,1,0:T(8,128)S(1)}, f32[4,17,16,128]{3,2,1,0:T(8,128)S(1)}, u32[]{:S(2)}, u32[]{:S(2)}) collective-permute-start(f32[4,17,16,128]{3,2,1,0:T(8,128)S(1)} %get-tuple-element.36), channel_id=1, source_target_pairs={{0,16},{16,4},{4,20},{20,0},{1,17},{17,5},{5,21},{21,1},{2,18},{18... | collective-permute-start | bytes 1671176 | tf_op jit(solution)/shard_map/ppermute | solution.py:22
  121.4 14.0 %collective-permute-start.27 = (f32[4,17,16,128]{3,2,1,0:T(8,128)S(1)}, f32[4,17,16,128]{3,2,1,0:T(8,128)S(1)}, u32[]{:S(2)}, u32[]{:S(2)}) collective-permute-start(f32[4,17,16,128]{3,2,1,0:T(8,128)S(1)} %get-tuple-element.34), channel_id=1, source_target_pairs={{0,20},{16,0},{4,16},{20,4},{1,21},{17,1},{5,17},{21,5},{2,22},{18... | collective-permute-start | bytes 1671176 | tf_op jit(solution)/shard_map/ppermute | solution.py:22
  130.2 7.8 %collective-permute-start.36 = (f32[2,17,16,128]{3,2,1,0:T(8,128)S(1)}, f32[2,17,16,128]{3,2,1,0:T(8,128)S(1)}, u32[]{:S(2)}, u32[]{:S(2)}) collective-permute-start(f32[2,17,16,128]{3,2,1,0:T(8,128)S(1)} %slice_add_fusion.1), channel_id=1, source_target_pairs={{0,1},{1,2},{2,3},{3,0},{4,5},{5,6},{6,7},{7,4},{8,9},{9,10},{10,1... | collective-permute-start | bytes 835592 | tf_op jit(solution)/shard_map/ppermute | solution.py:22
  130.4 7.7 %collective-permute-start.37 = (f32[2,17,16,128]{3,2,1,0:T(8,128)S(1)}, f32[2,17,16,128]{3,2,1,0:T(8,128)S(1)}, u32[]{:S(2)}, u32[]{:S(2)}) collective-permute-start(f32[2,17,16,128]{3,2,1,0:T(8,128)S(1)} %slice_add_fusion), channel_id=1, source_target_pairs={{0,3},{1,0},{2,1},{3,2},{4,7},{5,4},{6,5},{7,6},{8,11},{9,8},{10,9... | collective-permute-start | bytes 835592 | tf_op jit(solution)/shard_map/ppermute | solution.py:22
  133.7 4.5 %copy-start.7 = (f32[17,1,16,128]{3,2,1,0:T(8,128)S(1)}, f32[17,1,16,128]{3,2,1,0:T(8,128)}, u32[]{:S(2)}) copy-start(f32[17,1,16,128]{3,2,1,0:T(8,128)} %get-tuple-element.49) | copy-start | bytes 417796
  133.7 8.2 %collective-permute-start.29 = (f32[2,17,16,128]{3,2,1,0:T(8,128)S(1)}, f32[2,17,16,128]{3,2,1,0:T(8,128)S(1)}, u32[]{:S(2)}, u32[]{:S(2)}) collective-permute-start(f32[2,17,16,128]{3,2,1,0:T(8,128)S(1)} %slice_add_fusion.3), channel_id=1, source_target_pairs={{0,16},{16,4},{4,20},{20,0},{1,17},{17,5},{5,21},{21,1},{2,18},{18... | collective-permute-start | bytes 835592 | tf_op jit(solution)/shard_map/ppermute | solution.py:22
  135.4 11.0 %collective-permute-start.30 = (f32[2,17,16,128]{3,2,1,0:T(8,128)S(1)}, f32[2,17,16,128]{3,2,1,0:T(8,128)S(1)}, u32[]{:S(2)}, u32[]{:S(2)}) collective-permute-start(f32[2,17,16,128]{3,2,1,0:T(8,128)S(1)} %slice_add_fusion.2), channel_id=1, source_target_pairs={{0,20},{16,0},{4,16},{20,4},{1,21},{17,1},{5,17},{21,5},{2,22},{18... | collective-permute-start | bytes 835592 | tf_op jit(solution)/shard_map/ppermute | solution.py:22
  138.2 20.8 %collective-permute-start.40 = (f32[17,2,16,128]{3,2,1,0:T(8,128)S(1)}, f32[17,2,16,128]{3,2,1,0:T(8,128)S(1)}, u32[]{:S(2)}, u32[]{:S(2)}) collective-permute-start(f32[17,2,16,128]{3,2,1,0:T(8,128)S(1)} %pad_maximum_fusion.7), channel_id=1, source_target_pairs={{0,20},{16,0},{4,16},{20,4},{1,21},{17,1},{5,17},{21,5},{2,22},{18... | collective-permute-start | bytes 835592 | tf_op jit(solution)/shard_map/ppermute | solution.py:22
  139.2 12.6 %collective-permute-start.39 = (f32[17,2,16,128]{3,2,0,1:T(8,128)S(1)}, f32[17,2,16,128]{3,2,0,1:T(8,128)S(1)}, u32[]{:S(2)}, u32[]{:S(2)}) collective-permute-start(f32[17,2,16,128]{3,2,0,1:T(8,128)S(1)} %pad_maximum_fusion.6), channel_id=1, source_target_pairs={{0,16},{16,4},{4,20},{20,0},{1,17},{17,5},{5,21},{21,1},{2,18},{18... | collective-permute-start | bytes 835592 | tf_op jit(solution)/shard_map/ppermute | solution.py:22
  141.7 12.2 %collective-permute-start.38 = (f32[17,2,16,128]{3,2,0,1:T(8,128)S(1)}, f32[17,2,16,128]{3,2,0,1:T(8,128)S(1)}, u32[]{:S(2)}, u32[]{:S(2)}) collective-permute-start(f32[17,2,16,128]{3,2,0,1:T(8,128)S(1)} %pad_maximum_fusion.5), channel_id=1, source_target_pairs={{0,4},{16,20},{4,0},{20,16},{1,5},{17,21},{5,1},{21,17},{2,6},{18,... | collective-permute-start | bytes 835592 | tf_op jit(solution)/shard_map/ppermute | solution.py:22
  146.6 8.0 %collective-permute-start.32 = (f32[17,2,16,128]{3,2,0,1:T(8,128)S(1)}, f32[17,2,16,128]{3,2,0,1:T(8,128)S(1)}, u32[]{:S(2)}, u32[]{:S(2)}) collective-permute-start(f32[17,2,16,128]{3,2,0,1:T(8,128)S(1)} %pad_maximum_fusion.2), channel_id=1, source_target_pairs={{0,1},{1,2},{2,3},{3,0},{4,5},{5,6},{6,7},{7,4},{8,9},{9,10},{10,1... | collective-permute-start | bytes 835592 | tf_op jit(solution)/shard_map/ppermute | solution.py:22
  146.7 12.3 %collective-permute-start.31 = (f32[17,2,16,128]{3,2,0,1:T(8,128)S(1)}, f32[17,2,16,128]{3,2,0,1:T(8,128)S(1)}, u32[]{:S(2)}, u32[]{:S(2)}) collective-permute-start(f32[17,2,16,128]{3,2,0,1:T(8,128)S(1)} %pad_maximum_fusion.1), channel_id=1, source_target_pairs={{0,2},{1,3},{2,0},{3,1},{4,6},{5,7},{6,4},{7,5},{8,10},{9,11},{10,... | collective-permute-start | bytes 835592 | tf_op jit(solution)/shard_map/ppermute | solution.py:22
  151.7 7.4 %collective-permute-start.33 = (f32[17,2,16,128]{3,2,1,0:T(8,128)S(1)}, f32[17,2,16,128]{3,2,1,0:T(8,128)S(1)}, u32[]{:S(2)}, u32[]{:S(2)}) collective-permute-start(f32[17,2,16,128]{3,2,1,0:T(8,128)S(1)} %pad_maximum_fusion.3), channel_id=1, source_target_pairs={{0,3},{1,0},{2,1},{3,2},{4,7},{5,4},{6,5},{7,6},{8,11},{9,8},{10,9... | collective-permute-start | bytes 835592 | tf_op jit(solution)/shard_map/ppermute | solution.py:22
  (5 other events, 10.2 us)
Sparse Core Ops, SparseCore 0:
  53.3 53.6 all-gather.1
